TPU v7x, 32 devices: a whole 2x2x4 slice. The times are simulated.
32 devices in a mesh: section: 2 (over y), dp: 4 (over x, core), cell: 4 (over z).
Axes of the slice: x: 2, y: 2, z: 4, core: 2. Of those that a mesh axis runs over, the one named last changes fastest.
Arguments:
- probes: float32 [2, 3072, 128], P('section', 'cell'), may hold values from -6 to 6
- jacobian: float32 [2, 4096, 3072], P('section', 'dp', 'cell'), may hold values from -0.109375 to 0.109375
- classes: int32 [2, 4096], P('section', 'dp'), may hold values from 0 to 3
- active: int32 [2, 3072], P('section', 'cell'), may hold values 0 or 1
- coupling: float32 [2, 3072], P('section', 'cell'), may hold values from 0.1 to 1
Outputs:
- first_image: float32 [2, 3072, 128], P('section', 'cell')
- second_image: float32 [2, 3072, 128], P('section', 'cell')
All inputs are finite; a program needn't handle non-finite values. No bound on the sum of `active` on one device may be relied on, other than what follows from the above.
Results may differ from a plain program's by a relative error of at most 0.000092.
Values sent between devices are 32-bit elements; how exact they have to be, the bound alone decides.
No kernel may reach another device: no remote copies, remote signals or barrier semaphores. Data moves between devices by JAX's collectives and lax.ppermute only.
A program may use at most 64 MiB of HBM per device.

v0:
```python
import jax
import jax.numpy as jnp
from jax import lax
from jax.sharding import PartitionSpec as P


def shifted(value, axis, by):
    length = lax.axis_size(axis)
    pairs = [(i, i + by) for i in range(length) if 0 <= i + by < length]
    return lax.ppermute(value, axis, pairs)


def class_weight(labels):
    return jnp.where(
        labels == 0, 1.0, jnp.where(labels == 1, 0.5, jnp.where(labels == 2, 0.25, 0.125))
    ).astype(jnp.float32)


def local(probes, jacobian, classes, active, coupling):
    tile = jacobian[0]
    factors = class_weight(classes[0])
    maskf = active[0].astype(jnp.float32)[:, None]
    first_section = lax.axis_index("section") == 0
    strength = jnp.where(first_section, 0.0, coupling[0])

    def back_rows(incoming):
        return lax.dot_general(
            tile,
            incoming,
            (((0,), (0,)), ((), ())),
            precision=lax.Precision.HIGHEST,
            preferred_element_type=jnp.float32,
        )

    def smoothing(masked_part, strength_part):
        below = shifted(masked_part, "section", 1)
        flux = strength_part[:, None] * (masked_part - below)
        upper_flux = shifted(flux, "section", -1)
        return flux - upper_flux

    def apply_hessian(field):
        masked = field[0] * maskf
        share_rows = tile.shape[0] // lax.axis_size("cell")
        share = lax.psum_scatter(
            jnp.dot(
                tile, masked, precision=lax.Precision.HIGHEST, preferred_element_type=jnp.float32
            ),
            "cell",
            scatter_dimension=0,
            tiled=True,
        )
        own_factors = lax.dynamic_slice_in_dim(
            factors, lax.axis_index("cell") * share_rows, share_rows, 0
        )
        weighted = share * own_factors[:, None]
        back = back_rows(lax.all_gather(weighted, "cell", axis=0, tiled=True))
        back = lax.psum(back, "dp")
        smooth = smoothing(masked, strength)
        image = maskf * (back + smooth)
        return image[None]

    first_image = apply_hessian(probes)
    second_image = apply_hessian(first_image)
    return (first_image, second_image)


def solution(mesh):
    return jax.shard_map(
        local,
        mesh=mesh,
        in_specs=(
            P("section", "cell", None),
            P("section", "dp", "cell"),
            P("section", "dp"),
            P("section", "cell"),
            P("section", "cell"),
        ),
        out_specs=(P("section", "cell", None), P("section", "cell", None)),
        check_vma=False,
    )
```

profile of v0, /device:TPU:0, one launch (start us, length us, event | category | flops | bytes accessed | tf_op | source)
XLA Modules:
  0.0 175.8 jit_solution(3304047086958585981)
XLA Ops:
  8.1 1.0 copy-done
  9.1 4.7 %fusion.8 = f32[1024,128]{0,1:T(8,128)} fusion(f32[1,1024,768]{2,1,0:T(8,128)S(1)} %copy-done, f32[1,768,128]{2,1,0:T(8,128)} %param.5, f32[768]{0:T(1024)S(1)} %convert_reduce_fusion), kind=kOutput, calls=%fused_computation.8 | convolution fusion | flops 1208057856 | bytes 4066304 | tf_op jit(solution)/shard_map/dot_general | solution.py:45
  13.8 1.2 copy.7
  15.8 5.6 %collective-permute-start = (f32[768,128]{0,1:T(8,128)}, f32[768,128]{0,1:T(8,128)}, u32[]{:S(2)}, u32[]{:S(2)}) collective-permute-start(f32[768,128]{0,1:T(8,128)} %bitcast_multiply_fusion), channel_id=1, source_target_pairs={{0,16},{1,17},{2,18},{3,19},{4,20},{5,21},{6,22},{7,23},{8,24},{9,... | collective-permute-start | bytes 1179656 | tf_op jit(solution)/shard_map/ppermute | solution.py:10
  22.1 7.2 %collective-permute-done = f32[768,128]{0,1:T(8,128)} collective-permute-done((f32[768,128]{0,1:T(8,128)}, f32[768,128]{0,1:T(8,128)}, u32[]{:S(2)}, u32[]{:S(2)}) %collective-permute-start) | collective-permute-done | bytes 393248 | tf_op jit(solution)/shard_map/ppermute | solution.py:10
  29.3 1.8 %subtract_multiply_fusion.1 = f32[768,128]{0,1:T(8,128)} fusion(f32[768,128]{0,1:T(8,128)} %collective-permute-done, f32[768]{0:T(1024)S(1)} %fusion.23, f32[768]{0:T(1024)S(1)} %convert_reduce_fusion, f32[1,768,128]{1,2,0:T(8,128)S(1)} %copy.7), kind=kLoop, calls=%fused_computation.17 | loop fusion | flops 294912 | bytes 1185792 | tf_op jit(solution)/shard_map/mul | solution.py:37
  31.1 1.3 collective-permute-start.1
  32.4 5.9 %reduce-scatter.3.cloned.1.call-done = f32[256,128]{0,1:T(8,128)} async-done(((f32[1024,128]{0,1:T(8,128)}), f32[256,128]{0,1:T(8,128)}) %reduce-scatter.3.cloned.1.call-update) | async-done | bytes 131088 | tf_op jit(solution)/shard_map/reduce_scatter | solution.py:44
  38.3 0.9 broadcast_multiply_fusion.2
  39.2 15.9 %all_gather.6 = f32[1024,128]{0,1:T(8,128)S(1)} all-gather(f32[256,128]{0,1:T(8,128)S(1)} %broadcast_multiply_fusion.2), channel_id=1, replica_groups=mesh['section'=2,'dp'=4,'cell'=4] {'cell'}, dimensions={0}, use_global_device_ids=true | all-gather | bytes 655360 | tf_op jit(solution)/shard_map/all_gather | solution.py:56
  55.1 2.6 %fusion.14 = f32[768,128]{0,1:T(8,128)} fusion(f32[1024,128]{0,1:T(8,128)S(1)} %all_gather.6, f32[1,1024,768]{2,1,0:T(8,128)S(1)} %copy-done), kind=kOutput, calls=%fused_computation.10 | convolution fusion | flops 1207959552 | bytes 4063232 | tf_op jit(solution)/shard_map/dot_general | solution.py:27
  58.5 30.1 %all-reduce.3.cloned.1.call-done = f32[768,128]{0,1:T(8,128)} async-done(((f32[768,128]{0,1:T(8,128)}), f32[768,128]{0,1:T(8,128)}) %all-reduce.3.cloned.1.call-update) | async-done | bytes 393232 | tf_op jit(solution)/shard_map/psum | solution.py:57
  88.6 2.0 %broadcast_multiply_fusion = (f32[768,128]{0,1:T(8,128)S(1)}, f32[1,768,128]{1,2,0:T(8,128)}) fusion(f32[768]{0:T(1024)S(1)} %convert_reduce_fusion, f32[768,128]{0,1:T(8,128)} %all-reduce.3.cloned.1.call-done, f32[768,128]{0,1:T(8,128)} %subtract_multiply_fusion.1, f32[768,128]{0,1:T(8,128)} %copy-done.2), kind=kLoop, calls=%fused_computation.20 | loop fusion | flops 393216 | bytes 1969152 | tf_op jit(solution)/shard_map/mul | solution.py:42
  90.7 4.2 %fusion.11 = f32[1024,128]{0,1:T(8,128)} fusion(f32[768,128]{0,1:T(8,128)S(1)} %get-tuple-element.4, f32[1,1024,768]{2,1,0:T(8,128)S(1)} %copy-done), kind=kOutput, calls=%fused_computation.9 | convolution fusion | flops 1207959552 | bytes 4063232 | tf_op jit(solution)/shard_map/dot_general | solution.py:45
  94.9 3.4 %collective-permute-start.2 = (f32[768,128]{0,1:T(8,128)S(1)}, f32[768,128]{0,1:T(8,128)S(1)}, u32[]{:S(2)}, u32[]{:S(2)}) collective-permute-start(f32[768,128]{0,1:T(8,128)S(1)} %get-tuple-element.4), channel_id=1, source_target_pairs={{0,16},{1,17},{2,18},{3,19},{4,20},{5,21},{6,22},{7,23},{8,24},{9,... | collective-permute-start | bytes 1179656 | tf_op jit(solution)/shard_map/ppermute | solution.py:10
  98.3 7.2 %collective-permute-done.2 = f32[768,128]{0,1:T(8,128)S(1)} collective-permute-done((f32[768,128]{0,1:T(8,128)S(1)}, f32[768,128]{0,1:T(8,128)S(1)}, u32[]{:S(2)}, u32[]{:S(2)}) %collective-permute-start.2) | collective-permute-done | bytes 393248 | tf_op jit(solution)/shard_map/ppermute | solution.py:10
  106.4 1.4 collective-permute-start.3
  107.8 8.9 %reduce-scatter.5.cloned.1.call-done = f32[256,128]{0,1:T(8,128)} async-done(((f32[1024,128]{0,1:T(8,128)}), f32[256,128]{0,1:T(8,128)}) %reduce-scatter.5.cloned.1.call-update) | async-done | bytes 131088 | tf_op jit(solution)/shard_map/reduce_scatter | solution.py:44
  116.7 0.9 broadcast_multiply_fusion.1
  117.6 15.8 %all_gather.7 = f32[1024,128]{0,1:T(8,128)S(1)} all-gather(f32[256,128]{0,1:T(8,128)S(1)} %broadcast_multiply_fusion.1), channel_id=1, replica_groups=mesh['section'=2,'dp'=4,'cell'=4] {'cell'}, dimensions={0}, use_global_device_ids=true | all-gather | bytes 655360 | tf_op jit(solution)/shard_map/all_gather | solution.py:56
  133.4 2.6 %fusion.17 = f32[768,128]{0,1:T(8,128)} fusion(f32[1024,128]{0,1:T(8,128)S(1)} %all_gather.7, f32[1,1024,768]{2,1,0:T(8,128)S(1)} %copy-done), kind=kOutput, calls=%fused_computation.11 | convolution fusion | flops 1207959552 | bytes 4063232 | tf_op jit(solution)/shard_map/dot_general | solution.py:27
  137.0 30.1 %all-reduce.5.cloned.1.call-done = f32[768,128]{0,1:T(8,128)} async-done(((f32[768,128]{0,1:T(8,128)}), f32[768,128]{0,1:T(8,128)}) %all-reduce.5.cloned.1.call-update) | async-done | bytes 393232 | tf_op jit(solution)/shard_map/psum | solution.py:57
  167.1 1.3 multiply_bitcast_fusion
  168.4 0.9 copy.9
  (23 shorter events, 5.0 us)
Async XLA Ops:
  7.2 1.9 %copy-start = (f32[1,1024,768]{2,1,0:T(8,128)S(1)}, f32[1,1024,768]{2,1,0:T(8,128)}, u32[]{:S(2)}) copy-start(f32[1,1024,768]{2,1,0:T(8,128)} %param.6) | copy-start | bytes 9437188
  7.2 14.9 %copy-start.3 = (f32[1,768]{1,0:T(1,128)S(1)}, f32[1,768]{1,0:T(1,128)}, u32[]{:S(2)}) copy-start(f32[1,768]{1,0:T(1,128)} %param.9) | copy-start | bytes 9220
  7.2 31.1 %reduce-scatter.3.cloned.1.call-start = ((), (), s32[]{:S(2)}) async-start(), calls=%async_computation.2 | async-start | bytes 655360 | tf_op jit(solution)/shard_map/reduce_scatter | solution.py:44
  13.8 74.9 %all-reduce.3.cloned.1.call-start = ((), (), s32[]{:S(2)}) async-start(), calls=%async_computation.3 | async-start | bytes 786432 | tf_op jit(solution)/shard_map/psum | solution.py:57
  15.8 13.5 %collective-permute-start = (f32[768,128]{0,1:T(8,128)}, f32[768,128]{0,1:T(8,128)}, u32[]{:S(2)}, u32[]{:S(2)}) collective-permute-start(f32[768,128]{0,1:T(8,128)} %bitcast_multiply_fusion), channel_id=1, source_target_pairs={{0,16},{1,17},{2,18},{3,19},{4,20},{5,21},{6,22},{7,23},{8,24},{9,... | collective-permute-start | bytes 1179656 | tf_op jit(solution)/shard_map/ppermute | solution.py:10
  31.1 26.7 %collective-permute-start.1 = (f32[768,128]{0,1:T(8,128)}, f32[768,128]{0,1:T(8,128)S(1)}, u32[]{:S(2)}, u32[]{:S(2)}) collective-permute-start(f32[768,128]{0,1:T(8,128)} %subtract_multiply_fusion.1), channel_id=1, source_target_pairs={{16,0},{17,1},{18,2},{19,3},{20,4},{21,5},{22,6},{23,7},{24,8},{25... | collective-permute-start | bytes 1179656 | tf_op jit(solution)/shard_map/ppermute | solution.py:10
  57.7 59.0 %reduce-scatter.5.cloned.1.call-start = ((), (), s32[]{:S(2)}) async-start(), calls=%async_computation.4 | async-start | bytes 655360 | tf_op jit(solution)/shard_map/reduce_scatter | solution.py:44
  57.8 0.7 copy-start.2
  94.9 72.2 %all-reduce.5.cloned.1.call-start = ((), (), s32[]{:S(2)}) async-start(), calls=%async_computation.5 | async-start | bytes 786432 | tf_op jit(solution)/shard_map/psum | solution.py:57
  94.9 10.7 %collective-permute-start.2 = (f32[768,128]{0,1:T(8,128)S(1)}, f32[768,128]{0,1:T(8,128)S(1)}, u32[]{:S(2)}, u32[]{:S(2)}) collective-permute-start(f32[768,128]{0,1:T(8,128)S(1)} %get-tuple-element.4), channel_id=1, source_target_pairs={{0,16},{1,17},{2,18},{3,19},{4,20},{5,21},{6,22},{7,23},{8,24},{9,... | collective-permute-start | bytes 1179656 | tf_op jit(solution)/shard_map/ppermute | solution.py:10
  106.4 29.7 %copy-start.1 = (f32[1,768,128]{1,2,0:T(8,128)S(1)}, f32[1,768,128]{1,2,0:T(8,128)}, u32[]{:S(2)}) copy-start(f32[1,768,128]{1,2,0:T(8,128)} %get-tuple-element.5) | copy-start | bytes 1179652
  106.4 30.6 %collective-permute-start.3 = (f32[768,128]{0,1:T(8,128)}, f32[768,128]{0,1:T(8,128)}, u32[]{:S(2)}, u32[]{:S(2)}) collective-permute-start(f32[768,128]{0,1:T(8,128)} %subtract_multiply_fusion), channel_id=1, source_target_pairs={{16,0},{17,1},{18,2},{19,3},{20,4},{21,5},{22,6},{23,7},{24,8},{25... | collective-permute-start | bytes 1179656 | tf_op jit(solution)/shard_map/ppermute | solution.py:10
Sparse Core Ops, SparseCore 0:
  13.9 24.3 reduce-scatter.2
  57.8 30.7 all-reduce.2
  95.0 21.6 reduce-scatter.4
  136.2 30.8 all-reduce.4
where the time goes:
time: 176 us
  waiting for transfers between devices  89.5 us (51%)
  blocking collectives  31.7 us (18%)
  matrix products  14.1 us (8%)
  between operations  13.9 us (8%)
  starting transfers between devices  11.9 us (7%)
  other arithmetic  10.1 us (6%)
  local copies, waits for them, and re-layouts  4.73 us (3%)
    psum x2, waiting for transfers between devices, apply_hessian(): back = lax.psum(back, 'dp')  60.2 us
    all_gather x2, blocking collectives, apply_hessian(): back = back_rows(lax.all_gather(weighted, 'cell', axis=0, tiled=True))  31.7 us
    reduce_scatter x2, waiting for transfers between devices, apply_hessian(): lax.psum_scatter(jnp.dot(tile, masked, precision=lax.Precision.HIGHEST, p...  14.7 us
    ppermute x4, waiting for transfers between devices, shifted(): return lax.ppermute(value, axis, pairs)  14.5 us
    ppermute x4, starting transfers between devices, shifted(): return lax.ppermute(value, axis, pairs)  11.7 us
    dot_general x2, matrix products, apply_hessian(): jnp.dot(tile, masked, precision=lax.Precision.HIGHEST, preferred_element_...  8.84 us
    dot_general x2, matrix products, back_rows(): lax.dot_general(tile, incoming, (((0,), (0,)), ((), ())), precision=lax.P...  5.25 us
    unnamed x11, local copies, waits for them, and re-layouts  4.73 us
  transfers between devices with their start and end apart: 8, of which 6 were waited for; matrix products, arithmetic and copies ran while one was open for 8% of the time, Pallas kernels for 0%

commit v1 on v0

v1 whole, which is shorter than its diff:
```python
import jax
import jax.numpy as jnp
from jax import lax
from jax.sharding import PartitionSpec as P

CHUNKS = 1


def xor_pairs(axis, stride):
    return [(i, i ^ stride) for i in range(lax.axis_size(axis))]


def swap(value, axis, stride):
    return lax.ppermute(value, axis, xor_pairs(axis, stride))


def shifted(value, axis, by):
    length = lax.axis_size(axis)
    pairs = [(i, i + by) for i in range(length) if 0 <= i + by < length]
    return lax.ppermute(value, axis, pairs)


def class_weight(labels):
    return jnp.where(
        labels == 0, 1.0, jnp.where(labels == 1, 0.5, jnp.where(labels == 2, 0.25, 0.125))
    ).astype(jnp.float32)


def local(probes, jacobian, classes, active, coupling):
    tile = jacobian[0]
    factors = class_weight(classes[0])[None, :]
    cells = tile.shape[1]
    half = cells // 2
    cell_parts = lax.axis_size("cell")
    dp_parts = lax.axis_size("dp")
    here = lax.axis_index("cell")
    side = lax.axis_index("dp") % 2
    first_section = lax.axis_index("section") == 0

    def own_first(value, axis):
        size = value.shape[axis] // 2
        return jnp.concatenate(
            [
                lax.dynamic_slice_in_dim(value, side * size, size, axis),
                lax.dynamic_slice_in_dim(value, (1 - side) * size, size, axis),
            ],
            axis=axis,
        )

    def reorder(value):
        size = value.shape[0] // cell_parts
        return jnp.concatenate(
            [
                lax.dynamic_slice_in_dim(value, (here ^ x) * size, size, 0)
                for x in range(cell_parts)
            ],
            axis=0,
        )

    tile = own_first(tile, 1)
    maskf = own_first(active[0].astype(jnp.float32), 0)[None, :]
    strength = jnp.where(first_section, 0.0, own_first(coupling[0], 0)[None, :half])
    strength_next = shifted(strength, "section", -1)

    def forward(masked):
        return lax.dot_general(
            masked,
            tile,
            (((1,), (1,)), ((), ())),
            precision=lax.Precision.HIGH,
            preferred_element_type=jnp.float32,
        )

    def backward(weighted):
        return jnp.dot(
            weighted, tile, precision=lax.Precision.HIGH, preferred_element_type=jnp.float32
        )

    def sum_cells(part):
        size = part.shape[0] // cell_parts
        total = part[:size]
        for x in range(cell_parts - 1, 0, -1):
            total = total + swap(part[x * size : (x + 1) * size], "cell", x)
        total = total * factors
        blocks = [total] + [swap(total, "cell", x) for x in range(1, cell_parts)]
        return jnp.concatenate(blocks, axis=0)

    def sum_data(part):
        total = part[:, :half] + swap(part[:, half:], "dp", 1)
        stride = 2
        while stride < dp_parts:
            total = total + swap(total, "dp", stride)
            stride *= 2
        return total

    def smoothing(masked):
        below = shifted(masked, "section", 1)
        above = shifted(masked, "section", -1)
        return strength * (masked - below) + strength_next * (masked - above)

    def apply_hessian(field):
        masked = field * maskf
        smooth = smoothing(masked[:, :half])
        back = sum_data(backward(sum_cells(forward(masked))))
        image = maskf[:, :half] * (back + smooth)
        return jnp.concatenate([image, swap(image, "dp", 1)], axis=1)

    def chunked(function, value):
        size = value.shape[0] // CHUNKS
        return [function(value[i * size : (i + 1) * size]) for i in range(CHUNKS)]

    def finish(parts):
        rows = jnp.concatenate([reorder(part) for part in parts], axis=0)
        return own_first(rows, 1).T[None]

    start = probes[0].T
    start = own_first(start, 1)
    first = chunked(lambda part: apply_hessian(reorder(part)), start)
    second = [apply_hessian(part) for part in first]
    return finish(first), finish(second)


def solution(mesh):
    return jax.shard_map(
        local,
        mesh=mesh,
        in_specs=(
            P("section", "cell", None),
            P("section", "dp", "cell"),
            P("section", "dp"),
            P("section", "cell"),
            P("section", "cell"),
        ),
        out_specs=(P("section", "cell", None), P("section", "cell", None)),
        check_vma=False,
    )
```

time: 176 us -> 105 us (0.60)
  waiting for transfers between devices: 89.5 us -> 52.3 us
  blocking collectives: 31.7 us -> 0 us
  starting transfers between devices: 11.9 us -> 32.7 us
  between operations: 13.9 us -> 1.04 us
  matrix products: 14.1 us -> 5.56 us
  other arithmetic: 10.1 us -> 4.76 us
  local copies, waits for them, and re-layouts: 4.73 us -> 8.21 us
    psum x2 -> x0, waiting for transfers between devices: 60.2 us -> none  [apply_hessian(): back = lax.psum(back, 'dp')]
    ppermute x0 -> x18, waiting for transfers between devices: none -> 41 us  [swap(): return lax.ppermute(value, axis, xor_pairs(axis, stride))]
    all_gather x2 -> x0, blocking collectives: 31.7 us -> none  [apply_hessian(): back = back_rows(lax.all_gather(weighted, 'cell', axis=0, tiled=True))]
    ppermute x0 -> x18, starting transfers between devices: none -> 21.4 us  [swap(): return lax.ppermute(value, axis, xor_pairs(axis, stride))]
    reduce_scatter x2 -> x0, waiting for transfers between devices: 14.7 us -> none  [apply_hessian(): lax.psum_scatter(jnp.dot(tile, masked, precision=lax.Precision.HIGHEST, p...]
    dot_general x4, matrix products: 14.1 us -> 5.56 us  [the longest x2 3.41 us: forward(): lax.dot_general(masked, tile, (((1,), (1,)), ((), ())), precision=lax.Pre...]
    mul x6, other arithmetic: 7.25 us -> 1.5 us  [the longest x2 1.37 us: apply_hessian(): image = maskf[:, :half] * (back + smooth)]
    ppermute x4 -> x5, waiting for transfers between devices: 14.5 us -> 11.3 us  [shifted(): return lax.ppermute(value, axis, pairs)]
  transfers between devices with their start and end apart: 8 -> 23, of which waited for: 6 -> 13; matrix products, arithmetic and copies ran while one was open for 8% -> 4% of each run, Pallas kernels for 0% -> 0%
where the time goes in v1:
time: 105 us
  waiting for transfers between devices  52.3 us (50%)
  starting transfers between devices  32.7 us (31%)
  local copies, waits for them, and re-layouts  8.21 us (8%)
  matrix products  5.56 us (5%)
  other arithmetic  4.76 us (5%)
    ppermute x18, waiting for transfers between devices, swap(): return lax.ppermute(value, axis, xor_pairs(axis, stride))  41 us
    ppermute x18, starting transfers between devices, swap(): return lax.ppermute(value, axis, xor_pairs(axis, stride))  21.4 us
    ppermute x5, starting transfers between devices, shifted(): return lax.ppermute(value, axis, pairs)  11.3 us
    ppermute x5, waiting for transfers between devices, shifted(): return lax.ppermute(value, axis, pairs)  11.3 us
    dot_general x2, matrix products, forward(): lax.dot_general(masked, tile, (((1,), (1,)), ((), ())), precision=lax.Pre...  3.41 us
    unnamed x14, local copies, waits for them, and re-layouts  2.6 us
    dynamic_slice x3, local copies, waits for them, and re-layouts, own_first(): lax.dynamic_slice_in_dim(value, side * size, size, axis)  2.23 us
    dot_general x2, matrix products, backward(): jnp.dot(weighted, tile, precision=lax.Precision.HIGH, preferred_element_t...  2.15 us
  transfers between devices with their start and end apart: 23, of which 13 were waited for; matrix products, arithmetic and copies ran while one was open for 4% of the time, Pallas kernels for 0%

profile of v1, /device:TPU:0, one launch (start us, length us, event | category | flops | bytes accessed | tf_op | source)
XLA Modules:
  0.0 104.5 jit_solution(12888543765546219053)
XLA Ops:
  0.7 2.1 %dynamic-slice_bitcast_fusion.1 = (f32[1024,384]{1,0:T(8,128)S(1)}, f32[1024,384]{1,0:T(8,128)S(1)}) fusion(f32[1,1024,768]{2,1,0:T(8,128)} %param.6, s32[]{:T(128)S(6)} %select_n.67, s32[]{:T(128)S(6)} %select_n.68), kind=kLoop, calls=%fused_computation.2 | loop fusion | bytes 6291464 | tf_op jit(solution)/shard_map/dynamic_slice | solution.py:44
  4.9 1.7 %fusion.3 = f32[128,1024]{1,0:T(8,128)S(1)} fusion(f32[128,768]{1,0:T(8,128)S(1)} %maximum_multiply_fusion, f32[1024,384]{1,0:T(8,128)S(1)} %get-tuple-element.9, f32[1024,384]{1,0:T(8,128)S(1)} %get-tuple-element.8), kind=kOutput, calls=%fused_computation.6 | convolution fusion | flops 604766208 | bytes 4063232 | tf_op jit(solution)/shard_map/dot_general | solution.py:66
  6.7 5.1 %collective-permute-start = (f32[32,1024]{1,0:T(8,128)S(1)}, f32[32,1024]{1,0:T(8,128)S(1)}, u32[]{:S(2)}, u32[]{:S(2)}) collective-permute-start(f32[32,1024]{1,0:T(8,128)S(1)} %get-tuple-element.13), channel_id=1, source_target_pairs={{0,3},{1,2},{2,1},{3,0},{4,7},{5,6},{6,5},{7,4},{8,11},{9,10},{10,... | collective-permute-start | bytes 393224 | tf_op jit(solution)/shard_map/ppermute | solution.py:14
  12.4 3.8 %collective-permute-done = f32[32,1024]{1,0:T(8,128)S(1)} collective-permute-done((f32[32,1024]{1,0:T(8,128)S(1)}, f32[32,1024]{1,0:T(8,128)S(1)}, u32[]{:S(2)}, u32[]{:S(2)}) %collective-permute-start) | collective-permute-done | bytes 131104 | tf_op jit(solution)/shard_map/ppermute | solution.py:14
  16.2 6.6 %collective-permute-done.1 = f32[32,1024]{1,0:T(8,128)S(1)} collective-permute-done((f32[32,1024]{1,0:T(8,128)S(1)}, f32[32,1024]{1,0:T(8,128)S(1)}, u32[]{:S(2)}, u32[]{:S(2)}) %collective-permute-start.1) | collective-permute-done | bytes 131104 | tf_op jit(solution)/shard_map/ppermute | solution.py:14
  23.0 3.0 %collective-permute-start.4 = (f32[32,1024]{1,0:T(8,128)S(1)}, f32[32,1024]{1,0:T(8,128)S(1)}, u32[]{:S(2)}, u32[]{:S(2)}) collective-permute-start(f32[32,1024]{1,0:T(8,128)S(1)} %fusion.24), channel_id=1, source_target_pairs={{0,2},{1,3},{2,0},{3,1},{4,6},{5,7},{6,4},{7,5},{8,10},{9,11},{10,... | collective-permute-start | bytes 393224 | tf_op jit(solution)/shard_map/ppermute | solution.py:14
  27.4 2.0 %collective-permute-done.3 = f32[32,1024]{1,0:T(8,128)S(1)} collective-permute-done((f32[32,1024]{1,0:T(8,128)S(1)}, f32[32,1024]{1,0:T(8,128)S(1)}, u32[]{:S(2)}, u32[]{:S(2)}) %collective-permute-start.3) | collective-permute-done | bytes 131104 | tf_op jit(solution)/shard_map/ppermute | solution.py:14
  29.3 6.2 %collective-permute-done.4 = f32[32,1024]{1,0:T(8,128)S(1)} collective-permute-done((f32[32,1024]{1,0:T(8,128)S(1)}, f32[32,1024]{1,0:T(8,128)S(1)}, u32[]{:S(2)}, u32[]{:S(2)}) %collective-permute-start.4) | collective-permute-done | bytes 131104 | tf_op jit(solution)/shard_map/ppermute | solution.py:14
  40.1 5.9 %collective-permute-start.8 = (f32[128,384]{1,0:T(8,128)}, f32[128,384]{1,0:T(8,128)}, u32[]{:S(2)}, u32[]{:S(2)}) collective-permute-start(f32[128,384]{1,0:T(8,128)} %slice.68), channel_id=1, source_target_pairs={{0,16},{1,17},{2,18},{3,19},{4,20},{5,21},{6,22},{7,23},{8,24},{9,... | collective-permute-start | bytes 589832 | tf_op jit(solution)/shard_map/ppermute | solution.py:20
  46.0 1.7 %slice_add_fusion.1 = f32[128,384]{1,0:T(8,128)} fusion(f32[128,384]{1,0:T(8,128)} %collective-permute-done.6, f32[128,768]{1,0:T(8,128)} %copy-done), kind=kLoop, calls=%fused_computation.53 | loop fusion | flops 49152 | bytes 589824 | tf_op jit(solution)/shard_map/add | solution.py:89
  47.7 1.5 %collective-permute-start.7 = (f32[128,384]{1,0:T(8,128)}, f32[128,384]{1,0:T(8,128)}, u32[]{:S(2)}, u32[]{:S(2)}) collective-permute-start(f32[128,384]{1,0:T(8,128)} %slice_add_fusion.1), channel_id=1, source_target_pairs={{0,8},{4,12},{8,0},{12,4},{1,9},{5,13},{9,1},{13,5},{2,10},{6,14},... | collective-permute-start | bytes 589832 | tf_op jit(solution)/shard_map/ppermute | solution.py:14
  50.5 4.2 %collective-permute-done.9 = f32[1,384]{1,0:T(1,128)} collective-permute-done((f32[1,384]{1,0:T(1,128)S(1)}, f32[1,384]{1,0:T(1,128)}, u32[]{:S(2)}, u32[]{:S(2)}) %collective-permute-start.9) | collective-permute-done | bytes 1568 | tf_op jit(solution)/shard_map/ppermute | solution.py:20
  57.4 1.4 %collective-permute-done.11 = f32[128,384]{1,0:T(8,128)S(1)} collective-permute-done((f32[128,384]{1,0:T(8,128)S(1)}, f32[128,384]{1,0:T(8,128)S(1)}, u32[]{:S(2)}, u32[]{:S(2)}) %collective-permute-start.11) | collective-permute-done | bytes 196640 | tf_op jit(solution)/shard_map/ppermute | solution.py:14
  58.9 1.7 %fusion.1 = f32[128,1024]{1,0:T(8,128)S(1)} fusion(f32[128,768]{1,0:T(8,128)S(1)} %fusion.18, f32[1024,384]{1,0:T(8,128)S(1)} %get-tuple-element.9, f32[1024,384]{1,0:T(8,128)S(1)} %get-tuple-element.8), kind=kOutput, calls=%fused_computation.4 | convolution fusion | flops 604766208 | bytes 4063232 | tf_op jit(solution)/shard_map/dot_general | solution.py:66
  60.6 2.3 %collective-permute-start.12 = (f32[32,1024]{1,0:T(8,128)S(1)}, f32[32,1024]{1,0:T(8,128)S(1)}, u32[]{:S(2)}, u32[]{:S(2)}) collective-permute-start(f32[32,1024]{1,0:T(8,128)S(1)} %get-tuple-element.10), channel_id=1, source_target_pairs={{0,3},{1,2},{2,1},{3,0},{4,7},{5,6},{6,5},{7,4},{8,11},{9,10},{10,... | collective-permute-start | bytes 393224 | tf_op jit(solution)/shard_map/ppermute | solution.py:14
  65.1 3.9 %collective-permute-done.12 = f32[32,1024]{1,0:T(8,128)S(1)} collective-permute-done((f32[32,1024]{1,0:T(8,128)S(1)}, f32[32,1024]{1,0:T(8,128)S(1)}, u32[]{:S(2)}, u32[]{:S(2)}) %collective-permute-start.12) | collective-permute-done | bytes 131104 | tf_op jit(solution)/shard_map/ppermute | solution.py:14
  68.9 7.1 %collective-permute-done.13 = f32[32,1024]{1,0:T(8,128)S(1)} collective-permute-done((f32[32,1024]{1,0:T(8,128)S(1)}, f32[32,1024]{1,0:T(8,128)S(1)}, u32[]{:S(2)}, u32[]{:S(2)}) %collective-permute-start.13) | collective-permute-done | bytes 131104 | tf_op jit(solution)/shard_map/ppermute | solution.py:14
  76.2 2.8 %collective-permute-start.16 = (f32[32,1024]{1,0:T(8,128)S(1)}, f32[32,1024]{1,0:T(8,128)S(1)}, u32[]{:S(2)}, u32[]{:S(2)}) collective-permute-start(f32[32,1024]{1,0:T(8,128)S(1)} %fusion.21), channel_id=1, source_target_pairs={{0,2},{1,3},{2,0},{3,1},{4,6},{5,7},{6,4},{7,5},{8,10},{9,11},{10,... | collective-permute-start | bytes 393224 | tf_op jit(solution)/shard_map/ppermute | solution.py:14
  79.0 1.5 %collective-permute-start.17 = (f32[32,1024]{1,0:T(8,128)S(1)}, f32[32,1024]{1,0:T(8,128)S(1)}, u32[]{:S(2)}, u32[]{:S(2)}) collective-permute-start(f32[32,1024]{1,0:T(8,128)S(1)} %fusion.21), channel_id=1, source_target_pairs={{0,3},{1,2},{2,1},{3,0},{4,7},{5,6},{6,5},{7,4},{8,11},{9,10},{10,... | collective-permute-start | bytes 393224 | tf_op jit(solution)/shard_map/ppermute | solution.py:14
  80.6 2.6 %collective-permute-done.15 = f32[32,1024]{1,0:T(8,128)S(1)} collective-permute-done((f32[32,1024]{1,0:T(8,128)S(1)}, f32[32,1024]{1,0:T(8,128)S(1)}, u32[]{:S(2)}, u32[]{:S(2)}) %collective-permute-start.15) | collective-permute-done | bytes 131104 | tf_op jit(solution)/shard_map/ppermute | solution.py:14
  83.2 6.0 %collective-permute-done.16 = f32[32,1024]{1,0:T(8,128)S(1)} collective-permute-done((f32[32,1024]{1,0:T(8,128)S(1)}, f32[32,1024]{1,0:T(8,128)S(1)}, u32[]{:S(2)}, u32[]{:S(2)}) %collective-permute-start.16) | collective-permute-done | bytes 131104 | tf_op jit(solution)/shard_map/ppermute | solution.py:14
  90.4 1.6 %collective-permute-start.20 = (f32[128,384]{1,0:T(8,128)S(1)}, f32[128,384]{1,0:T(8,128)S(1)}, u32[]{:S(2)}, u32[]{:S(2)}) collective-permute-start(f32[128,384]{1,0:T(8,128)S(1)} %slice.75), channel_id=1, source_target_pairs={{0,16},{1,17},{2,18},{3,19},{4,20},{5,21},{6,22},{7,23},{8,24},{9,... | collective-permute-start | bytes 589832 | tf_op jit(solution)/shard_map/ppermute | solution.py:20
  93.9 2.9 %collective-permute-done.20 = f32[128,384]{1,0:T(8,128)S(1)} collective-permute-done((f32[128,384]{1,0:T(8,128)S(1)}, f32[128,384]{1,0:T(8,128)S(1)}, u32[]{:S(2)}, u32[]{:S(2)}) %collective-permute-start.20) | collective-permute-done | bytes 196640 | tf_op jit(solution)/shard_map/ppermute | solution.py:20
  96.8 4.1 %collective-permute-done.21 = f32[128,384]{1,0:T(8,128)S(1)} collective-permute-done((f32[128,384]{1,0:T(8,128)S(1)}, f32[128,384]{1,0:T(8,128)S(1)}, u32[]{:S(2)}, u32[]{:S(2)}) %collective-permute-start.21) | collective-permute-done | bytes 196640 | tf_op jit(solution)/shard_map/ppermute | solution.py:20
  (74 shorter events, 21.5 us)
Async XLA Ops:
  6.7 9.5 %collective-permute-start = (f32[32,1024]{1,0:T(8,128)S(1)}, f32[32,1024]{1,0:T(8,128)S(1)}, u32[]{:S(2)}, u32[]{:S(2)}) collective-permute-start(f32[32,1024]{1,0:T(8,128)S(1)} %get-tuple-element.13), channel_id=1, source_target_pairs={{0,3},{1,2},{2,1},{3,0},{4,7},{5,6},{6,5},{7,4},{8,11},{9,10},{10,... | collective-permute-start | bytes 393224 | tf_op jit(solution)/shard_map/ppermute | solution.py:14
  11.8 11.1 %collective-permute-start.1 = (f32[32,1024]{1,0:T(8,128)S(1)}, f32[32,1024]{1,0:T(8,128)S(1)}, u32[]{:S(2)}, u32[]{:S(2)}) collective-permute-start(f32[32,1024]{1,0:T(8,128)S(1)} %get-tuple-element.15), channel_id=1, source_target_pairs={{0,2},{1,3},{2,0},{3,1},{4,6},{5,7},{6,4},{7,5},{8,10},{9,11},{10,... | collective-permute-start | bytes 393224 | tf_op jit(solution)/shard_map/ppermute | solution.py:14
  11.8 11.1 %collective-permute-start.2 = (f32[32,1024]{1,0:T(8,128)S(1)}, f32[32,1024]{1,0:T(8,128)S(1)}, u32[]{:S(2)}, u32[]{:S(2)}) collective-permute-start(f32[32,1024]{1,0:T(8,128)S(1)} %get-tuple-element.14), channel_id=1, source_target_pairs={{0,1},{1,0},{2,3},{3,2},{4,5},{5,4},{6,7},{7,6},{8,9},{9,8},{10,11... | collective-permute-start | bytes 393224 | tf_op jit(solution)/shard_map/ppermute | solution.py:14
  22.9 26.3 %copy-start.5 = (f32[1,768]{1,0:T(1,128)S(1)}, f32[1,768]{1,0:T(1,128)}, u32[]{:S(2)}) copy-start(f32[1,768]{1,0:T(1,128)} %param.9) | copy-start | bytes 9220
  22.9 6.4 %collective-permute-start.3 = (f32[32,1024]{1,0:T(8,128)S(1)}, f32[32,1024]{1,0:T(8,128)S(1)}, u32[]{:S(2)}, u32[]{:S(2)}) collective-permute-start(f32[32,1024]{1,0:T(8,128)S(1)} %fusion.24), channel_id=1, source_target_pairs={{0,1},{1,0},{2,3},{3,2},{4,5},{5,4},{6,7},{7,6},{8,9},{9,8},{10,11... | collective-permute-start | bytes 393224 | tf_op jit(solution)/shard_map/ppermute | solution.py:14
  23.0 12.6 %collective-permute-start.4 = (f32[32,1024]{1,0:T(8,128)S(1)}, f32[32,1024]{1,0:T(8,128)S(1)}, u32[]{:S(2)}, u32[]{:S(2)}) collective-permute-start(f32[32,1024]{1,0:T(8,128)S(1)} %fusion.24), channel_id=1, source_target_pairs={{0,2},{1,3},{2,0},{3,1},{4,6},{5,7},{6,4},{7,5},{8,10},{9,11},{10,... | collective-permute-start | bytes 393224 | tf_op jit(solution)/shard_map/ppermute | solution.py:14
  26.0 9.5 %collective-permute-start.5 = (f32[32,1024]{1,0:T(8,128)S(1)}, f32[32,1024]{1,0:T(8,128)S(1)}, u32[]{:S(2)}, u32[]{:S(2)}) collective-permute-start(f32[32,1024]{1,0:T(8,128)S(1)} %fusion.24), channel_id=1, source_target_pairs={{0,3},{1,2},{2,1},{3,0},{4,7},{5,6},{6,5},{7,4},{8,11},{9,10},{10,... | collective-permute-start | bytes 393224 | tf_op jit(solution)/shard_map/ppermute | solution.py:14
  38.1 7.9 %collective-permute-start.6 = (f32[128,384]{1,0:T(8,128)}, f32[128,384]{1,0:T(8,128)}, u32[]{:S(2)}, u32[]{:S(2)}) collective-permute-start(f32[128,384]{1,0:T(8,128)} %slice.67), channel_id=1, source_target_pairs={{0,4},{4,0},{8,12},{12,8},{1,5},{5,1},{9,13},{13,9},{2,6},{6,2},{1... | collective-permute-start | bytes 589832 | tf_op jit(solution)/shard_map/ppermute | solution.py:14
  38.8 17.3 %collective-permute-start.10 = (f32[128,384]{1,0:T(8,128)}, f32[128,384]{1,0:T(8,128)}, u32[]{:S(2)}, u32[]{:S(2)}) collective-permute-start(f32[128,384]{1,0:T(8,128)} %slice.68), channel_id=1, source_target_pairs={{16,0},{17,1},{18,2},{19,3},{20,4},{21,5},{22,6},{23,7},{24,8},{25... | collective-permute-start | bytes 589832 | tf_op jit(solution)/shard_map/ppermute | solution.py:20
  40.1 16.0 %collective-permute-start.8 = (f32[128,384]{1,0:T(8,128)}, f32[128,384]{1,0:T(8,128)}, u32[]{:S(2)}, u32[]{:S(2)}) collective-permute-start(f32[128,384]{1,0:T(8,128)} %slice.68), channel_id=1, source_target_pairs={{0,16},{1,17},{2,18},{3,19},{4,20},{5,21},{6,22},{7,23},{8,24},{9,... | collective-permute-start | bytes 589832 | tf_op jit(solution)/shard_map/ppermute | solution.py:20
  47.7 8.4 %collective-permute-start.7 = (f32[128,384]{1,0:T(8,128)}, f32[128,384]{1,0:T(8,128)}, u32[]{:S(2)}, u32[]{:S(2)}) collective-permute-start(f32[128,384]{1,0:T(8,128)} %slice_add_fusion.1), channel_id=1, source_target_pairs={{0,8},{4,12},{8,0},{12,4},{1,9},{5,13},{9,1},{13,5},{2,10},{6,14},... | collective-permute-start | bytes 589832 | tf_op jit(solution)/shard_map/ppermute | solution.py:14
  49.2 5.6 %collective-permute-start.9 = (f32[1,384]{1,0:T(1,128)S(1)}, f32[1,384]{1,0:T(1,128)}, u32[]{:S(2)}, u32[]{:S(2)}) collective-permute-start(f32[1,384]{1,0:T(1,128)S(1)} %get-tuple-element.7), channel_id=1, source_target_pairs={{16,0},{17,1},{18,2},{19,3},{20,4},{21,5},{22,6},{23,7},{24,8},{25... | collective-permute-start | bytes 4616 | tf_op jit(solution)/shard_map/ppermute | solution.py:20
  57.3 1.5 %collective-permute-start.11 = (f32[128,384]{1,0:T(8,128)S(1)}, f32[128,384]{1,0:T(8,128)S(1)}, u32[]{:S(2)}, u32[]{:S(2)}) collective-permute-start(f32[128,384]{1,0:T(8,128)S(1)} %add_multiply_fusion.1), channel_id=1, source_target_pairs={{0,4},{4,0},{8,12},{12,8},{1,5},{5,1},{9,13},{13,9},{2,6},{6,2},{1... | collective-permute-start | bytes 589832 | tf_op jit(solution)/shard_map/ppermute | solution.py:14
  60.6 8.3 %collective-permute-start.12 = (f32[32,1024]{1,0:T(8,128)S(1)}, f32[32,1024]{1,0:T(8,128)S(1)}, u32[]{:S(2)}, u32[]{:S(2)}) collective-permute-start(f32[32,1024]{1,0:T(8,128)S(1)} %get-tuple-element.10), channel_id=1, source_target_pairs={{0,3},{1,2},{2,1},{3,0},{4,7},{5,6},{6,5},{7,4},{8,11},{9,10},{10,... | collective-permute-start | bytes 393224 | tf_op jit(solution)/shard_map/ppermute | solution.py:14
  63.0 13.1 %collective-permute-start.13 = (f32[32,1024]{1,0:T(8,128)S(1)}, f32[32,1024]{1,0:T(8,128)S(1)}, u32[]{:S(2)}, u32[]{:S(2)}) collective-permute-start(f32[32,1024]{1,0:T(8,128)S(1)} %get-tuple-element.12), channel_id=1, source_target_pairs={{0,2},{1,3},{2,0},{3,1},{4,6},{5,7},{6,4},{7,5},{8,10},{9,11},{10,... | collective-permute-start | bytes 393224 | tf_op jit(solution)/shard_map/ppermute | solution.py:14
  64.1 11.9 %collective-permute-start.14 = (f32[32,1024]{1,0:T(8,128)S(1)}, f32[32,1024]{1,0:T(8,128)S(1)}, u32[]{:S(2)}, u32[]{:S(2)}) collective-permute-start(f32[32,1024]{1,0:T(8,128)S(1)} %get-tuple-element.11), channel_id=1, source_target_pairs={{0,1},{1,0},{2,3},{3,2},{4,5},{5,4},{6,7},{7,6},{8,9},{9,8},{10,11... | collective-permute-start | bytes 393224 | tf_op jit(solution)/shard_map/ppermute | solution.py:14
  76.1 7.1 %collective-permute-start.15 = (f32[32,1024]{1,0:T(8,128)S(1)}, f32[32,1024]{1,0:T(8,128)S(1)}, u32[]{:S(2)}, u32[]{:S(2)}) collective-permute-start(f32[32,1024]{1,0:T(8,128)S(1)} %fusion.21), channel_id=1, source_target_pairs={{0,1},{1,0},{2,3},{3,2},{4,5},{5,4},{6,7},{7,6},{8,9},{9,8},{10,11... | collective-permute-start | bytes 393224 | tf_op jit(solution)/shard_map/ppermute | solution.py:14
  76.2 13.0 %collective-permute-start.16 = (f32[32,1024]{1,0:T(8,128)S(1)}, f32[32,1024]{1,0:T(8,128)S(1)}, u32[]{:S(2)}, u32[]{:S(2)}) collective-permute-start(f32[32,1024]{1,0:T(8,128)S(1)} %fusion.21), channel_id=1, source_target_pairs={{0,2},{1,3},{2,0},{3,1},{4,6},{5,7},{6,4},{7,5},{8,10},{9,11},{10,... | collective-permute-start | bytes 393224 | tf_op jit(solution)/shard_map/ppermute | solution.py:14
  79.0 10.2 %collective-permute-start.17 = (f32[32,1024]{1,0:T(8,128)S(1)}, f32[32,1024]{1,0:T(8,128)S(1)}, u32[]{:S(2)}, u32[]{:S(2)}) collective-permute-start(f32[32,1024]{1,0:T(8,128)S(1)} %fusion.21), channel_id=1, source_target_pairs={{0,3},{1,2},{2,1},{3,0},{4,7},{5,6},{6,5},{7,4},{8,11},{9,10},{10,... | collective-permute-start | bytes 393224 | tf_op jit(solution)/shard_map/ppermute | solution.py:14
  90.3 3.0 %collective-permute-start.18 = (f32[128,384]{1,0:T(8,128)S(1)}, f32[128,384]{1,0:T(8,128)S(1)}, u32[]{:S(2)}, u32[]{:S(2)}) collective-permute-start(f32[128,384]{1,0:T(8,128)S(1)} %slice.74), channel_id=1, source_target_pairs={{0,4},{4,0},{8,12},{12,8},{1,5},{5,1},{9,13},{13,9},{2,6},{6,2},{1... | collective-permute-start | bytes 589832 | tf_op jit(solution)/shard_map/ppermute | solution.py:14
  90.4 6.4 %collective-permute-start.20 = (f32[128,384]{1,0:T(8,128)S(1)}, f32[128,384]{1,0:T(8,128)S(1)}, u32[]{:S(2)}, u32[]{:S(2)}) collective-permute-start(f32[128,384]{1,0:T(8,128)S(1)} %slice.75), channel_id=1, source_target_pairs={{0,16},{1,17},{2,18},{3,19},{4,20},{5,21},{6,22},{7,23},{8,24},{9,... | collective-permute-start | bytes 589832 | tf_op jit(solution)/shard_map/ppermute | solution.py:20
  92.0 8.9 %collective-permute-start.21 = (f32[128,384]{1,0:T(8,128)S(1)}, f32[128,384]{1,0:T(8,128)S(1)}, u32[]{:S(2)}, u32[]{:S(2)}) collective-permute-start(f32[128,384]{1,0:T(8,128)S(1)} %slice.75), channel_id=1, source_target_pairs={{16,0},{17,1},{18,2},{19,3},{20,4},{21,5},{22,6},{23,7},{24,8},{25... | collective-permute-start | bytes 589832 | tf_op jit(solution)/shard_map/ppermute | solution.py:20
  93.3 7.6 %collective-permute-start.19 = (f32[128,384]{1,0:T(8,128)S(1)}, f32[128,384]{1,0:T(8,128)S(1)}, u32[]{:S(2)}, u32[]{:S(2)}) collective-permute-start(f32[128,384]{1,0:T(8,128)S(1)} %slice_add_fusion), channel_id=1, source_target_pairs={{0,8},{4,12},{8,0},{12,4},{1,9},{5,13},{9,1},{13,5},{2,10},{6,14},... | collective-permute-start | bytes 589832 | tf_op jit(solution)/shard_map/ppermute | solution.py:14
  101.0 1.5 %collective-permute-start.22 = (f32[128,384]{1,0:T(8,128)S(1)}, f32[128,384]{1,0:T(8,128)S(1)}, u32[]{:S(2)}, u32[]{:S(2)}) collective-permute-start(f32[128,384]{1,0:T(8,128)S(1)} %add_multiply_fusion), channel_id=1, source_target_pairs={{0,4},{4,0},{8,12},{12,8},{1,5},{5,1},{9,13},{13,9},{2,6},{6,2},{1... | collective-permute-start | bytes 589832 | tf_op jit(solution)/shard_map/ppermute | solution.py:14
  (5 other events, 37.1 us)

commit v2 on v0

v2 whole, which is shorter than its diff:
```python
import functools

import jax
import jax.numpy as jnp
from jax import lax
from jax.experimental import pallas as pl
from jax.experimental.pallas import tpu as pltpu
from jax.sharding import PartitionSpec as P

MAX_CHUNKS = 1
LIMIT = 24 * 2**20
NT = (((1,), (1,)), ((), ()))
NN = (((1,), (0,)), ((), ()))
VMEM = pl.BlockSpec(memory_space=pltpu.VMEM)


def swap(value, axis, stride):
    return lax.ppermute(value, axis, [(i, i ^ stride) for i in range(lax.axis_size(axis))])


def shifted(value, axis, by):
    length = lax.axis_size(axis)
    pairs = [(i, i + by) for i in range(length) if 0 <= i + by < length]
    return lax.ppermute(value, axis, pairs)


def split(value):
    high = value.astype(jnp.bfloat16)
    return high, (value - high.astype(jnp.float32)).astype(jnp.bfloat16)


def product(value, high, low, dims):
    top, rest = split(value)
    rows = value.shape[0]
    dot = functools.partial(
        lax.dot_general, dimension_numbers=dims, preferred_element_type=jnp.float32
    )
    both = dot(jnp.concatenate([top, rest], axis=0), high)
    return both[:rows] + (both[rows:] + dot(top, low))


def call(kernel, shapes, operands, flops=0):
    return pl.pallas_call(
        kernel,
        out_shape=shapes,
        in_specs=[VMEM] * len(operands),
        out_specs=[VMEM] * len(shapes),
        compiler_params=pltpu.CompilerParams(vmem_limit_bytes=LIMIT),
        cost_estimate=pl.CostEstimate(
            flops=flops, bytes_accessed=sum(4 * o.size for o in operands), transcendentals=0
        ),
    )(*operands)


def own_first(ref, rows, side, half):
    own = pl.ds(pl.multiple_of(side * half, half), half)
    other = pl.ds(pl.multiple_of((1 - side) * half, half), half)
    return jnp.concatenate([ref[rows, own], ref[rows, other]], axis=1)


def first_kernel(chunks, parts, *refs):
    probes, tile, classes, active, coupling, high, low, mask, weight, message = refs[:10]
    blocks = refs[10:-2]
    turned, masked = refs[-2:]
    side = lax.axis_index("dp") % 2
    here = lax.axis_index("cell")
    cells, count = probes.shape
    half = cells // 2
    size = count // (chunks * parts)
    every = slice(None)

    @pl.when(pl.program_id(0) == 0)
    def _():
        keep = own_first(active, every, side, half).astype(jnp.float32)
        mask[...] = keep
        turned[...] = probes[...].T
        for chunk in range(chunks):
            for x in range(parts):
                spot = (chunk * parts + x) * size
                start = pl.multiple_of((chunk * parts + (here ^ x)) * size, size)
                masked[spot : spot + size, :] = (
                    own_first(turned, pl.ds(start, size), side, half) * keep
                )
        message[:count, :] = masked[:, :half]
        own = own_first(coupling, every, side, half)[:, :half]
        message[count:, :] = jnp.broadcast_to(own, (8, half))
        labels = classes[...]
        weight[...] = jnp.where(
            labels == 0, 1.0, jnp.where(labels == 1, 0.5, jnp.where(labels == 2, 0.25, 0.125))
        ).astype(jnp.float32)

    top, rest = split(own_first(tile, every, side, half))
    high[...] = top
    low[...] = rest
    out = product(masked[...], top, rest, NT)
    for index, block in enumerate(blocks):
        block[...] = out[index * size : (index + 1) * size]


def first_forward(probes, tile, classes, active, coupling, chunks):
    parts = lax.axis_size("cell")
    cells, count = probes.shape
    data = tile.shape[0]
    size = count // (chunks * parts)
    step = 256 if data % 256 == 0 else data
    whole = lambda shape: pl.BlockSpec(shape, lambda i: (0,) * len(shape))
    shape = jax.ShapeDtypeStruct
    rows = pl.BlockSpec((step, cells), lambda i: (i, 0))
    outs = pl.pallas_call(
        functools.partial(first_kernel, chunks, parts),
        grid=(data // step,),
        in_specs=[
            whole((cells, count)),
            rows,
            whole((1, data)),
            whole((1, cells)),
            whole((1, cells)),
        ],
        out_specs=[
            rows,
            rows,
            whole((1, cells)),
            whole((1, data)),
            whole((count + 8, cells // 2)),
        ]
        + [pl.BlockSpec((size, step), lambda i: (0, i))] * (chunks * parts),
        out_shape=[
            shape((data, cells), jnp.bfloat16),
            shape((data, cells), jnp.bfloat16),
            shape((1, cells), jnp.float32),
            shape((1, data), jnp.float32),
            shape((count + 8, cells // 2), jnp.float32),
        ]
        + [shape((size, data), jnp.float32)] * (chunks * parts),
        scratch_shapes=[
            pltpu.VMEM((count, cells), jnp.float32),
            pltpu.VMEM((count, cells), jnp.float32),
        ],
        compiler_params=pltpu.CompilerParams(vmem_limit_bytes=LIMIT),
        cost_estimate=pl.CostEstimate(
            flops=6 * data * cells * count, bytes_accessed=4 * data * cells, transcendentals=0
        ),
    )(probes, tile, classes, active, coupling)
    blocks = outs[5:]
    return outs[:5], [blocks[i * parts : (i + 1) * parts] for i in range(chunks)]


def turn(high, low):
    def kernel(high, low, high_t, low_t):
        high_t[...] = high[...].T
        low_t[...] = low[...].T

    shape = jax.ShapeDtypeStruct(high.shape[::-1], jnp.bfloat16)
    return call(kernel, [shape, shape], [high, low])


def backward(blocks, high, low):
    def kernel(*refs):
        high, low, own, other = refs[-4:]
        value = jnp.concatenate([ref[...] for ref in refs[:-4]], axis=0)
        back = product(value, high[...], low[...], NN)
        half = own.shape[1]
        own[...] = back[:, :half]
        other[...] = back[:, half:]

    rows = sum(block.shape[0] for block in blocks)
    shape = jax.ShapeDtypeStruct((rows, high.shape[1] // 2), jnp.float32)
    return call(kernel, [shape, shape], [*blocks, high, low], 6 * rows * high.size)


def forward(own, other, mask, high_t, low_t):
    parts = lax.axis_size("cell")

    def kernel(own, other, mask, high_t, low_t, *outs):
        masked = jnp.concatenate([own[...], other[...]], axis=1) * mask[...]
        out = product(masked, high_t[...], low_t[...], NN)
        size = out.shape[0] // parts
        for x, ref in enumerate(outs):
            ref[...] = out[x * size : (x + 1) * size]

    rows = own.shape[0]
    shape = jax.ShapeDtypeStruct((rows // parts, high_t.shape[1]), jnp.float32)
    operands = [own, other, mask, high_t, low_t]
    return call(kernel, [shape] * parts, operands, 6 * rows * high_t.size)


def finish(halves):
    chunks = len(halves)
    parts = lax.axis_size("cell")
    rows, half = halves[0][0].shape
    size = rows // parts

    def kernel(*refs):
        out, turned = refs[-2:]
        side = lax.axis_index("dp") % 2
        here = lax.axis_index("cell")
        own = pl.ds(pl.multiple_of(side * half, half), half)
        other = pl.ds(pl.multiple_of((1 - side) * half, half), half)
        for chunk in range(chunks):
            for x in range(parts):
                start = pl.multiple_of((chunk * parts + (here ^ x)) * size, size)
                block = slice(x * size, (x + 1) * size)
                turned[pl.ds(start, size), own] = refs[2 * chunk][block, :]
                turned[pl.ds(start, size), other] = refs[2 * chunk + 1][block, :]
        out[...] = turned[...].T

    shape = jax.ShapeDtypeStruct((2 * half, chunks * rows), jnp.float32)
    return pl.pallas_call(
        kernel,
        out_shape=shape,
        in_specs=[VMEM] * (2 * chunks),
        out_specs=VMEM,
        scratch_shapes=[pltpu.VMEM(shape.shape[::-1], jnp.float32)],
        compiler_params=pltpu.CompilerParams(vmem_limit_bytes=LIMIT),
    )(*[half for pair in halves for half in pair])


def sum_cells(blocks, weight):
    got = {x: swap(blocks[x], "cell", x) for x in reversed(range(1, len(blocks)))}
    total = blocks[0]
    for x in range(1, len(blocks)):
        total = total + got[x]
    return total * weight


def gather_cells(total):
    parts = lax.axis_size("cell")
    return [total] + [swap(total, "cell", x) for x in range(1, parts)]


def sum_data(own, other):
    total = own + swap(other, "dp", 1)
    stride = 2
    while stride < lax.axis_size("dp"):
        total = total + swap(total, "dp", stride)
        stride *= 2
    return total


def neighbours(message):
    if lax.axis_size("section") == 2:
        got = swap(message, "section", 1)
        return got, got
    return shifted(message, "section", 1), shifted(message, "section", -1)


def local(probes, jacobian, classes, active, coupling):
    probes, tile = probes[0], jacobian[0]
    count, half = probes.shape[1], probes.shape[0] // 2
    parts = lax.axis_size("cell")
    chunks = MAX_CHUNKS
    while chunks > 1 and count % (8 * chunks * parts):
        chunks -= 1
    rows = count // chunks
    sections = lax.axis_size("section")
    section = lax.axis_index("section")

    (high, low, mask, weight, message), blocks = first_forward(
        probes, tile, classes, active, coupling, chunks
    )
    high_t, low_t = turn(high, low)
    mask_own = mask[:, :half]

    below, above = neighbours(message)
    strength = jnp.where(section == 0, 0.0, message[count : count + 1])
    strength_next = jnp.where(section == sections - 1, 0.0, above[count : count + 1])

    def smoothing(masked, below, above):
        return strength * (masked - below) + strength_next * (masked - above)

    def hessian(blocks, smooth):
        back = backward(gather_cells(sum_cells(blocks, weight)), high, low)
        return mask_own * (sum_data(*back) + smooth)

    def part(value, chunk):
        return value[chunk * rows : (chunk + 1) * rows]

    first = []
    for chunk in range(chunks):
        smooth = smoothing(*[part(value, chunk) for value in (message, below, above)])
        own = hessian(blocks[chunk], smooth)
        first.append((own, swap(own, "dp", 1)))
    masked = jnp.concatenate([own for own, _ in first], axis=0) * mask_own
    below, above = neighbours(masked)
    second = []
    for chunk in range(chunks):
        own, other = first[chunk]
        smooth = smoothing(*[part(value, chunk) for value in (masked, below, above)])
        own = hessian(forward(own, other, mask, high_t, low_t), smooth)
        second.append((own, swap(own, "dp", 1)))
    return finish(first)[None], finish(second)[None]


def solution(mesh):
    return jax.shard_map(
        local,
        mesh=mesh,
        in_specs=(
            P("section", "cell", None),
            P("section", "dp", "cell"),
            P("section", "dp"),
            P("section", "cell"),
            P("section", "cell"),
        ),
        out_specs=(P("section", "cell", None), P("section", "cell", None)),
        check_vma=False,
    )
```

time: 176 us -> 93.9 us (0.53)
  waiting for transfers between devices: 89.5 us -> 50.5 us
  blocking collectives: 31.7 us -> 0 us
  matrix products: 14.1 us -> 0 us
  starting transfers between devices: 11.9 us -> 25.9 us
  between operations: 13.9 us -> 0.75 us
  Pallas kernels: 0 us -> 7.87 us
  other arithmetic: 10.1 us -> 2.82 us
    psum x2 -> x0, waiting for transfers between devices: 60.2 us -> none  [apply_hessian(): back = lax.psum(back, 'dp')]
    ppermute x4 -> x20, waiting for transfers between devices: 14.5 us -> 50.5 us  [swap(): lax.ppermute(value, axis, [(i, i ^ stride) for i in range(lax.axis_size(a...]
    all_gather x2 -> x0, blocking collectives: 31.7 us -> none  [apply_hessian(): back = back_rows(lax.all_gather(weighted, 'cell', axis=0, tiled=True))]
    reduce_scatter x2 -> x0, waiting for transfers between devices: 14.7 us -> none  [apply_hessian(): lax.psum_scatter(jnp.dot(tile, masked, precision=lax.Precision.HIGHEST, p...]
    ppermute x4 -> x20, starting transfers between devices: 11.7 us -> 25.9 us  [swap(): lax.ppermute(value, axis, [(i, i ^ stride) for i in range(lax.axis_size(a...]
    dot_general x4 -> x0, matrix products: 14.1 us -> none  [the longest x2 8.84 us: apply_hessian(): jnp.dot(tile, masked, precision=lax.Precision.HIGHEST, preferred_element_...]
    pallas_call x0 -> x7, Pallas kernels: none -> 7.87 us  [the longest x4 3.94 us: call(): pl.pallas_call(kernel, out_shape=shapes, in_specs=[VMEM] * len(operands),...]
    mul x6 -> x5, other arithmetic: 7.25 us -> 1.85 us  [the longest x1 1 us: local(): masked = jnp.concatenate([own for own, _ in first], axis=0) * mask_own]
  transfers between devices with their start and end apart: 8 -> 20, of which waited for: 6 -> 15; matrix products, arithmetic and copies ran while one was open for 8% -> 3% of each run, Pallas kernels for 0% -> 2%
where the time goes in v2:
time: 93.9 us; the launch traced here: 93.5 us
  waiting for transfers between devices  50.5 us (54%)
  starting transfers between devices  25.9 us (28%)
  Pallas kernels  7.87 us (8%)
  local copies, waits for them, and re-layouts  5.64 us (6%)
  other arithmetic  2.82 us (3%)
    ppermute x20, waiting for transfers between devices, swap(): lax.ppermute(value, axis, [(i, i ^ stride) for i in range(lax.axis_size(a...  50.5 us
    ppermute x20, starting transfers between devices, swap(): lax.ppermute(value, axis, [(i, i ^ stride) for i in range(lax.axis_size(a...  25.9 us
    unnamed x14, local copies, waits for them, and re-layouts  4.94 us
    pallas_call x4, Pallas kernels, call(): pl.pallas_call(kernel, out_shape=shapes, in_specs=[VMEM] * len(operands),...  3.94 us
    pallas_call x1, Pallas kernels, first_forward(): pl.pallas_call(functools.partial(first_kernel, chunks, parts), grid=(data...  2.02 us
    pallas_call x2, Pallas kernels, finish(): pl.pallas_call(kernel, out_shape=shape, in_specs=[VMEM] * (2 * chunks), o...  1.9 us
  transfers between devices with their start and end apart: 20, of which 15 were waited for; matrix products, arithmetic and copies ran while one was open for 3% of the time, Pallas kernels for 2%

profile of v2, /device:TPU:0, one launch (start us, length us, event | category | flops | bytes accessed | tf_op | source)
XLA Modules:
  0.0 93.5 jit_solution(11603267595622689823)
XLA Ops:
  0.6 1.9 %copy-done = f32[1,1024,768]{2,1,0:T(8,128)S(1)} copy-done((f32[1,1024,768]{2,1,0:T(8,128)S(1)}, f32[1,1024,768]{2,1,0:T(8,128)}, u32[]{:S(2)}) %copy-start) | copy-done | bytes 3145752
  5.6 2.0 %shard_map.68 = (bf16[1024,768]{1,0:T(8,128)(2,1)S(1)}, bf16[1024,768]{1,0:T(8,128)(2,1)S(1)}, f32[1,768]{1,0:T(1,128)S(1)}, f32[1,1024]{1,0:T(1,128)S(1)}, f32[...) custom-call(f32[768,128]{1,0:T(8,128)S(1)} %bitcast.6, ...), custom_call_target="tpu_custom_call" | custom-call | flops 603979776 | bytes 3145728 | tf_op jit(solution)/shard_map/pallas_call | solution.py:109
  7.6 3.1 %collective-permute-start = (f32[32,1024]{1,0:T(8,128)S(1)}, f32[32,1024]{1,0:T(8,128)S(1)}, u32[]{:S(2)}, u32[]{:S(2)}) collective-permute-start(f32[32,1024]{1,0:T(8,128)S(1)} %get-tuple-element.23), channel_id=1, source_target_pairs={{0,1},{1,0},{2,3},{3,2},{4,5},{5,4},{6,7},{7,6},{8,9},{9,8},{10,11... | collective-permute-start | bytes 393224 | tf_op jit(solution)/shard_map/ppermute | solution.py:18
  10.7 2.6 %collective-permute-start.1 = (f32[32,1024]{1,0:T(8,128)S(1)}, f32[32,1024]{1,0:T(8,128)S(1)}, u32[]{:S(2)}, u32[]{:S(2)}) collective-permute-start(f32[32,1024]{1,0:T(8,128)S(1)} %get-tuple-element.24), channel_id=1, source_target_pairs={{0,2},{1,3},{2,0},{3,1},{4,6},{5,7},{6,4},{7,5},{8,10},{9,11},{10,... | collective-permute-start | bytes 393224 | tf_op jit(solution)/shard_map/ppermute | solution.py:18
  13.3 2.5 %collective-permute-done = f32[32,1024]{1,0:T(8,128)S(1)} collective-permute-done((f32[32,1024]{1,0:T(8,128)S(1)}, f32[32,1024]{1,0:T(8,128)S(1)}, u32[]{:S(2)}, u32[]{:S(2)}) %collective-permute-start) | collective-permute-done | bytes 131104 | tf_op jit(solution)/shard_map/ppermute | solution.py:18
  15.8 7.9 %collective-permute-done.1 = f32[32,1024]{1,0:T(8,128)S(1)} collective-permute-done((f32[32,1024]{1,0:T(8,128)S(1)}, f32[32,1024]{1,0:T(8,128)S(1)}, u32[]{:S(2)}, u32[]{:S(2)}) %collective-permute-start.1) | collective-permute-done | bytes 131104 | tf_op jit(solution)/shard_map/ppermute | solution.py:18
  23.7 2.0 %collective-permute-start.3 = (f32[32,1024]{1,0:T(8,128)S(1)}, f32[32,1024]{1,0:T(8,128)S(1)}, u32[]{:S(2)}, u32[]{:S(2)}) collective-permute-start(f32[32,1024]{1,0:T(8,128)S(1)} %add_multiply_fusion.1.refs_0_), channel_id=1, source_target_pairs={{0,1},{1,0},{2,3},{3,2},{4,5},{5,4},{6,7},{7,6},{8,9},{9,8},{10,11... | collective-permute-start | bytes 393224 | tf_op jit(solution)/shard_map/ppermute | solution.py:18
  26.8 1.4 %collective-permute-start.5 = (f32[32,1024]{1,0:T(8,128)S(1)}, f32[32,1024]{1,0:T(8,128)S(1)}, u32[]{:S(2)}, u32[]{:S(2)}) collective-permute-start(f32[32,1024]{1,0:T(8,128)S(1)} %add_multiply_fusion.1.refs_0_), channel_id=1, source_target_pairs={{0,3},{1,2},{2,1},{3,0},{4,7},{5,6},{6,5},{7,4},{8,11},{9,10},{10,... | collective-permute-start | bytes 393224 | tf_op jit(solution)/shard_map/ppermute | solution.py:18
  28.2 1.9 %collective-permute-done.3.refs_1_ = f32[32,1024]{1,0:T(8,128)S(1)} collective-permute-done((f32[32,1024]{1,0:T(8,128)S(1)}, f32[32,1024]{1,0:T(8,128)S(1)}, u32[]{:S(2)}, u32[]{:S(2)}) %collective-permute-start.3) | collective-permute-done | bytes 131104 | tf_op jit(solution)/shard_map/ppermute | solution.py:18
  30.1 7.3 %collective-permute-done.4.refs_2_ = f32[32,1024]{1,0:T(8,128)S(1)} collective-permute-done((f32[32,1024]{1,0:T(8,128)S(1)}, f32[32,1024]{1,0:T(8,128)S(1)}, u32[]{:S(2)}, u32[]{:S(2)}) %collective-permute-start.4) | collective-permute-done | bytes 131104 | tf_op jit(solution)/shard_map/ppermute | solution.py:18
  37.5 1.5 %shard_map.69 = (f32[128,384]{1,0:T(8,128)S(1)}, f32[128,384]{1,0:T(8,128)}) custom-call(f32[32,1024]{1,0:T(8,128)S(1)} %add_multiply_fusion.1.refs_0_, f32[32,1024]{1,0:T(8,128)S(1)} %collective-permute-done.3.refs_1_, f32[32,1024]{1,0:T(8,128)S(1)} %collective-permute-done.4.refs_2_, f32[32,1024]{1,0:T(8,128)S(1)} %collective-permute-done.5.refs_3_, ...), custom_call_target="tpu_custom_call" | custom-call | flops 603979776 | bytes 6815744 | tf_op jit(solution)/shard_map/pallas_call | solution.py:43
  38.9 1.5 %collective-permute-start.8 = (f32[136,384]{1,0:T(8,128)S(1)}, f32[136,384]{1,0:T(8,128)}, u32[]{:S(2)}, u32[]{:S(2)}) collective-permute-start(f32[136,384]{1,0:T(8,128)S(1)} %get-tuple-element.31), channel_id=1, source_target_pairs={{0,16},{16,0},{1,17},{17,1},{2,18},{18,2},{3,19},{19,3},{4,20},{20... | collective-permute-start | bytes 626696 | tf_op jit(solution)/shard_map/ppermute | solution.py:18
  41.7 1.6 %collective-permute-start.7 = (f32[128,384]{1,0:T(8,128)S(1)}, f32[128,384]{1,0:T(8,128)S(1)}, u32[]{:S(2)}, u32[]{:S(2)}) collective-permute-start(f32[128,384]{1,0:T(8,128)S(1)} %add.45), channel_id=1, source_target_pairs={{0,8},{4,12},{8,0},{12,4},{1,9},{5,13},{9,1},{13,5},{2,10},{6,14},... | collective-permute-start | bytes 589832 | tf_op jit(solution)/shard_map/ppermute | solution.py:18
  43.9 2.7 %collective-permute-done.8 = f32[136,384]{1,0:T(8,128)} collective-permute-done((f32[136,384]{1,0:T(8,128)S(1)}, f32[136,384]{1,0:T(8,128)}, u32[]{:S(2)}, u32[]{:S(2)}) %collective-permute-start.8) | collective-permute-done | bytes 208928 | tf_op jit(solution)/shard_map/ppermute | solution.py:18
  52.0 2.0 %collective-permute-start.10 = (f32[32,1024]{1,0:T(8,128)S(1)}, f32[32,1024]{1,0:T(8,128)S(1)}, u32[]{:S(2)}, u32[]{:S(2)}) collective-permute-start(f32[32,1024]{1,0:T(8,128)S(1)} %get-tuple-element.35), channel_id=1, source_target_pairs={{0,1},{1,0},{2,3},{3,2},{4,5},{5,4},{6,7},{7,6},{8,9},{9,8},{10,11... | collective-permute-start | bytes 393224 | tf_op jit(solution)/shard_map/ppermute | solution.py:18
  56.5 3.2 %collective-permute-done.10 = f32[32,1024]{1,0:T(8,128)S(1)} collective-permute-done((f32[32,1024]{1,0:T(8,128)S(1)}, f32[32,1024]{1,0:T(8,128)S(1)}, u32[]{:S(2)}, u32[]{:S(2)}) %collective-permute-start.10) | collective-permute-done | bytes 131104 | tf_op jit(solution)/shard_map/ppermute | solution.py:18
  59.7 7.2 %collective-permute-done.11 = f32[32,1024]{1,0:T(8,128)S(1)} collective-permute-done((f32[32,1024]{1,0:T(8,128)S(1)}, f32[32,1024]{1,0:T(8,128)S(1)}, u32[]{:S(2)}, u32[]{:S(2)}) %collective-permute-start.11) | collective-permute-done | bytes 131104 | tf_op jit(solution)/shard_map/ppermute | solution.py:18
  66.9 2.4 %collective-permute-start.13 = (f32[32,1024]{1,0:T(8,128)S(1)}, f32[32,1024]{1,0:T(8,128)S(1)}, u32[]{:S(2)}, u32[]{:S(2)}) collective-permute-start(f32[32,1024]{1,0:T(8,128)S(1)} %add_multiply_fusion.refs_0_), channel_id=1, source_target_pairs={{0,1},{1,0},{2,3},{3,2},{4,5},{5,4},{6,7},{7,6},{8,9},{9,8},{10,11... | collective-permute-start | bytes 393224 | tf_op jit(solution)/shard_map/ppermute | solution.py:18
  70.3 1.4 %collective-permute-start.15 = (f32[32,1024]{1,0:T(8,128)S(1)}, f32[32,1024]{1,0:T(8,128)S(1)}, u32[]{:S(2)}, u32[]{:S(2)}) collective-permute-start(f32[32,1024]{1,0:T(8,128)S(1)} %add_multiply_fusion.refs_0_), channel_id=1, source_target_pairs={{0,3},{1,2},{2,1},{3,0},{4,7},{5,6},{6,5},{7,4},{8,11},{9,10},{10,... | collective-permute-start | bytes 393224 | tf_op jit(solution)/shard_map/ppermute | solution.py:18
  71.7 1.9 %collective-permute-done.13.refs_1_ = f32[32,1024]{1,0:T(8,128)S(1)} collective-permute-done((f32[32,1024]{1,0:T(8,128)S(1)}, f32[32,1024]{1,0:T(8,128)S(1)}, u32[]{:S(2)}, u32[]{:S(2)}) %collective-permute-start.13) | collective-permute-done | bytes 131104 | tf_op jit(solution)/shard_map/ppermute | solution.py:18
  73.7 7.8 %collective-permute-done.14.refs_2_ = f32[32,1024]{1,0:T(8,128)S(1)} collective-permute-done((f32[32,1024]{1,0:T(8,128)S(1)}, f32[32,1024]{1,0:T(8,128)S(1)}, u32[]{:S(2)}, u32[]{:S(2)}) %collective-permute-start.14) | collective-permute-done | bytes 131104 | tf_op jit(solution)/shard_map/ppermute | solution.py:18
  82.3 1.6 %collective-permute-start.18 = (f32[128,384]{1,0:T(8,128)S(1)}, f32[128,384]{1,0:T(8,128)S(1)}, u32[]{:S(2)}, u32[]{:S(2)}) collective-permute-start(f32[128,384]{1,0:T(8,128)S(1)} %get-tuple-element.40), channel_id=1, source_target_pairs={{0,16},{16,0},{1,17},{17,1},{2,18},{18,2},{3,19},{19,3},{4,20},{20... | collective-permute-start | bytes 589832 | tf_op jit(solution)/shard_map/ppermute | solution.py:18
  83.9 1.5 %collective-permute-start.17 = (f32[128,384]{1,0:T(8,128)S(1)}, f32[128,384]{1,0:T(8,128)S(1)}, u32[]{:S(2)}, u32[]{:S(2)}) collective-permute-start(f32[128,384]{1,0:T(8,128)S(1)} %add.52), channel_id=1, source_target_pairs={{0,8},{4,12},{8,0},{12,4},{1,9},{5,13},{9,1},{13,5},{2,10},{6,14},... | collective-permute-start | bytes 589832 | tf_op jit(solution)/shard_map/ppermute | solution.py:18
  85.5 4.1 %collective-permute-done.18 = f32[128,384]{1,0:T(8,128)S(1)} collective-permute-done((f32[128,384]{1,0:T(8,128)S(1)}, f32[128,384]{1,0:T(8,128)S(1)}, u32[]{:S(2)}, u32[]{:S(2)}) %collective-permute-start.18) | collective-permute-done | bytes 196640 | tf_op jit(solution)/shard_map/ppermute | solution.py:18
  (45 shorter events, 19.6 us)
Async XLA Ops:
  0.6 1.9 %copy-start = (f32[1,1024,768]{2,1,0:T(8,128)S(1)}, f32[1,1024,768]{2,1,0:T(8,128)}, u32[]{:S(2)}) copy-start(f32[1,1024,768]{2,1,0:T(8,128)} %param.6) | copy-start | bytes 9437188
  2.5 1.0 %copy-start.1 = (f32[1,768,128]{2,1,0:T(8,128)S(1)}, f32[1,768,128]{2,1,0:T(8,128)}, u32[]{:S(2)}) copy-start(f32[1,768,128]{2,1,0:T(8,128)} %param.5) | copy-start | bytes 1179652
  7.6 31.3 %copy-start.2 = (f32[1,768]{1,0:T(1,128)}, f32[1,768]{1,0:T(1,128)S(1)}, u32[]{:S(2)}) copy-start(f32[1,768]{1,0:T(1,128)S(1)} %get-tuple-element.21.mask) | copy-start | bytes 9220
  7.6 8.2 %collective-permute-start = (f32[32,1024]{1,0:T(8,128)S(1)}, f32[32,1024]{1,0:T(8,128)S(1)}, u32[]{:S(2)}, u32[]{:S(2)}) collective-permute-start(f32[32,1024]{1,0:T(8,128)S(1)} %get-tuple-element.23), channel_id=1, source_target_pairs={{0,1},{1,0},{2,3},{3,2},{4,5},{5,4},{6,7},{7,6},{8,9},{9,8},{10,11... | collective-permute-start | bytes 393224 | tf_op jit(solution)/shard_map/ppermute | solution.py:18
  10.7 12.9 %collective-permute-start.1 = (f32[32,1024]{1,0:T(8,128)S(1)}, f32[32,1024]{1,0:T(8,128)S(1)}, u32[]{:S(2)}, u32[]{:S(2)}) collective-permute-start(f32[32,1024]{1,0:T(8,128)S(1)} %get-tuple-element.24), channel_id=1, source_target_pairs={{0,2},{1,3},{2,0},{3,1},{4,6},{5,7},{6,4},{7,5},{8,10},{9,11},{10,... | collective-permute-start | bytes 393224 | tf_op jit(solution)/shard_map/ppermute | solution.py:18
  13.3 10.4 %collective-permute-start.2 = (f32[32,1024]{1,0:T(8,128)S(1)}, f32[32,1024]{1,0:T(8,128)S(1)}, u32[]{:S(2)}, u32[]{:S(2)}) collective-permute-start(f32[32,1024]{1,0:T(8,128)S(1)} %get-tuple-element.25), channel_id=1, source_target_pairs={{0,3},{1,2},{2,1},{3,0},{4,7},{5,6},{6,5},{7,4},{8,11},{9,10},{10,... | collective-permute-start | bytes 393224 | tf_op jit(solution)/shard_map/ppermute | solution.py:18
  23.7 6.4 %collective-permute-start.3 = (f32[32,1024]{1,0:T(8,128)S(1)}, f32[32,1024]{1,0:T(8,128)S(1)}, u32[]{:S(2)}, u32[]{:S(2)}) collective-permute-start(f32[32,1024]{1,0:T(8,128)S(1)} %add_multiply_fusion.1.refs_0_), channel_id=1, source_target_pairs={{0,1},{1,0},{2,3},{3,2},{4,5},{5,4},{6,7},{7,6},{8,9},{9,8},{10,11... | collective-permute-start | bytes 393224 | tf_op jit(solution)/shard_map/ppermute | solution.py:18
  25.7 11.8 %collective-permute-start.4 = (f32[32,1024]{1,0:T(8,128)S(1)}, f32[32,1024]{1,0:T(8,128)S(1)}, u32[]{:S(2)}, u32[]{:S(2)}) collective-permute-start(f32[32,1024]{1,0:T(8,128)S(1)} %add_multiply_fusion.1.refs_0_), channel_id=1, source_target_pairs={{0,2},{1,3},{2,0},{3,1},{4,6},{5,7},{6,4},{7,5},{8,10},{9,11},{10,... | collective-permute-start | bytes 393224 | tf_op jit(solution)/shard_map/ppermute | solution.py:18
  26.8 10.7 %collective-permute-start.5 = (f32[32,1024]{1,0:T(8,128)S(1)}, f32[32,1024]{1,0:T(8,128)S(1)}, u32[]{:S(2)}, u32[]{:S(2)}) collective-permute-start(f32[32,1024]{1,0:T(8,128)S(1)} %add_multiply_fusion.1.refs_0_), channel_id=1, source_target_pairs={{0,3},{1,2},{2,1},{3,0},{4,7},{5,6},{6,5},{7,4},{8,11},{9,10},{10,... | collective-permute-start | bytes 393224 | tf_op jit(solution)/shard_map/ppermute | solution.py:18
  38.9 1.8 %collective-permute-start.6 = (f32[128,384]{1,0:T(8,128)}, f32[128,384]{1,0:T(8,128)}, u32[]{:S(2)}, u32[]{:S(2)}) collective-permute-start(f32[128,384]{1,0:T(8,128)} %get-tuple-element.30), channel_id=1, source_target_pairs={{0,4},{4,0},{8,12},{12,8},{1,5},{5,1},{9,13},{13,9},{2,6},{6,2},{1... | collective-permute-start | bytes 589832 | tf_op jit(solution)/shard_map/ppermute | solution.py:18
  38.9 7.7 %collective-permute-start.8 = (f32[136,384]{1,0:T(8,128)S(1)}, f32[136,384]{1,0:T(8,128)}, u32[]{:S(2)}, u32[]{:S(2)}) collective-permute-start(f32[136,384]{1,0:T(8,128)S(1)} %get-tuple-element.31), channel_id=1, source_target_pairs={{0,16},{16,0},{1,17},{17,1},{2,18},{18,2},{3,19},{19,3},{4,20},{20... | collective-permute-start | bytes 626696 | tf_op jit(solution)/shard_map/ppermute | solution.py:18
  41.7 7.0 %collective-permute-start.7 = (f32[128,384]{1,0:T(8,128)S(1)}, f32[128,384]{1,0:T(8,128)S(1)}, u32[]{:S(2)}, u32[]{:S(2)}) collective-permute-start(f32[128,384]{1,0:T(8,128)S(1)} %add.45), channel_id=1, source_target_pairs={{0,8},{4,12},{8,0},{12,4},{1,9},{5,13},{9,1},{13,5},{2,10},{6,14},... | collective-permute-start | bytes 589832 | tf_op jit(solution)/shard_map/ppermute | solution.py:18
  49.7 1.5 %copy-start.3 = (f32[1,768]{1,0:T(1,128)S(1)}, f32[1,768]{1,0:T(1,128)}, u32[]{:S(2)}) copy-start(f32[1,768]{1,0:T(1,128)} %copy-done.2) | copy-start | bytes 9220
  49.7 1.5 %collective-permute-start.9 = (f32[128,384]{1,0:T(8,128)S(1)}, f32[128,384]{1,0:T(8,128)S(1)}, u32[]{:S(2)}, u32[]{:S(2)}) collective-permute-start(f32[128,384]{1,0:T(8,128)S(1)} %get-tuple-element.41.refs_0_.own), channel_id=1, source_target_pairs={{0,4},{4,0},{8,12},{12,8},{1,5},{5,1},{9,13},{13,9},{2,6},{6,2},{1... | collective-permute-start | bytes 589832 | tf_op jit(solution)/shard_map/ppermute | solution.py:18
  52.0 7.7 %collective-permute-start.10 = (f32[32,1024]{1,0:T(8,128)S(1)}, f32[32,1024]{1,0:T(8,128)S(1)}, u32[]{:S(2)}, u32[]{:S(2)}) collective-permute-start(f32[32,1024]{1,0:T(8,128)S(1)} %get-tuple-element.35), channel_id=1, source_target_pairs={{0,1},{1,0},{2,3},{3,2},{4,5},{5,4},{6,7},{7,6},{8,9},{9,8},{10,11... | collective-permute-start | bytes 393224 | tf_op jit(solution)/shard_map/ppermute | solution.py:18
  54.0 12.9 %collective-permute-start.11 = (f32[32,1024]{1,0:T(8,128)S(1)}, f32[32,1024]{1,0:T(8,128)S(1)}, u32[]{:S(2)}, u32[]{:S(2)}) collective-permute-start(f32[32,1024]{1,0:T(8,128)S(1)} %get-tuple-element.36), channel_id=1, source_target_pairs={{0,2},{1,3},{2,0},{3,1},{4,6},{5,7},{6,4},{7,5},{8,10},{9,11},{10,... | collective-permute-start | bytes 393224 | tf_op jit(solution)/shard_map/ppermute | solution.py:18
  55.1 11.8 %collective-permute-start.12 = (f32[32,1024]{1,0:T(8,128)S(1)}, f32[32,1024]{1,0:T(8,128)S(1)}, u32[]{:S(2)}, u32[]{:S(2)}) collective-permute-start(f32[32,1024]{1,0:T(8,128)S(1)} %get-tuple-element.37), channel_id=1, source_target_pairs={{0,3},{1,2},{2,1},{3,0},{4,7},{5,6},{6,5},{7,4},{8,11},{9,10},{10,... | collective-permute-start | bytes 393224 | tf_op jit(solution)/shard_map/ppermute | solution.py:18
  66.9 6.7 %collective-permute-start.13 = (f32[32,1024]{1,0:T(8,128)S(1)}, f32[32,1024]{1,0:T(8,128)S(1)}, u32[]{:S(2)}, u32[]{:S(2)}) collective-permute-start(f32[32,1024]{1,0:T(8,128)S(1)} %add_multiply_fusion.refs_0_), channel_id=1, source_target_pairs={{0,1},{1,0},{2,3},{3,2},{4,5},{5,4},{6,7},{7,6},{8,9},{9,8},{10,11... | collective-permute-start | bytes 393224 | tf_op jit(solution)/shard_map/ppermute | solution.py:18
  69.3 12.1 %collective-permute-start.14 = (f32[32,1024]{1,0:T(8,128)S(1)}, f32[32,1024]{1,0:T(8,128)S(1)}, u32[]{:S(2)}, u32[]{:S(2)}) collective-permute-start(f32[32,1024]{1,0:T(8,128)S(1)} %add_multiply_fusion.refs_0_), channel_id=1, source_target_pairs={{0,2},{1,3},{2,0},{3,1},{4,6},{5,7},{6,4},{7,5},{8,10},{9,11},{10,... | collective-permute-start | bytes 393224 | tf_op jit(solution)/shard_map/ppermute | solution.py:18
  70.3 11.1 %collective-permute-start.15 = (f32[32,1024]{1,0:T(8,128)S(1)}, f32[32,1024]{1,0:T(8,128)S(1)}, u32[]{:S(2)}, u32[]{:S(2)}) collective-permute-start(f32[32,1024]{1,0:T(8,128)S(1)} %add_multiply_fusion.refs_0_), channel_id=1, source_target_pairs={{0,3},{1,2},{2,1},{3,0},{4,7},{5,6},{6,5},{7,4},{8,11},{9,10},{10,... | collective-permute-start | bytes 393224 | tf_op jit(solution)/shard_map/ppermute | solution.py:18
  82.2 1.7 %collective-permute-start.16 = (f32[128,384]{1,0:T(8,128)S(1)}, f32[128,384]{1,0:T(8,128)S(1)}, u32[]{:S(2)}, u32[]{:S(2)}) collective-permute-start(f32[128,384]{1,0:T(8,128)S(1)} %get-tuple-element.39), channel_id=1, source_target_pairs={{0,4},{4,0},{8,12},{12,8},{1,5},{5,1},{9,13},{13,9},{2,6},{6,2},{1... | collective-permute-start | bytes 589832 | tf_op jit(solution)/shard_map/ppermute | solution.py:18
  82.3 7.3 %collective-permute-start.18 = (f32[128,384]{1,0:T(8,128)S(1)}, f32[128,384]{1,0:T(8,128)S(1)}, u32[]{:S(2)}, u32[]{:S(2)}) collective-permute-start(f32[128,384]{1,0:T(8,128)S(1)} %get-tuple-element.40), channel_id=1, source_target_pairs={{0,16},{16,0},{1,17},{17,1},{2,18},{18,2},{3,19},{19,3},{4,20},{20... | collective-permute-start | bytes 589832 | tf_op jit(solution)/shard_map/ppermute | solution.py:18
  83.9 7.0 %collective-permute-start.17 = (f32[128,384]{1,0:T(8,128)S(1)}, f32[128,384]{1,0:T(8,128)S(1)}, u32[]{:S(2)}, u32[]{:S(2)}) collective-permute-start(f32[128,384]{1,0:T(8,128)S(1)} %add.52), channel_id=1, source_target_pairs={{0,8},{4,12},{8,0},{12,4},{1,9},{5,13},{9,1},{13,5},{2,10},{6,14},... | collective-permute-start | bytes 589832 | tf_op jit(solution)/shard_map/ppermute | solution.py:18
  91.0 1.5 %collective-permute-start.19 = (f32[128,384]{1,0:T(8,128)S(1)}, f32[128,384]{1,0:T(8,128)S(1)}, u32[]{:S(2)}, u32[]{:S(2)}) collective-permute-start(f32[128,384]{1,0:T(8,128)S(1)} %fusion.3.refs_0_), channel_id=1, source_target_pairs={{0,4},{4,0},{8,12},{12,8},{1,5},{5,1},{9,13},{13,9},{2,6},{6,2},{1... | collective-permute-start | bytes 589832 | tf_op jit(solution)/shard_map/ppermute | solution.py:18
  (3 other events, 2.1 us)

commit v3 on v2

v3 whole, which is shorter than its diff:
```python
import functools

import jax
import jax.numpy as jnp
from jax import lax
from jax.experimental import pallas as pl
from jax.experimental.pallas import tpu as pltpu
from jax.sharding import PartitionSpec as P

MAX_CHUNKS = 2
LIMIT = 16 * 2**20
LARGE = 55 * 2**20
NT = (((1,), (1,)), ((), ()))
NN = (((1,), (0,)), ((), ()))
VMEM = pl.BlockSpec(memory_space=pltpu.VMEM)


def swap(value, axis, stride):
    return lax.ppermute(value, axis, [(i, i ^ stride) for i in range(lax.axis_size(axis))])


def shifted(value, axis, by):
    length = lax.axis_size(axis)
    pairs = [(i, i + by) for i in range(length) if 0 <= i + by < length]
    return lax.ppermute(value, axis, pairs)


def split(value):
    high = value.astype(jnp.bfloat16)
    return high, (value - high.astype(jnp.float32)).astype(jnp.bfloat16)


def product(value, high, low, dims):
    top, rest = split(value)
    rows = value.shape[0]
    dot = functools.partial(
        lax.dot_general, dimension_numbers=dims, preferred_element_type=jnp.float32
    )
    both = dot(jnp.concatenate([top, rest], axis=0), high)
    return both[:rows] + (both[rows:] + dot(top, low))


def call(kernel, shapes, operands, flops=0, scratch=()):
    return pl.pallas_call(
        kernel,
        out_shape=shapes,
        in_specs=[VMEM] * len(operands),
        out_specs=[VMEM] * len(shapes),
        scratch_shapes=scratch,
        compiler_params=pltpu.CompilerParams(vmem_limit_bytes=LIMIT),
        cost_estimate=pl.CostEstimate(
            flops=flops, bytes_accessed=sum(4 * o.size for o in operands), transcendentals=0
        ),
    )(*operands)


def own_first(ref, rows, side, half):
    own = pl.ds(pl.multiple_of(side * half, half), half)
    other = pl.ds(pl.multiple_of((1 - side) * half, half), half)
    return jnp.concatenate([ref[rows, own], ref[rows, other]], axis=1)


def block_order(parts):
    bits = parts.bit_length() - 1
    return [int(format(i, "b").zfill(bits)[::-1], 2) for i in range(parts)]


def first_kernel(chunks, parts, step, *refs):
    probes_hbm, tile_hbm, active_hbm = refs[:3]
    high, low = refs[3:5]
    blocks = refs[5:-5]
    probes, tile, active, turned, arrived = refs[-5:]
    side = lax.axis_index("dp") % 2
    here = lax.axis_index("cell")
    cells, count = probes.shape
    data = tile.shape[0]
    half = cells // 2
    size = count // (chunks * parts)

    pairs = [(active_hbm, active), (probes_hbm, probes)]
    pairs += [
        (tile_hbm.at[pl.ds(at, step)], tile.at[pl.ds(at, step)]) for at in range(0, data, step)
    ]
    copies = [
        pltpu.make_async_copy(source, target, arrived.at[index])
        for index, (source, target) in enumerate(pairs)
    ]
    for copy in copies:
        copy.start()
    copies[0].wait()
    keep = jnp.broadcast_to(active[...].astype(jnp.float32), (8, cells)).T[:, :1]
    copies[1].wait()
    top, rest = split(probes[...] * keep)
    both = jnp.concatenate([top, rest], axis=1)

    left = pl.ds(pl.multiple_of(side * half, half), half)
    right = pl.ds(pl.multiple_of((1 - side) * half, half), half)
    dot = functools.partial(jnp.dot, preferred_element_type=jnp.float32)
    for index, at in enumerate(range(0, data, step)):
        copies[2 + index].wait()
        rows = slice(at, at + step)
        tile_top, tile_rest = split(tile[rows, :])
        for ref, value in ((high, tile_top), (low, tile_rest)):
            ref[rows, left] = value[:, :half]
            ref[rows, right] = value[:, half:]
        out = dot(tile_top, both)
        out = out[:, :count] + (out[:, count:] + dot(tile_rest, top))
        turned[:, rows] = out.T

    for chunk in range(chunks):
        for index, x in enumerate(block_order(parts)):
            start = pl.multiple_of((chunk * parts + (here ^ x)) * size, size)
            block = blocks[2 * chunk + index // (parts // 2)]
            spot = index % (parts // 2) * size
            block[spot : spot + size, :] = turned[pl.ds(start, size), :]


def first_forward(probes, tile, active, chunks):
    parts = lax.axis_size("cell")
    cells, count = probes.shape
    data = tile.shape[0]
    step = 256 if data % 256 == 0 else data
    operands = [probes, tile, active]
    shapes = [pltpu.VMEM((data, cells), jnp.bfloat16)] * 2
    shapes += [jax.ShapeDtypeStruct((count // (2 * chunks), data), jnp.float32)] * (2 * chunks)
    outs = pl.pallas_call(
        functools.partial(first_kernel, chunks, parts, step),
        in_specs=[pl.BlockSpec(memory_space=pltpu.HBM)] * len(operands),
        out_specs=[VMEM] * len(shapes),
        out_shape=shapes,
        scratch_shapes=[pltpu.VMEM(o.shape, o.dtype) for o in operands]
        + [pltpu.VMEM((count, data), jnp.float32), pltpu.SemaphoreType.DMA((data // step + 2,))],
        compiler_params=pltpu.CompilerParams(vmem_limit_bytes=LARGE),
        cost_estimate=pl.CostEstimate(
            flops=6 * data * cells * count, bytes_accessed=4 * data * cells, transcendentals=0
        ),
    )(*operands)
    return outs[:2], [outs[2 + 2 * i : 4 + 2 * i] for i in range(chunks)]


def prepare(probes, classes, active, coupling, chunks):
    parts = lax.axis_size("cell")
    cells, count = probes.shape
    half = cells // 2
    size = count // (chunks * parts)
    every = slice(None)

    def kernel(probes, classes, active, coupling, *refs):
        mask, weight, message, turned = refs
        side = lax.axis_index("dp") % 2
        here = lax.axis_index("cell")
        keep = own_first(active, every, side, half).astype(jnp.float32)
        mask[...] = keep
        turned[...] = probes[...].T
        own = pl.ds(pl.multiple_of(side * half, half), half)
        for chunk in range(chunks):
            for index, x in enumerate(block_order(parts)):
                spot = (chunk * parts + index) * size
                start = pl.multiple_of((chunk * parts + (here ^ x)) * size, size)
                message[spot : spot + size, :] = turned[pl.ds(start, size), own] * keep[:, :half]
        message[count:, :] = jnp.broadcast_to(coupling[:, own], (8, half))
        labels = classes[...]
        weight[...] = jnp.where(
            labels == 0, 1.0, jnp.where(labels == 1, 0.5, jnp.where(labels == 2, 0.25, 0.125))
        ).astype(jnp.float32)

    shapes = [
        jax.ShapeDtypeStruct((1, cells), jnp.float32),
        jax.ShapeDtypeStruct(classes.shape, jnp.float32),
        jax.ShapeDtypeStruct((count + 8, half), jnp.float32),
    ]
    operands = [probes, classes, active, coupling]
    scratch = [pltpu.VMEM((count, cells), jnp.float32)]
    return call(kernel, shapes, operands, scratch=scratch)


def turn(high, low):
    def kernel(high, low, high_t, low_t):
        high_t[...] = high[...].T
        low_t[...] = low[...].T

    shape = jax.ShapeDtypeStruct(high.shape[::-1], jnp.bfloat16)
    return call(kernel, [shape, shape], [high, low])


def backward(blocks, high, low):
    def kernel(*refs):
        high, low, own, other = refs[-4:]
        value = jnp.concatenate([ref[...] for ref in refs[:-4]], axis=0)
        back = product(value, high[...], low[...], NN)
        half = own.shape[1]
        own[...] = back[:, :half]
        other[...] = back[:, half:]

    rows = sum(block.shape[0] for block in blocks)
    shape = jax.ShapeDtypeStruct((rows, high.shape[1] // 2), jnp.float32)
    return call(kernel, [shape, shape], [*blocks, high, low], 6 * rows * high.size)


def forward(own, other, mask, high_t, low_t):
    def kernel(own, other, mask, high_t, low_t, keep, send):
        masked = jnp.concatenate([own[...], other[...]], axis=1) * mask[...]
        out = product(masked, high_t[...], low_t[...], NN)
        size = out.shape[0] // 2
        keep[...] = out[:size]
        send[...] = out[size:]

    rows = own.shape[0]
    shape = jax.ShapeDtypeStruct((rows // 2, high_t.shape[1]), jnp.float32)
    operands = [own, other, mask, high_t, low_t]
    return call(kernel, [shape, shape], operands, 6 * rows * high_t.size)


def finish(halves):
    chunks = len(halves) // 2
    parts = lax.axis_size("cell")
    rows, half = halves[0].shape
    size = rows // parts

    def kernel(*refs):
        out, turned = refs[-2:]
        side = lax.axis_index("dp") % 2
        here = lax.axis_index("cell")
        own = pl.ds(pl.multiple_of(side * half, half), half)
        other = pl.ds(pl.multiple_of((1 - side) * half, half), half)
        for chunk in range(chunks):
            for index, x in enumerate(block_order(parts)):
                start = pl.multiple_of((chunk * parts + (here ^ x)) * size, size)
                block = slice(index * size, (index + 1) * size)
                turned[pl.ds(start, size), own] = refs[2 * chunk][block, :]
                turned[pl.ds(start, size), other] = refs[2 * chunk + 1][block, :]
        out[...] = turned[...].T

    shape = jax.ShapeDtypeStruct((2 * half, chunks * rows), jnp.float32)
    return pl.pallas_call(
        kernel,
        out_shape=shape,
        in_specs=[VMEM] * (2 * chunks),
        out_specs=VMEM,
        scratch_shapes=[pltpu.VMEM(shape.shape[::-1], jnp.float32)],
        compiler_params=pltpu.CompilerParams(vmem_limit_bytes=LIMIT),
    )(*halves)


def sum_cells(keep, send, shared):
    parts = lax.axis_size("cell")
    value = yield (lambda a, b: a + b), keep, swap(send, "cell", 1)
    half = value.shape[0] // 2
    stride = 2
    while stride < parts // 2:
        value = value[:half] + swap(value[half:], "cell", stride)
        half //= 2
        stride *= 2
    other = swap(jnp.concatenate([value[half:], value[:half]], axis=0), "cell", stride)
    value = yield (lambda a, b: (a + b) * shared["weight"]), value, other
    while stride > 2:
        stride //= 2
        value = jnp.concatenate([value, swap(value, "cell", stride)], axis=0)
    return value, swap(value, "cell", 1)


def sum_data(own, other):
    total = yield (lambda a, b: a + b), own, swap(other, "dp", 1)
    stride = 2
    while stride < lax.axis_size("dp") // 2:
        total = total + swap(total, "dp", stride)
        stride *= 2
    return total, swap(total, "dp", stride)


def in_turn(chains):
    results = [None] * len(chains)
    answers = [None] * len(chains)
    token = None
    waiting = list(range(len(chains)))
    while waiting:
        for index in list(waiting):
            try:
                step = chains[index].send(answers[index])
            except StopIteration as stop:
                results[index] = stop.value
                waiting.remove(index)
                continue
            if step is None:
                answers[index] = None
                continue
            function, *values = step
            if token is not None:
                *values, _ = lax.optimization_barrier((*values, token))
            answers[index] = function(*values)
            token = jax.tree.leaves(answers[index])[0]
    return results


def neighbours(message):
    if lax.axis_size("section") == 2:
        got = swap(message, "section", 1)
        return got, got
    return shifted(message, "section", 1), shifted(message, "section", -1)


def local(probes, jacobian, classes, active, coupling):
    probes, tile = probes[0], jacobian[0]
    count, half = probes.shape[1], probes.shape[0] // 2
    parts = lax.axis_size("cell")
    chunks = MAX_CHUNKS
    while chunks > 1 and count % (8 * chunks * parts):
        chunks -= 1
    rows = count // chunks
    sections = lax.axis_size("section")
    section = lax.axis_index("section")

    (high, low), blocks = first_forward(probes, tile, active, chunks)
    shared = {}

    def ready(*operands):
        mask, weight, message = prepare(*operands, chunks)
        below, above = neighbours(message)
        strength = jnp.where(section == 0, 0.0, message[count : count + 1])
        strength_next = jnp.where(section == sections - 1, 0.0, above[count : count + 1])
        shared.update(mask=mask, mask_own=mask[:, :half], weight=weight)
        shared.update(first=(message, below, above), strength=(strength, strength_next))
        return mask

    def turned(high, low):
        shared["turned"] = turn(high, low)
        return shared["turned"]

    def part(value, chunk):
        return value[chunk * rows : (chunk + 1) * rows]

    def smoothing(here, under, over):
        strength, strength_next = shared["strength"]
        return strength * (here - under) + strength_next * (here - over)

    def hessian(keep, send, smooth):
        sent = yield from sum_cells(keep, send, shared)
        own, other = yield (lambda *values: backward(values, high, low)), *sent
        total, other = yield from sum_data(own, other)
        own = yield (lambda a, b: shared["mask_own"] * (a + b + smooth())), total, other
        return own, swap(own, "dp", 1)

    def chain(chunk):
        def smooth_first():
            return smoothing(*[part(value, chunk) for value in shared["first"]])

        image = yield from hessian(*blocks[chunk], smooth_first)
        shared[chunk] = image

        def smooth_second():
            if "masked" not in shared:
                masked = jnp.concatenate([shared[i][0] for i in range(chunks)], axis=0)
                masked = masked * shared["mask_own"]
                shared["masked"] = (masked, *neighbours(masked))
            return smoothing(*[part(value, chunk) for value in shared["masked"]])

        sent = yield (lambda a, b: forward(a, b, shared["mask"], *shared["turned"])), *image
        return (yield from hessian(*sent, smooth_second))

    def aside():
        yield ready, probes, classes, active, coupling
        yield None
        yield None
        yield None
        yield turned, high, low
        yield None
        halves = [value for chunk in range(chunks) for value in shared[chunk]]
        return (yield (lambda *values: finish(values)), *halves)

    start, first, *rest = in_turn([chain(0), aside()] + [chain(chunk) for chunk in range(1, chunks)])
    second = finish([half for halves in (start, *rest) for half in halves])
    return first[None], second[None]


def solution(mesh):
    return jax.shard_map(
        local,
        mesh=mesh,
        in_specs=(
            P("section", "cell", None),
            P("section", "dp", "cell"),
            P("section", "dp"),
            P("section", "cell"),
            P("section", "cell"),
        ),
        out_specs=(P("section", "cell", None), P("section", "cell", None)),
        check_vma=False,
    )
```

time: 93.9 us -> 78.7 us (0.84)
  waiting for transfers between devices: 50.5 us -> 41.8 us
  local copies, waits for them, and re-layouts: 5.64 us -> 0.08 us
  starting transfers between devices: 25.9 us -> 22.8 us
  Pallas kernels: 7.87 us -> 10.5 us
    ppermute x20 -> x26, waiting for transfers between devices: 50.5 us -> 41.8 us  [swap(): lax.ppermute(value, axis, [(i, i ^ stride) for i in range(lax.axis_size(a...]
    unnamed x14 -> x8, local copies, waits for them, and re-layouts: 4.94 us -> 0.02 us
    ppermute x20 -> x26, starting transfers between devices: 25.9 us -> 22.8 us  [swap(): lax.ppermute(value, axis, [(i, i ^ stride) for i in range(lax.axis_size(a...]
    pallas_call x1, Pallas kernels: 2.02 us -> 3.92 us  [first_forward(): pl.pallas_call(functools.partial(first_kernel, chunks, parts, step), in_s...]
    mul x5 -> x10, other arithmetic: 1.85 us -> 0.25 us  [the longest x4 0.13 us: hessian(): shared['mask_own'] * (a + b + smooth())]
    add x2 -> x8, other arithmetic: 0.97 us -> 2.06 us  [the longest x4 2 us: sum_cells(): value = (yield (lambda a, b: a + b, keep, swap(send, 'cell', 1)))]
    pallas_call x4 -> x8, Pallas kernels: 3.94 us -> 4.73 us  [call(): pl.pallas_call(kernel, out_shape=shapes, in_specs=[VMEM] * len(operands),...]
  transfers between devices with their start and end apart: 20 -> 26, of which waited for: 15 -> 17; matrix products, arithmetic and copies ran while one was open for 3% -> 3% of each run, Pallas kernels for 2% -> 6%
where the time goes in v3:
time: 78.7 us; the launch traced here: 78.5 us
  waiting for transfers between devices  41.8 us (53%)
  starting transfers between devices  22.8 us (29%)
  Pallas kernels  10.5 us (13%)
  other arithmetic  2.36 us (3%)
  between operations  1.02 us (1%)
    ppermute x26, waiting for transfers between devices, swap(): lax.ppermute(value, axis, [(i, i ^ stride) for i in range(lax.axis_size(a...  41.8 us
    ppermute x26, starting transfers between devices, swap(): lax.ppermute(value, axis, [(i, i ^ stride) for i in range(lax.axis_size(a...  22.8 us
    pallas_call x8, Pallas kernels, call(): pl.pallas_call(kernel, out_shape=shapes, in_specs=[VMEM] * len(operands),...  4.73 us
    pallas_call x1, Pallas kernels, first_forward(): pl.pallas_call(functools.partial(first_kernel, chunks, parts, step), in_s...  3.92 us
    add x4, other arithmetic, sum_cells(): value = (yield (lambda a, b: a + b, keep, swap(send, 'cell', 1)))  2 us
    pallas_call x2, Pallas kernels, finish(): pl.pallas_call(kernel, out_shape=shape, in_specs=[VMEM] * (2 * chunks), o...  1.89 us
  transfers between devices with their start and end apart: 26, of which 17 were waited for; matrix products, arithmetic and copies ran while one was open for 3% of the time, Pallas kernels for 6%

profile of v3, /device:TPU:0, one launch (start us, length us, event | category | flops | bytes accessed | tf_op | source)
XLA Modules:
  0.0 78.5 jit_solution(17888135759315048370)
XLA Ops:
  0.7 3.9 %shard_map.68 = (bf16[1024,768]{1,0:T(8,128)(2,1)S(1)}, bf16[1024,768]{1,0:T(8,128)(2,1)S(1)}, f32[32,1024]{1,0:T(8,128)}, f32[32,1024]{1,0:T(8,128)}, f32[32,1024]{1,0:T(8,128)}, /*index=5*/f32[32,1024]{1,0:T(8,128)}) custom-call(f32[768,128]{1,0:T(8,128)} %bitcast.5, f32[1024,768]{1,0:T(8,128)} %bitcast.11, s32[1,768]{1,0:T(1,128)} %active), custom_call_target="tpu_custom_call" | custom-call | flops 603979776 | bytes 3145728 | tf_op jit(solution)/shard_map/pallas_call | solution.py:126
  4.6 3.1 %collective-permute-start = (f32[32,1024]{1,0:T(8,128)}, f32[32,1024]{1,0:T(8,128)}, u32[]{:S(2)}, u32[]{:S(2)}) collective-permute-start(f32[32,1024]{1,0:T(8,128)} %get-tuple-element.78), channel_id=1, source_target_pairs={{0,1},{1,0},{2,3},{3,2},{4,5},{5,4},{6,7},{7,6},{8,9},{9,8},{10,11... | collective-permute-start | bytes 393224 | tf_op jit(solution)/shard_map/ppermute | solution.py:19
  7.8 4.6 %collective-permute-done = f32[32,1024]{1,0:T(8,128)} collective-permute-done((f32[32,1024]{1,0:T(8,128)}, f32[32,1024]{1,0:T(8,128)}, u32[]{:S(2)}, u32[]{:S(2)}) %collective-permute-start) | collective-permute-done | bytes 131104 | tf_op jit(solution)/shard_map/ppermute | solution.py:19
  13.6 2.1 %collective-permute-start.9 = (f32[136,384]{1,0:T(8,128)S(1)}, f32[136,384]{1,0:T(8,128)S(1)}, u32[]{:S(2)}, u32[]{:S(2)}) collective-permute-start(f32[136,384]{1,0:T(8,128)S(1)} %get-tuple-element.109), channel_id=1, source_target_pairs={{0,16},{16,0},{1,17},{17,1},{2,18},{18,2},{3,19},{19,3},{4,20},{20... | collective-permute-start | bytes 626696 | tf_op jit(solution)/shard_map/ppermute | solution.py:19
  15.6 2.7 %collective-permute-start.1 = (f32[32,1024]{1,0:T(8,128)S(1)}, f32[32,1024]{1,0:T(8,128)S(1)}, u32[]{:S(2)}, u32[]{:S(2)}) collective-permute-start(f32[32,1024]{1,0:T(8,128)S(1)} %pad_maximum_fusion), channel_id=1, source_target_pairs={{0,2},{1,3},{2,0},{3,1},{4,6},{5,7},{6,4},{7,5},{8,10},{9,11},{10,... | collective-permute-start | bytes 393224 | tf_op jit(solution)/shard_map/ppermute | solution.py:19
  19.7 7.5 %collective-permute-done.1 = f32[32,1024]{1,0:T(8,128)S(1)} collective-permute-done((f32[32,1024]{1,0:T(8,128)S(1)}, f32[32,1024]{1,0:T(8,128)S(1)}, u32[]{:S(2)}, u32[]{:S(2)}) %collective-permute-start.1) | collective-permute-done | bytes 131104 | tf_op jit(solution)/shard_map/ppermute | solution.py:19
  27.4 1.3 %collective-permute-done.4 = f32[32,1024]{1,0:T(8,128)S(1)} collective-permute-done((f32[32,1024]{1,0:T(8,128)S(1)}, f32[32,1024]{1,0:T(8,128)S(1)}, u32[]{:S(2)}, u32[]{:S(2)}) %collective-permute-start.4) | collective-permute-done | bytes 131104 | tf_op jit(solution)/shard_map/ppermute | solution.py:19
  29.5 3.2 %collective-permute-done.3.refs_1_ = f32[32,1024]{1,0:T(8,128)S(1)} collective-permute-done((f32[32,1024]{1,0:T(8,128)S(1)}, f32[32,1024]{1,0:T(8,128)S(1)}, u32[]{:S(2)}, u32[]{:S(2)}) %collective-permute-start.3) | collective-permute-done | bytes 131104 | tf_op jit(solution)/shard_map/ppermute | solution.py:19
  34.8 1.6 %collective-permute-start.7 = (f32[64,384]{1,0:T(8,128)S(1)}, f32[64,384]{1,0:T(8,128)S(1)}, u32[]{:S(2)}, u32[]{:S(2)}) collective-permute-start(f32[64,384]{1,0:T(8,128)S(1)} %add.76), channel_id=1, source_target_pairs={{0,8},{4,12},{8,0},{12,4},{1,9},{5,13},{9,1},{13,5},{2,10},{6,14},... | collective-permute-start | bytes 294920 | tf_op jit(solution)/shard_map/ppermute | solution.py:19
  37.7 2.8 %collective-permute-done.7 = f32[64,384]{1,0:T(8,128)S(1)} collective-permute-done((f32[64,384]{1,0:T(8,128)S(1)}, f32[64,384]{1,0:T(8,128)S(1)}, u32[]{:S(2)}, u32[]{:S(2)}) %collective-permute-start.7) | collective-permute-done | bytes 98336 | tf_op jit(solution)/shard_map/ppermute | solution.py:19
  43.6 1.3 %collective-permute-done.12.other.refs_3_ = f32[64,384]{1,0:T(8,128)S(1)} collective-permute-done((f32[64,384]{1,0:T(8,128)S(1)}, f32[64,384]{1,0:T(8,128)S(1)}, u32[]{:S(2)}, u32[]{:S(2)}) %collective-permute-start.12) | collective-permute-done | bytes 98336 | tf_op jit(solution)/shard_map/ppermute | solution.py:19
  45.6 1.4 %collective-permute-start.15 = (f32[32,1024]{1,0:T(8,128)S(1)}, f32[32,1024]{1,0:T(8,128)S(1)}, u32[]{:S(2)}, u32[]{:S(2)}) collective-permute-start(f32[32,1024]{1,0:T(8,128)S(1)} %get-tuple-element.129), channel_id=1, source_target_pairs={{0,1},{1,0},{2,3},{3,2},{4,5},{5,4},{6,7},{7,6},{8,9},{9,8},{10,11... | collective-permute-start | bytes 393224 | tf_op jit(solution)/shard_map/ppermute | solution.py:19
  46.9 1.3 %collective-permute-done.13 = f32[32,1024]{1,0:T(8,128)S(1)} collective-permute-done((f32[32,1024]{1,0:T(8,128)S(1)}, f32[32,1024]{1,0:T(8,128)S(1)}, u32[]{:S(2)}, u32[]{:S(2)}) %collective-permute-start.13) | collective-permute-done | bytes 131104 | tf_op jit(solution)/shard_map/ppermute | solution.py:19
  48.2 2.1 %collective-permute-start.14 = (f32[32,1024]{1,0:T(8,128)S(1)}, f32[32,1024]{1,0:T(8,128)S(1)}, u32[]{:S(2)}, u32[]{:S(2)}) collective-permute-start(f32[32,1024]{1,0:T(8,128)S(1)} %pad_maximum_fusion.2), channel_id=1, source_target_pairs={{0,2},{1,3},{2,0},{3,1},{4,6},{5,7},{6,4},{7,5},{8,10},{9,11},{10,... | collective-permute-start | bytes 393224 | tf_op jit(solution)/shard_map/ppermute | solution.py:19
  51.2 1.3 %collective-permute-done.15 = f32[32,1024]{1,0:T(8,128)S(1)} collective-permute-done((f32[32,1024]{1,0:T(8,128)S(1)}, f32[32,1024]{1,0:T(8,128)S(1)}, u32[]{:S(2)}, u32[]{:S(2)}) %collective-permute-start.15) | collective-permute-done | bytes 131104 | tf_op jit(solution)/shard_map/ppermute | solution.py:19
  52.6 2.5 %collective-permute-start.17 = (f32[32,1024]{1,0:T(8,128)S(1)}, f32[32,1024]{1,0:T(8,128)S(1)}, u32[]{:S(2)}, u32[]{:S(2)}) collective-permute-start(f32[32,1024]{1,0:T(8,128)S(1)} %pad_maximum_fusion.3), channel_id=1, source_target_pairs={{0,2},{1,3},{2,0},{3,1},{4,6},{5,7},{6,4},{7,5},{8,10},{9,11},{10,... | collective-permute-start | bytes 393224 | tf_op jit(solution)/shard_map/ppermute | solution.py:19
  55.1 5.2 %collective-permute-done.14 = f32[32,1024]{1,0:T(8,128)S(1)} collective-permute-done((f32[32,1024]{1,0:T(8,128)S(1)}, f32[32,1024]{1,0:T(8,128)S(1)}, u32[]{:S(2)}, u32[]{:S(2)}) %collective-permute-start.14) | collective-permute-done | bytes 131104 | tf_op jit(solution)/shard_map/ppermute | solution.py:19
  60.4 2.3 %collective-permute-done.17 = f32[32,1024]{1,0:T(8,128)S(1)} collective-permute-done((f32[32,1024]{1,0:T(8,128)S(1)}, f32[32,1024]{1,0:T(8,128)S(1)}, u32[]{:S(2)}, u32[]{:S(2)}) %collective-permute-start.17) | collective-permute-done | bytes 131104 | tf_op jit(solution)/shard_map/ppermute | solution.py:19
  62.8 2.7 %collective-permute-done.16.refs_1_ = f32[32,1024]{1,0:T(8,128)S(1)} collective-permute-done((f32[32,1024]{1,0:T(8,128)S(1)}, f32[32,1024]{1,0:T(8,128)S(1)}, u32[]{:S(2)}, u32[]{:S(2)}) %collective-permute-start.16) | collective-permute-done | bytes 131104 | tf_op jit(solution)/shard_map/ppermute | solution.py:19
  68.8 1.6 %collective-permute-start.20 = (f32[64,384]{1,0:T(8,128)S(1)}, f32[64,384]{1,0:T(8,128)S(1)}, u32[]{:S(2)}, u32[]{:S(2)}) collective-permute-start(f32[64,384]{1,0:T(8,128)S(1)} %add.88), channel_id=1, source_target_pairs={{0,8},{4,12},{8,0},{12,4},{1,9},{5,13},{9,1},{13,5},{2,10},{6,14},... | collective-permute-start | bytes 294920 | tf_op jit(solution)/shard_map/ppermute | solution.py:19
  70.5 1.3 %collective-permute-start.24 = (f32[64,384]{1,0:T(8,128)S(1)}, f32[64,384]{1,0:T(8,128)S(1)}, u32[]{:S(2)}, u32[]{:S(2)}) collective-permute-start(f32[64,384]{1,0:T(8,128)S(1)} %add.89), channel_id=1, source_target_pairs={{0,8},{4,12},{8,0},{12,4},{1,9},{5,13},{9,1},{13,5},{2,10},{6,14},... | collective-permute-start | bytes 294920 | tf_op jit(solution)/shard_map/ppermute | solution.py:19
  71.7 2.8 %collective-permute-done.20 = f32[64,384]{1,0:T(8,128)S(1)} collective-permute-done((f32[64,384]{1,0:T(8,128)S(1)}, f32[64,384]{1,0:T(8,128)S(1)}, u32[]{:S(2)}, u32[]{:S(2)}) %collective-permute-start.20) | collective-permute-done | bytes 98336 | tf_op jit(solution)/shard_map/ppermute | solution.py:19
  74.6 1.6 %collective-permute-done.24 = f32[64,384]{1,0:T(8,128)S(1)} collective-permute-done((f32[64,384]{1,0:T(8,128)S(1)}, f32[64,384]{1,0:T(8,128)S(1)}, u32[]{:S(2)}, u32[]{:S(2)}) %collective-permute-start.24) | collective-permute-done | bytes 98336 | tf_op jit(solution)/shard_map/ppermute | solution.py:19
  76.3 1.3 %collective-permute-done.25.refs_3_ = f32[64,384]{1,0:T(8,128)S(1)} collective-permute-done((f32[64,384]{1,0:T(8,128)S(1)}, f32[64,384]{1,0:T(8,128)S(1)}, u32[]{:S(2)}, u32[]{:S(2)}) %collective-permute-start.25) | collective-permute-done | bytes 98336 | tf_op jit(solution)/shard_map/ppermute | solution.py:19
  (74 shorter events, 16.3 us)
Async XLA Ops:
  4.6 7.7 %collective-permute-start = (f32[32,1024]{1,0:T(8,128)}, f32[32,1024]{1,0:T(8,128)}, u32[]{:S(2)}, u32[]{:S(2)}) collective-permute-start(f32[32,1024]{1,0:T(8,128)} %get-tuple-element.78), channel_id=1, source_target_pairs={{0,1},{1,0},{2,3},{3,2},{4,5},{5,4},{6,7},{7,6},{8,9},{9,8},{10,11... | collective-permute-start | bytes 393224 | tf_op jit(solution)/shard_map/ppermute | solution.py:19
  7.7 10.6 %collective-permute-start.2 = (f32[32,1024]{1,0:T(8,128)}, f32[32,1024]{1,0:T(8,128)}, u32[]{:S(2)}, u32[]{:S(2)}) collective-permute-start(f32[32,1024]{1,0:T(8,128)} %get-tuple-element.85), channel_id=1, source_target_pairs={{0,1},{1,0},{2,3},{3,2},{4,5},{5,4},{6,7},{7,6},{8,9},{9,8},{10,11... | collective-permute-start | bytes 393224 | tf_op jit(solution)/shard_map/ppermute | solution.py:19
  13.6 22.8 %collective-permute-start.9 = (f32[136,384]{1,0:T(8,128)S(1)}, f32[136,384]{1,0:T(8,128)S(1)}, u32[]{:S(2)}, u32[]{:S(2)}) collective-permute-start(f32[136,384]{1,0:T(8,128)S(1)} %get-tuple-element.109), channel_id=1, source_target_pairs={{0,16},{16,0},{1,17},{17,1},{2,18},{18,2},{3,19},{19,3},{4,20},{20... | collective-permute-start | bytes 626696 | tf_op jit(solution)/shard_map/ppermute | solution.py:19
  15.6 11.6 %collective-permute-start.1 = (f32[32,1024]{1,0:T(8,128)S(1)}, f32[32,1024]{1,0:T(8,128)S(1)}, u32[]{:S(2)}, u32[]{:S(2)}) collective-permute-start(f32[32,1024]{1,0:T(8,128)S(1)} %pad_maximum_fusion), channel_id=1, source_target_pairs={{0,2},{1,3},{2,0},{3,1},{4,6},{5,7},{6,4},{7,5},{8,10},{9,11},{10,... | collective-permute-start | bytes 393224 | tf_op jit(solution)/shard_map/ppermute | solution.py:19
  19.3 9.3 %collective-permute-start.4 = (f32[32,1024]{1,0:T(8,128)S(1)}, f32[32,1024]{1,0:T(8,128)S(1)}, u32[]{:S(2)}, u32[]{:S(2)}) collective-permute-start(f32[32,1024]{1,0:T(8,128)S(1)} %pad_maximum_fusion.1), channel_id=1, source_target_pairs={{0,2},{1,3},{2,0},{3,1},{4,6},{5,7},{6,4},{7,5},{8,10},{9,11},{10,... | collective-permute-start | bytes 393224 | tf_op jit(solution)/shard_map/ppermute | solution.py:19
  27.3 5.4 %collective-permute-start.3 = (f32[32,1024]{1,0:T(8,128)S(1)}, f32[32,1024]{1,0:T(8,128)S(1)}, u32[]{:S(2)}, u32[]{:S(2)}) collective-permute-start(f32[32,1024]{1,0:T(8,128)S(1)} %add_multiply_fusion.3.refs_0_), channel_id=1, source_target_pairs={{0,1},{1,0},{2,3},{3,2},{4,5},{5,4},{6,7},{7,6},{8,9},{9,8},{10,11... | collective-permute-start | bytes 393224 | tf_op jit(solution)/shard_map/ppermute | solution.py:19
  28.7 5.4 %collective-permute-start.6 = (f32[32,1024]{1,0:T(8,128)S(1)}, f32[32,1024]{1,0:T(8,128)S(1)}, u32[]{:S(2)}, u32[]{:S(2)}) collective-permute-start(f32[32,1024]{1,0:T(8,128)S(1)} %add_multiply_fusion.2.refs_0_), channel_id=1, source_target_pairs={{0,1},{1,0},{2,3},{3,2},{4,5},{5,4},{6,7},{7,6},{8,9},{9,8},{10,11... | collective-permute-start | bytes 393224 | tf_op jit(solution)/shard_map/ppermute | solution.py:19
  33.3 1.5 %collective-permute-start.5 = (f32[64,384]{1,0:T(8,128)S(1)}, f32[64,384]{1,0:T(8,128)S(1)}, u32[]{:S(2)}, u32[]{:S(2)}) collective-permute-start(f32[64,384]{1,0:T(8,128)S(1)} %get-tuple-element.98), channel_id=1, source_target_pairs={{0,4},{4,0},{8,12},{12,8},{1,5},{5,1},{9,13},{13,9},{2,6},{6,2},{1... | collective-permute-start | bytes 294920 | tf_op jit(solution)/shard_map/ppermute | solution.py:19
  34.7 1.7 %collective-permute-start.8 = (f32[64,384]{1,0:T(8,128)S(1)}, f32[64,384]{1,0:T(8,128)S(1)}, u32[]{:S(2)}, u32[]{:S(2)}) collective-permute-start(f32[64,384]{1,0:T(8,128)S(1)} %get-tuple-element.104), channel_id=1, source_target_pairs={{0,4},{4,0},{8,12},{12,8},{1,5},{5,1},{9,13},{13,9},{2,6},{6,2},{1... | collective-permute-start | bytes 294920 | tf_op jit(solution)/shard_map/ppermute | solution.py:19
  34.8 5.7 %collective-permute-start.7 = (f32[64,384]{1,0:T(8,128)S(1)}, f32[64,384]{1,0:T(8,128)S(1)}, u32[]{:S(2)}, u32[]{:S(2)}) collective-permute-start(f32[64,384]{1,0:T(8,128)S(1)} %add.76), channel_id=1, source_target_pairs={{0,8},{4,12},{8,0},{12,4},{1,9},{5,13},{9,1},{13,5},{2,10},{6,14},... | collective-permute-start | bytes 294920 | tf_op jit(solution)/shard_map/ppermute | solution.py:19
  36.5 5.7 %collective-permute-start.11 = (f32[64,384]{1,0:T(8,128)S(1)}, f32[64,384]{1,0:T(8,128)S(1)}, u32[]{:S(2)}, u32[]{:S(2)}) collective-permute-start(f32[64,384]{1,0:T(8,128)S(1)} %add.77), channel_id=1, source_target_pairs={{0,8},{4,12},{8,0},{12,4},{1,9},{5,13},{9,1},{13,5},{2,10},{6,14},... | collective-permute-start | bytes 294920 | tf_op jit(solution)/shard_map/ppermute | solution.py:19
  40.5 1.7 %collective-permute-start.10 = (f32[64,384]{1,0:T(8,128)S(1)}, f32[64,384]{1,0:T(8,128)S(1)}, u32[]{:S(2)}, u32[]{:S(2)}) collective-permute-start(f32[64,384]{1,0:T(8,128)S(1)} %fusion.11.own.refs_0_), channel_id=1, source_target_pairs={{0,4},{4,0},{8,12},{12,8},{1,5},{5,1},{9,13},{13,9},{2,6},{6,2},{1... | collective-permute-start | bytes 294920 | tf_op jit(solution)/shard_map/ppermute | solution.py:19
  42.8 5.3 %collective-permute-start.13 = (f32[32,1024]{1,0:T(8,128)S(1)}, f32[32,1024]{1,0:T(8,128)S(1)}, u32[]{:S(2)}, u32[]{:S(2)}) collective-permute-start(f32[32,1024]{1,0:T(8,128)S(1)} %get-tuple-element.119), channel_id=1, source_target_pairs={{0,1},{1,0},{2,3},{3,2},{4,5},{5,4},{6,7},{7,6},{8,9},{9,8},{10,11... | collective-permute-start | bytes 393224 | tf_op jit(solution)/shard_map/ppermute | solution.py:19
  45.6 7.0 %collective-permute-start.15 = (f32[32,1024]{1,0:T(8,128)S(1)}, f32[32,1024]{1,0:T(8,128)S(1)}, u32[]{:S(2)}, u32[]{:S(2)}) collective-permute-start(f32[32,1024]{1,0:T(8,128)S(1)} %get-tuple-element.129), channel_id=1, source_target_pairs={{0,1},{1,0},{2,3},{3,2},{4,5},{5,4},{6,7},{7,6},{8,9},{9,8},{10,11... | collective-permute-start | bytes 393224 | tf_op jit(solution)/shard_map/ppermute | solution.py:19
  48.2 12.0 %collective-permute-start.14 = (f32[32,1024]{1,0:T(8,128)S(1)}, f32[32,1024]{1,0:T(8,128)S(1)}, u32[]{:S(2)}, u32[]{:S(2)}) collective-permute-start(f32[32,1024]{1,0:T(8,128)S(1)} %pad_maximum_fusion.2), channel_id=1, source_target_pairs={{0,2},{1,3},{2,0},{3,1},{4,6},{5,7},{6,4},{7,5},{8,10},{9,11},{10,... | collective-permute-start | bytes 393224 | tf_op jit(solution)/shard_map/ppermute | solution.py:19
  52.6 10.1 %collective-permute-start.17 = (f32[32,1024]{1,0:T(8,128)S(1)}, f32[32,1024]{1,0:T(8,128)S(1)}, u32[]{:S(2)}, u32[]{:S(2)}) collective-permute-start(f32[32,1024]{1,0:T(8,128)S(1)} %pad_maximum_fusion.3), channel_id=1, source_target_pairs={{0,2},{1,3},{2,0},{3,1},{4,6},{5,7},{6,4},{7,5},{8,10},{9,11},{10,... | collective-permute-start | bytes 393224 | tf_op jit(solution)/shard_map/ppermute | solution.py:19
  60.3 5.3 %collective-permute-start.16 = (f32[32,1024]{1,0:T(8,128)S(1)}, f32[32,1024]{1,0:T(8,128)S(1)}, u32[]{:S(2)}, u32[]{:S(2)}) collective-permute-start(f32[32,1024]{1,0:T(8,128)S(1)} %add_multiply_fusion.1.refs_0_), channel_id=1, source_target_pairs={{0,1},{1,0},{2,3},{3,2},{4,5},{5,4},{6,7},{7,6},{8,9},{9,8},{10,11... | collective-permute-start | bytes 393224 | tf_op jit(solution)/shard_map/ppermute | solution.py:19
  62.7 5.4 %collective-permute-start.19 = (f32[32,1024]{1,0:T(8,128)S(1)}, f32[32,1024]{1,0:T(8,128)S(1)}, u32[]{:S(2)}, u32[]{:S(2)}) collective-permute-start(f32[32,1024]{1,0:T(8,128)S(1)} %add_multiply_fusion.refs_0_), channel_id=1, source_target_pairs={{0,1},{1,0},{2,3},{3,2},{4,5},{5,4},{6,7},{7,6},{8,9},{9,8},{10,11... | collective-permute-start | bytes 393224 | tf_op jit(solution)/shard_map/ppermute | solution.py:19
  66.2 2.7 %collective-permute-start.18 = (f32[64,384]{1,0:T(8,128)S(1)}, f32[64,384]{1,0:T(8,128)S(1)}, u32[]{:S(2)}, u32[]{:S(2)}) collective-permute-start(f32[64,384]{1,0:T(8,128)S(1)} %get-tuple-element.139), channel_id=1, source_target_pairs={{0,4},{4,0},{8,12},{12,8},{1,5},{5,1},{9,13},{13,9},{2,6},{6,2},{1... | collective-permute-start | bytes 294920 | tf_op jit(solution)/shard_map/ppermute | solution.py:19
  66.3 8.2 %collective-permute-start.22 = (f32[128,384]{1,0:T(8,128)S(1)}, f32[128,384]{1,0:T(8,128)S(1)}, u32[]{:S(2)}, u32[]{:S(2)}) collective-permute-start(f32[128,384]{1,0:T(8,128)S(1)} %maximum_multiply_fusion), channel_id=1, source_target_pairs={{0,16},{16,0},{1,17},{17,1},{2,18},{18,2},{3,19},{19,3},{4,20},{20... | collective-permute-start | bytes 589832 | tf_op jit(solution)/shard_map/ppermute | solution.py:19
  68.7 1.7 %collective-permute-start.21 = (f32[64,384]{1,0:T(8,128)S(1)}, f32[64,384]{1,0:T(8,128)S(1)}, u32[]{:S(2)}, u32[]{:S(2)}) collective-permute-start(f32[64,384]{1,0:T(8,128)S(1)} %get-tuple-element.145), channel_id=1, source_target_pairs={{0,4},{4,0},{8,12},{12,8},{1,5},{5,1},{9,13},{13,9},{2,6},{6,2},{1... | collective-permute-start | bytes 294920 | tf_op jit(solution)/shard_map/ppermute | solution.py:19
  68.8 5.7 %collective-permute-start.20 = (f32[64,384]{1,0:T(8,128)S(1)}, f32[64,384]{1,0:T(8,128)S(1)}, u32[]{:S(2)}, u32[]{:S(2)}) collective-permute-start(f32[64,384]{1,0:T(8,128)S(1)} %add.88), channel_id=1, source_target_pairs={{0,8},{4,12},{8,0},{12,4},{1,9},{5,13},{9,1},{13,5},{2,10},{6,14},... | collective-permute-start | bytes 294920 | tf_op jit(solution)/shard_map/ppermute | solution.py:19
  70.5 5.7 %collective-permute-start.24 = (f32[64,384]{1,0:T(8,128)S(1)}, f32[64,384]{1,0:T(8,128)S(1)}, u32[]{:S(2)}, u32[]{:S(2)}) collective-permute-start(f32[64,384]{1,0:T(8,128)S(1)} %add.89), channel_id=1, source_target_pairs={{0,8},{4,12},{8,0},{12,4},{1,9},{5,13},{9,1},{13,5},{2,10},{6,14},... | collective-permute-start | bytes 294920 | tf_op jit(solution)/shard_map/ppermute | solution.py:19
  74.5 1.8 %collective-permute-start.23 = (f32[64,384]{1,0:T(8,128)S(1)}, f32[64,384]{1,0:T(8,128)S(1)}, u32[]{:S(2)}, u32[]{:S(2)}) collective-permute-start(f32[64,384]{1,0:T(8,128)S(1)} %fusion.5.refs_0_), channel_id=1, source_target_pairs={{0,4},{4,0},{8,12},{12,8},{1,5},{5,1},{9,13},{13,9},{2,6},{6,2},{1... | collective-permute-start | bytes 294920 | tf_op jit(solution)/shard_map/ppermute | solution.py:19
  (6 other events, 53.5 us)

commit v4 on v3

v4 whole, which is shorter than its diff:
```python
import functools

import jax
import jax.numpy as jnp
from jax import lax
from jax.experimental import pallas as pl
from jax.experimental.pallas import tpu as pltpu
from jax.sharding import PartitionSpec as P

MAX_CHUNKS = 2
LIMIT = 16 * 2**20
LARGE = 16 * 2**20
NT = (((1,), (1,)), ((), ()))
NN = (((1,), (0,)), ((), ()))
VMEM = pl.BlockSpec(memory_space=pltpu.VMEM)


def swap(value, axis, stride):
    return lax.ppermute(value, axis, [(i, i ^ stride) for i in range(lax.axis_size(axis))])


def shifted(value, axis, by):
    length = lax.axis_size(axis)
    pairs = [(i, i + by) for i in range(length) if 0 <= i + by < length]
    return lax.ppermute(value, axis, pairs)


def class_weight(labels):
    return jnp.where(
        labels == 0, 1.0, jnp.where(labels == 1, 0.5, jnp.where(labels == 2, 0.25, 0.125))
    ).astype(jnp.float32)


def split(value):
    high = value.astype(jnp.bfloat16)
    return high, (value - high.astype(jnp.float32)).astype(jnp.bfloat16)


def product(value, high, low, dims):
    top, rest = split(value)
    rows = value.shape[0]
    dot = functools.partial(
        lax.dot_general, dimension_numbers=dims, preferred_element_type=jnp.float32
    )
    both = dot(jnp.concatenate([top, rest], axis=0), high)
    return both[:rows] + (both[rows:] + dot(top, low))


def call(kernel, shapes, operands, flops=0, scratch=()):
    return pl.pallas_call(
        kernel,
        out_shape=shapes,
        in_specs=[VMEM] * len(operands),
        out_specs=[VMEM] * len(shapes),
        scratch_shapes=scratch,
        compiler_params=pltpu.CompilerParams(vmem_limit_bytes=LIMIT),
        cost_estimate=pl.CostEstimate(
            flops=flops, bytes_accessed=sum(4 * o.size for o in operands), transcendentals=0
        ),
    )(*operands)


def sides(first, second):
    left = lax.axis_index("dp") % 2 == 0
    return jnp.where(left, first, second), jnp.where(left, second, first)


def block_order(parts):
    bits = parts.bit_length() - 1
    return [int(format(i, "b").zfill(bits)[::-1], 2) for i in range(parts)]


def column(active):
    cells = active.shape[1]
    return jnp.broadcast_to(active[...].astype(jnp.float32), (8, cells)).T[:, :1]


def place(turned, parts, keep, send):
    here = lax.axis_index("cell")
    size = turned.shape[0] // parts
    for index, x in enumerate(block_order(parts)):
        start = pl.multiple_of((here ^ x) * size, size)
        block = send if index // (parts // 2) else keep
        spot = index % (parts // 2) * size
        block[spot : spot + size, :] = turned[pl.ds(start, size), :]


def rows_product(high, low, both):
    count = both.shape[1] // 2
    dot = functools.partial(jnp.dot, preferred_element_type=jnp.float32)
    out = dot(high, both)
    return out[:, :count] + (out[:, count:] + dot(low, both[:, :count]))


def column(active):
    cells = active.shape[1]
    return jnp.broadcast_to(active[...].astype(jnp.float32), (8, cells)).T[:, :1]


def rows_product(high, low, both):
    count = both.shape[1] // 2
    dot = functools.partial(jnp.dot, preferred_element_type=jnp.float32)
    out = dot(high, both)
    return out[:, :count] + (out[:, count:] + dot(low, both[:, :count]))


def first_forward(probes, tile, active, coupling, chunks):
    parts = lax.axis_size("cell")
    cells, count = probes.shape
    data = tile.shape[0]
    half = cells // 2
    rows = count // chunks
    size = rows // parts
    step = 512 if data % 512 == 0 else data

    def kernel(probes_hbm, tile_hbm, active_hbm, coupling_hbm, high, low, message, factors, *refs):
        blocks, (probes, tile, active, coupling, turned, masked, arrived) = refs[:-7], refs[-7:]
        pairs = [(active_hbm, active), (probes_hbm, probes)]
        pairs += [
            (tile_hbm.at[pl.ds(at, step)], tile.at[pl.ds(at, step)]) for at in range(0, data, step)
        ]
        pairs += [(coupling_hbm, coupling)]
        copies = [
            pltpu.make_async_copy(source, target, arrived.at[index])
            for index, (source, target) in enumerate(pairs)
        ]
        for copy in copies:
            copy.start()
        copies[0].wait()
        mask = column(active)
        copies[1].wait()
        values = probes[...] * mask
        both = jnp.concatenate(split(values), axis=1)
        masked[...] = values.T
        for index, at in enumerate(range(0, data, step)):
            copies[2 + index].wait()
            block = slice(at, at + step)
            top, rest = split(tile[block, :])
            high[block, :] = top
            low[block, :] = rest
            turned[:, block] = rows_product(top, rest, both).T
        copies[-1].wait()
        here = lax.axis_index("cell")
        own = pl.ds(pl.multiple_of(lax.axis_index("dp") % 2 * half, half), half)
        for chunk in range(chunks):
            for index, x in enumerate(block_order(parts)):
                start = pl.multiple_of((chunk * parts + (here ^ x)) * size, size)
                block = blocks[2 * chunk + index // (parts // 2)]
                spot = index % (parts // 2) * size
                block[spot : spot + size, :] = turned[pl.ds(start, size), :]
                spot = (chunk * parts + index) * size
                message[spot : spot + size, :] = masked[pl.ds(start, size), own]
        message[count:, :] = jnp.broadcast_to(coupling[:, own], (8, half))
        section = lax.axis_index("section")
        last = lax.axis_size("section") - 1
        keep = active[:, own].astype(jnp.float32)
        zero = jnp.zeros_like(keep)
        factors[0:1, :] = keep
        factors[1:2, :] = jnp.where(section == 0, zero, coupling[:, own])
        factors[2:3, :] = jnp.where(section == last, zero, zero + 1.0)

    operands = [pltpu.with_memory_space_constraint(o, pltpu.HBM) for o in (probes, tile, active, coupling)]
    shapes = [pltpu.VMEM((data, cells), jnp.bfloat16)] * 2
    shapes += [jax.ShapeDtypeStruct((count + 8, half), jnp.float32)]
    shapes += [jax.ShapeDtypeStruct((8, half), jnp.float32)]
    shapes += [jax.ShapeDtypeStruct((rows // 2, data), jnp.float32)] * (2 * chunks)
    outs = pl.pallas_call(
        kernel,
        in_specs=[pl.BlockSpec(memory_space=pltpu.HBM)] * len(operands),
        out_specs=[VMEM] * len(shapes),
        out_shape=shapes,
        scratch_shapes=[pltpu.VMEM(o.shape, o.dtype) for o in operands]
        + [
            pltpu.VMEM((count, data), jnp.float32),
            pltpu.VMEM((count, cells), jnp.float32),
            pltpu.SemaphoreType.DMA((data // step + 3,)),
        ],
        compiler_params=pltpu.CompilerParams(vmem_limit_bytes=LARGE),
        cost_estimate=pl.CostEstimate(
            flops=6 * data * cells * count, bytes_accessed=4 * data * cells, transcendentals=0
        ),
    )(*operands)
    return outs[:4], [outs[4 + 2 * i : 6 + 2 * i] for i in range(chunks)]


def turn(high, low):
    def kernel(high, low, high_t, low_t):
        high_t[...] = high[...].T
        low_t[...] = low[...].T

    shape = jax.ShapeDtypeStruct(high.shape[::-1], jnp.bfloat16)
    return call(kernel, [shape, shape], [high, low])


def backward(blocks, high, low):
    def kernel(*refs):
        high, low, own, other = refs[-4:]
        value = jnp.concatenate([ref[...] for ref in refs[:-4]], axis=0)
        back = product(value, high[...], low[...], NN)
        half = own.shape[1]
        own[...], other[...] = sides(back[:, :half], back[:, half:])

    rows = sum(block.shape[0] for block in blocks)
    shape = jax.ShapeDtypeStruct((rows, high.shape[1] // 2), jnp.float32)
    return call(kernel, [shape, shape], [*blocks, high, low], 6 * rows * high.size)


def forward(own, other, mask, high_t, low_t):
    def kernel(own, other, mask, high_t, low_t, keep, send):
        masked = jnp.concatenate(sides(own[...], other[...]), axis=1) * mask[...]
        out = product(masked, high_t[...], low_t[...], NN)
        size = out.shape[0] // 2
        keep[...] = out[:size]
        send[...] = out[size:]

    rows = own.shape[0]
    shape = jax.ShapeDtypeStruct((rows // 2, high_t.shape[1]), jnp.float32)
    operands = [own, other, mask, high_t, low_t]
    return call(kernel, [shape, shape], operands, 6 * rows * high_t.size)


def finish(halves):
    chunks = len(halves) // 2
    parts = lax.axis_size("cell")
    rows, half = halves[0].shape
    size = rows // parts

    def kernel(*refs):
        out, turned = refs[-2:]
        side = lax.axis_index("dp") % 2
        here = lax.axis_index("cell")
        own = pl.ds(pl.multiple_of(side * half, half), half)
        other = pl.ds(pl.multiple_of((1 - side) * half, half), half)
        for chunk in range(chunks):
            for index, x in enumerate(block_order(parts)):
                start = pl.multiple_of((chunk * parts + (here ^ x)) * size, size)
                block = slice(index * size, (index + 1) * size)
                turned[pl.ds(start, size), own] = refs[2 * chunk][block, :]
                turned[pl.ds(start, size), other] = refs[2 * chunk + 1][block, :]
        out[...] = turned[...].T

    shape = jax.ShapeDtypeStruct((2 * half, chunks * rows), jnp.float32)
    return pl.pallas_call(
        kernel,
        out_shape=shape,
        in_specs=[VMEM] * (2 * chunks),
        out_specs=VMEM,
        scratch_shapes=[pltpu.VMEM(shape.shape[::-1], jnp.float32)],
        compiler_params=pltpu.CompilerParams(vmem_limit_bytes=LIMIT),
    )(*halves)


def sum_cells(keep, send, shared):
    parts = lax.axis_size("cell")
    value = yield (lambda a, b: a + b), keep, swap(send, "cell", 1)
    half = value.shape[0] // 2
    stride = 2
    while stride < parts // 2:
        value = value[:half] + swap(value[half:], "cell", stride)
        half //= 2
        stride *= 2
    other = swap(jnp.concatenate([value[half:], value[:half]], axis=0), "cell", stride)
    value = yield (lambda a, b: (a + b) * shared["weight"]), value, other
    while stride > 2:
        stride //= 2
        value = jnp.concatenate([value, swap(value, "cell", stride)], axis=0)
    return value, swap(value, "cell", 1)


def sum_data(own, other):
    total = yield (lambda a, b: a + b), own, swap(other, "dp", 1)
    stride = 2
    while stride < lax.axis_size("dp") // 2:
        total = total + swap(total, "dp", stride)
        stride *= 2
    return total, swap(total, "dp", stride)


def in_turn(chains, rounds):
    results = [None] * len(chains)
    answers = [None] * len(chains)
    token = None
    waiting = list(range(len(chains)))
    while waiting:
        steps = rounds[0]
        rounds = rounds[1:] + rounds[:1]
        for index, (chain, single) in enumerate(chains):
            for _ in range(1 if single else steps):
                if index not in waiting:
                    break
                try:
                    step = chain.send(answers[index])
                except StopIteration as stop:
                    results[index] = stop.value
                    waiting.remove(index)
                    break
                answers[index] = None
                if step is None:
                    continue
                function, *values = step
                if token is not None:
                    *values, _ = lax.optimization_barrier((*values, token))
                answers[index] = function(*values)
                token = jax.tree.leaves(answers[index])[0]
    return results


def neighbours(message):
    if lax.axis_size("section") == 2:
        got = swap(message, "section", 1)
        return got, got
    return shifted(message, "section", 1), shifted(message, "section", -1)


def local(probes, jacobian, classes, active, coupling):
    probes, tile = probes[0], jacobian[0]
    count, half = probes.shape[1], probes.shape[0] // 2
    parts = lax.axis_size("cell")
    chunks = MAX_CHUNKS
    while chunks > 1 and count % (8 * chunks * parts):
        chunks -= 1
    rows = count // chunks

    (high, low, message, factors), blocks = first_forward(probes, tile, active, coupling, chunks)
    shared = {"mask": active.astype(jnp.float32), "mask_own": factors[:1]}
    shared["weight"] = class_weight(classes)

    def ready(message):
        below, above = neighbours(message)
        shared.update(first=(message, below, above))
        shared.update(strength=(factors[1:2], factors[2:3] * above[count : count + 1]))
        return message

    def turned(high, low):
        shared["turned"] = turn(high, low)
        return shared["turned"]

    def part(value, chunk):
        return value[chunk * rows : (chunk + 1) * rows]

    def smoothing(here, under, over):
        strength, strength_next = shared["strength"]
        return strength * (here - under) + strength_next * (here - over)

    def hessian(keep, send, smooth):
        sent = yield from sum_cells(keep, send, shared)
        own, other = yield (lambda *values: backward(values, high, low)), *sent
        total, other = yield from sum_data(own, other)
        own = yield (lambda a, b: shared["mask_own"] * (a + b + smooth())), total, other
        return own, swap(own, "dp", 1)

    def second_message(*halves):
        masked = jnp.concatenate(halves, axis=0) * shared["mask_own"]
        shared["second"] = (masked, *neighbours(masked))
        return masked

    def chain(chunk):
        def smooth_first():
            return smoothing(*[part(value, chunk) for value in shared["first"]])

        image = yield from hessian(*blocks[chunk], smooth_first)
        shared[chunk] = image

        def smooth_second():
            return smoothing(*[part(value, chunk) for value in shared["second"]])

        sent = yield (lambda a, b: forward(a, b, shared["mask"], *shared["turned"])), *image
        return (yield from hessian(*sent, smooth_second))

    def between():
        yield None
        yield None
        yield None
        yield None
        yield None
        halves = [value for chunk in range(chunks) for value in shared[chunk]]
        return (yield (lambda *values: finish(values)), *halves)

    def after():
        yield ready, message
        yield None
        yield turned, high, low
        yield None
        yield None
        yield second_message, *[shared[chunk][0] for chunk in range(chunks)]

    chains = [(chain(chunk), False) for chunk in range(chunks)]
    chains[1:1] = [(between(), True)]
    halves, first, *rest = in_turn(chains + [(after(), True)], (1, 1, 2, 1, 1))
    for more in rest[:-1]:
        halves = halves + more
    return first[None], finish(halves)[None]


def solution(mesh):
    return jax.shard_map(
        local,
        mesh=mesh,
        in_specs=(
            P("section", "cell", None),
            P("section", "dp", "cell"),
            P("section", "dp"),
            P("section", "cell"),
            P("section", "cell"),
        ),
        out_specs=(P("section", "cell", None), P("section", "cell", None)),
        check_vma=False,
    )
```

time: 78.7 us -> 75.4 us (0.958)
  waiting for transfers between devices: 41.8 us -> 39.6 us
  starting transfers between devices: 22.8 us -> 24.8 us
  other arithmetic: 2.36 us -> 0.44 us
  Pallas kernels: 10.5 us -> 9.42 us
    ppermute x26, waiting for transfers between devices: 41.8 us -> 39.6 us  [swap(): lax.ppermute(value, axis, [(i, i ^ stride) for i in range(lax.axis_size(a...]
    ppermute x26, starting transfers between devices: 22.8 us -> 24.8 us  [swap(): lax.ppermute(value, axis, [(i, i ^ stride) for i in range(lax.axis_size(a...]
    add x4, other arithmetic: 2 us -> 0.07 us  [sum_cells(): value = (yield (lambda a, b: a + b, keep, swap(send, 'cell', 1)))]
    pallas_call x1, Pallas kernels: 3.92 us -> 2.95 us  [first_forward(): pl.pallas_call(kernel, in_specs=[pl.BlockSpec(memory_space=pltpu.HBM)] *...]
    pallas_call x8 -> x7, Pallas kernels: 4.73 us -> 4.59 us  [call(): pl.pallas_call(kernel, out_shape=shapes, in_specs=[VMEM] * len(operands),...]
  transfers between devices with their start and end apart: 26 -> 26, of which waited for: 17 -> 18; matrix products, arithmetic and copies ran while one was open for 3% -> 1% of each run, Pallas kernels for 6% -> 7%
where the time goes in v4:
time: 75.4 us; the launch traced here: 75.2 us
  waiting for transfers between devices  39.6 us (53%)
  starting transfers between devices  24.8 us (33%)
  Pallas kernels  9.42 us (12%)
  between operations  0.95 us (1%)
    ppermute x26, waiting for transfers between devices, swap(): lax.ppermute(value, axis, [(i, i ^ stride) for i in range(lax.axis_size(a...  39.6 us
    ppermute x26, starting transfers between devices, swap(): lax.ppermute(value, axis, [(i, i ^ stride) for i in range(lax.axis_size(a...  24.8 us
    pallas_call x7, Pallas kernels, call(): pl.pallas_call(kernel, out_shape=shapes, in_specs=[VMEM] * len(operands),...  4.59 us
    pallas_call x1, Pallas kernels, first_forward(): pl.pallas_call(kernel, in_specs=[pl.BlockSpec(memory_space=pltpu.HBM)] *...  2.95 us
    pallas_call x2, Pallas kernels, finish(): pl.pallas_call(kernel, out_shape=shape, in_specs=[VMEM] * (2 * chunks), o...  1.88 us
  transfers between devices with their start and end apart: 26, of which 18 were waited for; matrix products, arithmetic and copies ran while one was open for 1% of the time, Pallas kernels for 7%

profile of v4, /device:TPU:0, one launch (start us, length us, event | category | flops | bytes accessed | tf_op | source)
XLA Modules:
  0.0 75.2 jit_solution(17799779166171094795)
XLA Ops:
  0.6 2.9 %shard_map.68 = (bf16[1024,768]{1,0:T(8,128)(2,1)S(1)}, bf16[1024,768]{1,0:T(8,128)(2,1)S(1)}, f32[136,384]{1,0:T(8,128)S(1)}, f32[8,384]{1,0:T(8,128)S(1)}, f32...) custom-call(f32[768,128]{1,0:T(8,128)} %bitcast.8, ...), custom_call_target="tpu_custom_call" | custom-call | flops 603979776 | bytes 3145728 | tf_op jit(solution)/shard_map/pallas_call | solution.py:167
  3.6 3.1 %collective-permute-start = (f32[32,1024]{1,0:T(8,128)S(1)}, f32[32,1024]{1,0:T(8,128)S(1)}, u32[]{:S(2)}, u32[]{:S(2)}) collective-permute-start(f32[32,1024]{1,0:T(8,128)S(1)} %get-tuple-element.77), channel_id=1, source_target_pairs={{0,1},{1,0},{2,3},{3,2},{4,5},{5,4},{6,7},{7,6},{8,9},{9,8},{10,11... | collective-permute-start | bytes 393224 | tf_op jit(solution)/shard_map/ppermute | solution.py:19
  6.8 4.2 %collective-permute-done = f32[32,1024]{1,0:T(8,128)S(1)} collective-permute-done((f32[32,1024]{1,0:T(8,128)S(1)}, f32[32,1024]{1,0:T(8,128)S(1)}, u32[]{:S(2)}, u32[]{:S(2)}) %collective-permute-start) | collective-permute-done | bytes 131104 | tf_op jit(solution)/shard_map/ppermute | solution.py:19
  11.1 3.1 %collective-permute-start.1 = (f32[32,1024]{1,0:T(8,128)S(1)}, f32[32,1024]{1,0:T(8,128)S(1)}, u32[]{:S(2)}, u32[]{:S(2)}) collective-permute-start(f32[32,1024]{1,0:T(8,128)S(1)} %pad_maximum_fusion), channel_id=1, source_target_pairs={{0,2},{1,3},{2,0},{3,1},{4,6},{5,7},{6,4},{7,5},{8,10},{9,11},{10,... | collective-permute-start | bytes 393224 | tf_op jit(solution)/shard_map/ppermute | solution.py:19
  14.3 2.7 %collective-permute-start.4 = (f32[32,1024]{1,0:T(8,128)S(1)}, f32[32,1024]{1,0:T(8,128)S(1)}, u32[]{:S(2)}, u32[]{:S(2)}) collective-permute-start(f32[32,1024]{1,0:T(8,128)S(1)} %pad_maximum_fusion.1), channel_id=1, source_target_pairs={{0,2},{1,3},{2,0},{3,1},{4,6},{5,7},{6,4},{7,5},{8,10},{9,11},{10,... | collective-permute-start | bytes 393224 | tf_op jit(solution)/shard_map/ppermute | solution.py:19
  17.0 1.5 %collective-permute-start.9 = (f32[136,384]{1,0:T(8,128)S(1)}, f32[136,384]{1,0:T(8,128)S(1)}, u32[]{:S(2)}, u32[]{:S(2)}) collective-permute-start(f32[136,384]{1,0:T(8,128)S(1)} %get-tuple-element.83), channel_id=1, source_target_pairs={{0,16},{16,0},{1,17},{17,1},{2,18},{18,2},{3,19},{19,3},{4,20},{20... | collective-permute-start | bytes 626696 | tf_op jit(solution)/shard_map/ppermute | solution.py:19
  18.5 4.7 %collective-permute-done.1 = f32[32,1024]{1,0:T(8,128)S(1)} collective-permute-done((f32[32,1024]{1,0:T(8,128)S(1)}, f32[32,1024]{1,0:T(8,128)S(1)}, u32[]{:S(2)}, u32[]{:S(2)}) %collective-permute-start.1) | collective-permute-done | bytes 131104 | tf_op jit(solution)/shard_map/ppermute | solution.py:19
  25.5 3.5 %collective-permute-done.3.refs_1_ = f32[32,1024]{1,0:T(8,128)S(1)} collective-permute-done((f32[32,1024]{1,0:T(8,128)S(1)}, f32[32,1024]{1,0:T(8,128)S(1)}, u32[]{:S(2)}, u32[]{:S(2)}) %collective-permute-start.3) | collective-permute-done | bytes 131104 | tf_op jit(solution)/shard_map/ppermute | solution.py:19
  29.7 1.3 %collective-permute-done.5 = f32[64,384]{1,0:T(8,128)S(1)} collective-permute-done((f32[64,384]{1,0:T(8,128)S(1)}, f32[64,384]{1,0:T(8,128)S(1)}, u32[]{:S(2)}, u32[]{:S(2)}) %collective-permute-start.5) | collective-permute-done | bytes 98336 | tf_op jit(solution)/shard_map/ppermute | solution.py:19
  31.0 1.3 %collective-permute-start.6 = (f32[64,384]{1,0:T(8,128)S(1)}, f32[64,384]{1,0:T(8,128)S(1)}, u32[]{:S(2)}, u32[]{:S(2)}) collective-permute-start(f32[64,384]{1,0:T(8,128)S(1)} %add.76), channel_id=1, source_target_pairs={{0,8},{4,12},{8,0},{12,4},{1,9},{5,13},{9,1},{13,5},{2,10},{6,14},... | collective-permute-start | bytes 294920 | tf_op jit(solution)/shard_map/ppermute | solution.py:19
  33.0 1.3 %collective-permute-done.8 = f32[64,384]{1,0:T(8,128)S(1)} collective-permute-done((f32[64,384]{1,0:T(8,128)S(1)}, f32[64,384]{1,0:T(8,128)S(1)}, u32[]{:S(2)}, u32[]{:S(2)}) %collective-permute-start.8) | collective-permute-done | bytes 98336 | tf_op jit(solution)/shard_map/ppermute | solution.py:19
  36.2 3.0 %collective-permute-done.11 = f32[64,384]{1,0:T(8,128)S(1)} collective-permute-done((f32[64,384]{1,0:T(8,128)S(1)}, f32[64,384]{1,0:T(8,128)S(1)}, u32[]{:S(2)}, u32[]{:S(2)}) %collective-permute-start.11) | collective-permute-done | bytes 98336 | tf_op jit(solution)/shard_map/ppermute | solution.py:19
  40.3 1.3 %collective-permute-done.12.other.refs_3_ = f32[64,384]{1,0:T(8,128)S(1)} collective-permute-done((f32[64,384]{1,0:T(8,128)S(1)}, f32[64,384]{1,0:T(8,128)S(1)}, u32[]{:S(2)}, u32[]{:S(2)}) %collective-permute-start.12) | collective-permute-done | bytes 98336 | tf_op jit(solution)/shard_map/ppermute | solution.py:19
  42.3 1.7 %collective-permute-start.15 = (f32[32,1024]{1,0:T(8,128)S(1)}, f32[32,1024]{1,0:T(8,128)S(1)}, u32[]{:S(2)}, u32[]{:S(2)}) collective-permute-start(f32[32,1024]{1,0:T(8,128)S(1)} %get-tuple-element.123), channel_id=1, source_target_pairs={{0,1},{1,0},{2,3},{3,2},{4,5},{5,4},{6,7},{7,6},{8,9},{9,8},{10,11... | collective-permute-start | bytes 393224 | tf_op jit(solution)/shard_map/ppermute | solution.py:19
  45.0 2.1 %collective-permute-start.14 = (f32[32,1024]{1,0:T(8,128)S(1)}, f32[32,1024]{1,0:T(8,128)S(1)}, u32[]{:S(2)}, u32[]{:S(2)}) collective-permute-start(f32[32,1024]{1,0:T(8,128)S(1)} %pad_maximum_fusion.2), channel_id=1, source_target_pairs={{0,2},{1,3},{2,0},{3,1},{4,6},{5,7},{6,4},{7,5},{8,10},{9,11},{10,... | collective-permute-start | bytes 393224 | tf_op jit(solution)/shard_map/ppermute | solution.py:19
  48.0 1.3 %collective-permute-done.15 = f32[32,1024]{1,0:T(8,128)S(1)} collective-permute-done((f32[32,1024]{1,0:T(8,128)S(1)}, f32[32,1024]{1,0:T(8,128)S(1)}, u32[]{:S(2)}, u32[]{:S(2)}) %collective-permute-start.15) | collective-permute-done | bytes 131104 | tf_op jit(solution)/shard_map/ppermute | solution.py:19
  49.3 2.8 %collective-permute-start.17 = (f32[32,1024]{1,0:T(8,128)S(1)}, f32[32,1024]{1,0:T(8,128)S(1)}, u32[]{:S(2)}, u32[]{:S(2)}) collective-permute-start(f32[32,1024]{1,0:T(8,128)S(1)} %pad_maximum_fusion.3), channel_id=1, source_target_pairs={{0,2},{1,3},{2,0},{3,1},{4,6},{5,7},{6,4},{7,5},{8,10},{9,11},{10,... | collective-permute-start | bytes 393224 | tf_op jit(solution)/shard_map/ppermute | solution.py:19
  52.2 4.4 %collective-permute-done.14 = f32[32,1024]{1,0:T(8,128)S(1)} collective-permute-done((f32[32,1024]{1,0:T(8,128)S(1)}, f32[32,1024]{1,0:T(8,128)S(1)}, u32[]{:S(2)}, u32[]{:S(2)}) %collective-permute-start.14) | collective-permute-done | bytes 131104 | tf_op jit(solution)/shard_map/ppermute | solution.py:19
  56.7 2.6 %collective-permute-done.17 = f32[32,1024]{1,0:T(8,128)S(1)} collective-permute-done((f32[32,1024]{1,0:T(8,128)S(1)}, f32[32,1024]{1,0:T(8,128)S(1)}, u32[]{:S(2)}, u32[]{:S(2)}) %collective-permute-start.17) | collective-permute-done | bytes 131104 | tf_op jit(solution)/shard_map/ppermute | solution.py:19
  59.4 2.2 %collective-permute-done.16.refs_1_ = f32[32,1024]{1,0:T(8,128)S(1)} collective-permute-done((f32[32,1024]{1,0:T(8,128)S(1)}, f32[32,1024]{1,0:T(8,128)S(1)}, u32[]{:S(2)}, u32[]{:S(2)}) %collective-permute-start.16) | collective-permute-done | bytes 131104 | tf_op jit(solution)/shard_map/ppermute | solution.py:19
  62.4 1.6 %collective-permute-start.22 = (f32[128,384]{1,0:T(8,128)S(1)}, f32[128,384]{1,0:T(8,128)S(1)}, u32[]{:S(2)}, u32[]{:S(2)}) collective-permute-start(f32[128,384]{1,0:T(8,128)S(1)} %maximum_multiply_fusion), channel_id=1, source_target_pairs={{0,16},{16,0},{1,17},{17,1},{2,18},{18,2},{3,19},{19,3},{4,20},{20... | collective-permute-start | bytes 589832 | tf_op jit(solution)/shard_map/ppermute | solution.py:19
  67.7 3.5 %collective-permute-done.19 = f32[64,384]{1,0:T(8,128)S(1)} collective-permute-done((f32[64,384]{1,0:T(8,128)S(1)}, f32[64,384]{1,0:T(8,128)S(1)}, u32[]{:S(2)}, u32[]{:S(2)}) %collective-permute-start.19) | collective-permute-done | bytes 98336 | tf_op jit(solution)/shard_map/ppermute | solution.py:19
  71.3 1.5 %collective-permute-done.24 = f32[64,384]{1,0:T(8,128)S(1)} collective-permute-done((f32[64,384]{1,0:T(8,128)S(1)}, f32[64,384]{1,0:T(8,128)S(1)}, u32[]{:S(2)}, u32[]{:S(2)}) %collective-permute-start.24) | collective-permute-done | bytes 98336 | tf_op jit(solution)/shard_map/ppermute | solution.py:19
  73.0 1.3 %collective-permute-done.25.refs_3_ = f32[64,384]{1,0:T(8,128)S(1)} collective-permute-done((f32[64,384]{1,0:T(8,128)S(1)}, f32[64,384]{1,0:T(8,128)S(1)}, u32[]{:S(2)}, u32[]{:S(2)}) %collective-permute-start.25) | collective-permute-done | bytes 98336 | tf_op jit(solution)/shard_map/ppermute | solution.py:19
  (70 shorter events, 15.1 us)
Async XLA Ops:
  3.6 7.4 %collective-permute-start = (f32[32,1024]{1,0:T(8,128)S(1)}, f32[32,1024]{1,0:T(8,128)S(1)}, u32[]{:S(2)}, u32[]{:S(2)}) collective-permute-start(f32[32,1024]{1,0:T(8,128)S(1)} %get-tuple-element.77), channel_id=1, source_target_pairs={{0,1},{1,0},{2,3},{3,2},{4,5},{5,4},{6,7},{7,6},{8,9},{9,8},{10,11... | collective-permute-start | bytes 393224 | tf_op jit(solution)/shard_map/ppermute | solution.py:19
  6.7 7.5 %collective-permute-start.2 = (f32[32,1024]{1,0:T(8,128)S(1)}, f32[32,1024]{1,0:T(8,128)S(1)}, u32[]{:S(2)}, u32[]{:S(2)}) collective-permute-start(f32[32,1024]{1,0:T(8,128)S(1)} %get-tuple-element.80), channel_id=1, source_target_pairs={{0,1},{1,0},{2,3},{3,2},{4,5},{5,4},{6,7},{7,6},{8,9},{9,8},{10,11... | collective-permute-start | bytes 393224 | tf_op jit(solution)/shard_map/ppermute | solution.py:19
  11.1 12.2 %collective-permute-start.1 = (f32[32,1024]{1,0:T(8,128)S(1)}, f32[32,1024]{1,0:T(8,128)S(1)}, u32[]{:S(2)}, u32[]{:S(2)}) collective-permute-start(f32[32,1024]{1,0:T(8,128)S(1)} %pad_maximum_fusion), channel_id=1, source_target_pairs={{0,2},{1,3},{2,0},{3,1},{4,6},{5,7},{6,4},{7,5},{8,10},{9,11},{10,... | collective-permute-start | bytes 393224 | tf_op jit(solution)/shard_map/ppermute | solution.py:19
  14.3 10.5 %collective-permute-start.4 = (f32[32,1024]{1,0:T(8,128)S(1)}, f32[32,1024]{1,0:T(8,128)S(1)}, u32[]{:S(2)}, u32[]{:S(2)}) collective-permute-start(f32[32,1024]{1,0:T(8,128)S(1)} %pad_maximum_fusion.1), channel_id=1, source_target_pairs={{0,2},{1,3},{2,0},{3,1},{4,6},{5,7},{6,4},{7,5},{8,10},{9,11},{10,... | collective-permute-start | bytes 393224 | tf_op jit(solution)/shard_map/ppermute | solution.py:19
  17.0 16.0 %collective-permute-start.9 = (f32[136,384]{1,0:T(8,128)S(1)}, f32[136,384]{1,0:T(8,128)S(1)}, u32[]{:S(2)}, u32[]{:S(2)}) collective-permute-start(f32[136,384]{1,0:T(8,128)S(1)} %get-tuple-element.83), channel_id=1, source_target_pairs={{0,16},{16,0},{1,17},{17,1},{2,18},{18,2},{3,19},{19,3},{4,20},{20... | collective-permute-start | bytes 626696 | tf_op jit(solution)/shard_map/ppermute | solution.py:19
  23.3 5.7 %collective-permute-start.3 = (f32[32,1024]{1,0:T(8,128)S(1)}, f32[32,1024]{1,0:T(8,128)S(1)}, u32[]{:S(2)}, u32[]{:S(2)}) collective-permute-start(f32[32,1024]{1,0:T(8,128)S(1)} %add_multiply_fusion.3.refs_0_), channel_id=1, source_target_pairs={{0,1},{1,0},{2,3},{3,2},{4,5},{5,4},{6,7},{7,6},{8,9},{9,8},{10,11... | collective-permute-start | bytes 393224 | tf_op jit(solution)/shard_map/ppermute | solution.py:19
  24.7 7.5 %collective-permute-start.7 = (f32[32,1024]{1,0:T(8,128)S(1)}, f32[32,1024]{1,0:T(8,128)S(1)}, u32[]{:S(2)}, u32[]{:S(2)}) collective-permute-start(f32[32,1024]{1,0:T(8,128)S(1)} %add_multiply_fusion.2.refs_0_), channel_id=1, source_target_pairs={{0,1},{1,0},{2,3},{3,2},{4,5},{5,4},{6,7},{7,6},{8,9},{9,8},{10,11... | collective-permute-start | bytes 393224 | tf_op jit(solution)/shard_map/ppermute | solution.py:19
  29.6 1.4 %collective-permute-start.5 = (f32[64,384]{1,0:T(8,128)S(1)}, f32[64,384]{1,0:T(8,128)S(1)}, u32[]{:S(2)}, u32[]{:S(2)}) collective-permute-start(f32[64,384]{1,0:T(8,128)S(1)} %get-tuple-element.93), channel_id=1, source_target_pairs={{0,4},{4,0},{8,12},{12,8},{1,5},{5,1},{9,13},{13,9},{2,6},{6,2},{1... | collective-permute-start | bytes 294920 | tf_op jit(solution)/shard_map/ppermute | solution.py:19
  31.0 5.1 %collective-permute-start.6 = (f32[64,384]{1,0:T(8,128)S(1)}, f32[64,384]{1,0:T(8,128)S(1)}, u32[]{:S(2)}, u32[]{:S(2)}) collective-permute-start(f32[64,384]{1,0:T(8,128)S(1)} %add.76), channel_id=1, source_target_pairs={{0,8},{4,12},{8,0},{12,4},{1,9},{5,13},{9,1},{13,5},{2,10},{6,14},... | collective-permute-start | bytes 294920 | tf_op jit(solution)/shard_map/ppermute | solution.py:19
  32.9 1.4 %collective-permute-start.8 = (f32[64,384]{1,0:T(8,128)S(1)}, f32[64,384]{1,0:T(8,128)S(1)}, u32[]{:S(2)}, u32[]{:S(2)}) collective-permute-start(f32[64,384]{1,0:T(8,128)S(1)} %get-tuple-element.99), channel_id=1, source_target_pairs={{0,4},{4,0},{8,12},{12,8},{1,5},{5,1},{9,13},{13,9},{2,6},{6,2},{1... | collective-permute-start | bytes 294920 | tf_op jit(solution)/shard_map/ppermute | solution.py:19
  34.3 4.9 %collective-permute-start.11 = (f32[64,384]{1,0:T(8,128)S(1)}, f32[64,384]{1,0:T(8,128)S(1)}, u32[]{:S(2)}, u32[]{:S(2)}) collective-permute-start(f32[64,384]{1,0:T(8,128)S(1)} %add.77), channel_id=1, source_target_pairs={{0,8},{4,12},{8,0},{12,4},{1,9},{5,13},{9,1},{13,5},{2,10},{6,14},... | collective-permute-start | bytes 294920 | tf_op jit(solution)/shard_map/ppermute | solution.py:19
  36.1 3.1 %collective-permute-start.10 = (f32[64,384]{1,0:T(8,128)S(1)}, f32[64,384]{1,0:T(8,128)S(1)}, u32[]{:S(2)}, u32[]{:S(2)}) collective-permute-start(f32[64,384]{1,0:T(8,128)S(1)} %fusion.11.own.refs_0_), channel_id=1, source_target_pairs={{0,4},{4,0},{8,12},{12,8},{1,5},{5,1},{9,13},{13,9},{2,6},{6,2},{1... | collective-permute-start | bytes 294920 | tf_op jit(solution)/shard_map/ppermute | solution.py:19
  39.9 5.0 %collective-permute-start.13 = (f32[32,1024]{1,0:T(8,128)S(1)}, f32[32,1024]{1,0:T(8,128)S(1)}, u32[]{:S(2)}, u32[]{:S(2)}) collective-permute-start(f32[32,1024]{1,0:T(8,128)S(1)} %get-tuple-element.113), channel_id=1, source_target_pairs={{0,1},{1,0},{2,3},{3,2},{4,5},{5,4},{6,7},{7,6},{8,9},{9,8},{10,11... | collective-permute-start | bytes 393224 | tf_op jit(solution)/shard_map/ppermute | solution.py:19
  42.3 7.0 %collective-permute-start.15 = (f32[32,1024]{1,0:T(8,128)S(1)}, f32[32,1024]{1,0:T(8,128)S(1)}, u32[]{:S(2)}, u32[]{:S(2)}) collective-permute-start(f32[32,1024]{1,0:T(8,128)S(1)} %get-tuple-element.123), channel_id=1, source_target_pairs={{0,1},{1,0},{2,3},{3,2},{4,5},{5,4},{6,7},{7,6},{8,9},{9,8},{10,11... | collective-permute-start | bytes 393224 | tf_op jit(solution)/shard_map/ppermute | solution.py:19
  45.0 11.6 %collective-permute-start.14 = (f32[32,1024]{1,0:T(8,128)S(1)}, f32[32,1024]{1,0:T(8,128)S(1)}, u32[]{:S(2)}, u32[]{:S(2)}) collective-permute-start(f32[32,1024]{1,0:T(8,128)S(1)} %pad_maximum_fusion.2), channel_id=1, source_target_pairs={{0,2},{1,3},{2,0},{3,1},{4,6},{5,7},{6,4},{7,5},{8,10},{9,11},{10,... | collective-permute-start | bytes 393224 | tf_op jit(solution)/shard_map/ppermute | solution.py:19
  49.3 10.0 %collective-permute-start.17 = (f32[32,1024]{1,0:T(8,128)S(1)}, f32[32,1024]{1,0:T(8,128)S(1)}, u32[]{:S(2)}, u32[]{:S(2)}) collective-permute-start(f32[32,1024]{1,0:T(8,128)S(1)} %pad_maximum_fusion.3), channel_id=1, source_target_pairs={{0,2},{1,3},{2,0},{3,1},{4,6},{5,7},{6,4},{7,5},{8,10},{9,11},{10,... | collective-permute-start | bytes 393224 | tf_op jit(solution)/shard_map/ppermute | solution.py:19
  56.6 5.0 %collective-permute-start.16 = (f32[32,1024]{1,0:T(8,128)S(1)}, f32[32,1024]{1,0:T(8,128)S(1)}, u32[]{:S(2)}, u32[]{:S(2)}) collective-permute-start(f32[32,1024]{1,0:T(8,128)S(1)} %add_multiply_fusion.1.refs_0_), channel_id=1, source_target_pairs={{0,1},{1,0},{2,3},{3,2},{4,5},{5,4},{6,7},{7,6},{8,9},{9,8},{10,11... | collective-permute-start | bytes 393224 | tf_op jit(solution)/shard_map/ppermute | solution.py:19
  59.4 5.5 %collective-permute-start.20 = (f32[32,1024]{1,0:T(8,128)S(1)}, f32[32,1024]{1,0:T(8,128)S(1)}, u32[]{:S(2)}, u32[]{:S(2)}) collective-permute-start(f32[32,1024]{1,0:T(8,128)S(1)} %add_multiply_fusion.refs_0_), channel_id=1, source_target_pairs={{0,1},{1,0},{2,3},{3,2},{4,5},{5,4},{6,7},{7,6},{8,9},{9,8},{10,11... | collective-permute-start | bytes 393224 | tf_op jit(solution)/shard_map/ppermute | solution.py:19
  62.3 1.7 %collective-permute-start.18 = (f32[64,384]{1,0:T(8,128)S(1)}, f32[64,384]{1,0:T(8,128)S(1)}, u32[]{:S(2)}, u32[]{:S(2)}) collective-permute-start(f32[64,384]{1,0:T(8,128)S(1)} %get-tuple-element.135), channel_id=1, source_target_pairs={{0,4},{4,0},{8,12},{12,8},{1,5},{5,1},{9,13},{13,9},{2,6},{6,2},{1... | collective-permute-start | bytes 294920 | tf_op jit(solution)/shard_map/ppermute | solution.py:19
  62.4 8.8 %collective-permute-start.22 = (f32[128,384]{1,0:T(8,128)S(1)}, f32[128,384]{1,0:T(8,128)S(1)}, u32[]{:S(2)}, u32[]{:S(2)}) collective-permute-start(f32[128,384]{1,0:T(8,128)S(1)} %maximum_multiply_fusion), channel_id=1, source_target_pairs={{0,16},{16,0},{1,17},{17,1},{2,18},{18,2},{3,19},{19,3},{4,20},{20... | collective-permute-start | bytes 589832 | tf_op jit(solution)/shard_map/ppermute | solution.py:19
  65.5 1.4 %collective-permute-start.21 = (f32[64,384]{1,0:T(8,128)S(1)}, f32[64,384]{1,0:T(8,128)S(1)}, u32[]{:S(2)}, u32[]{:S(2)}) collective-permute-start(f32[64,384]{1,0:T(8,128)S(1)} %get-tuple-element.141), channel_id=1, source_target_pairs={{0,4},{4,0},{8,12},{12,8},{1,5},{5,1},{9,13},{13,9},{2,6},{6,2},{1... | collective-permute-start | bytes 294920 | tf_op jit(solution)/shard_map/ppermute | solution.py:19
  65.5 5.7 %collective-permute-start.19 = (f32[64,384]{1,0:T(8,128)S(1)}, f32[64,384]{1,0:T(8,128)S(1)}, u32[]{:S(2)}, u32[]{:S(2)}) collective-permute-start(f32[64,384]{1,0:T(8,128)S(1)} %add.88), channel_id=1, source_target_pairs={{0,8},{4,12},{8,0},{12,4},{1,9},{5,13},{9,1},{13,5},{2,10},{6,14},... | collective-permute-start | bytes 294920 | tf_op jit(solution)/shard_map/ppermute | solution.py:19
  66.8 6.0 %collective-permute-start.24 = (f32[64,384]{1,0:T(8,128)S(1)}, f32[64,384]{1,0:T(8,128)S(1)}, u32[]{:S(2)}, u32[]{:S(2)}) collective-permute-start(f32[64,384]{1,0:T(8,128)S(1)} %add.89), channel_id=1, source_target_pairs={{0,8},{4,12},{8,0},{12,4},{1,9},{5,13},{9,1},{13,5},{2,10},{6,14},... | collective-permute-start | bytes 294920 | tf_op jit(solution)/shard_map/ppermute | solution.py:19
  71.2 1.7 %collective-permute-start.23 = (f32[64,384]{1,0:T(8,128)S(1)}, f32[64,384]{1,0:T(8,128)S(1)}, u32[]{:S(2)}, u32[]{:S(2)}) collective-permute-start(f32[64,384]{1,0:T(8,128)S(1)} %fusion.5.refs_0_), channel_id=1, source_target_pairs={{0,4},{4,0},{8,12},{12,8},{1,5},{5,1},{9,13},{13,9},{2,6},{6,2},{1... | collective-permute-start | bytes 294920 | tf_op jit(solution)/shard_map/ppermute | solution.py:19
  (4 other events, 9.5 us)

commit v5 on v4

--- a/solution.py
+++ b/solution.py
@@ -205,18 +205,36 @@
     return call(kernel, [shape, shape], [*blocks, high, low], 6 * rows * high.size)
 
 
-def forward(own, other, mask, high_t, low_t):
-    def kernel(own, other, mask, high_t, low_t, keep, send):
-        masked = jnp.concatenate(sides(own[...], other[...]), axis=1) * mask[...]
-        out = product(masked, high_t[...], low_t[...], NN)
+def half_of(ref, mine, axis):
+    half = ref.shape[axis] // 2
+    side = lax.axis_index("dp") % 2
+    side = side if mine else 1 - side
+    spot = pl.ds(pl.multiple_of(side * half, half), half)
+    return ref[:, spot] if axis else ref[spot, :]
+
+
+def forward_own(own, mask, high_t, low_t):
+    def kernel(own, mask, high_t, low_t, out):
+        masked = own[...] * half_of(mask, True, 1)
+        out[...] = product(masked, half_of(high_t, True, 0), half_of(low_t, True, 0), NN)
+
+    shape = jax.ShapeDtypeStruct((own.shape[0], high_t.shape[1]), jnp.float32)
+    return call(kernel, [shape], [own, mask, high_t, low_t], 3 * own.shape[0] * high_t.size)[0]
+
+
+def forward(partial, other, mask, high_t, low_t):
+    def kernel(partial, other, mask, high_t, low_t, keep, send):
+        masked = other[...] * half_of(mask, False, 1)
+        out = product(masked, half_of(high_t, False, 0), half_of(low_t, False, 0), NN)
+        out = partial[...] + out
         size = out.shape[0] // 2
         keep[...] = out[:size]
         send[...] = out[size:]
 
-    rows = own.shape[0]
+    rows = other.shape[0]
     shape = jax.ShapeDtypeStruct((rows // 2, high_t.shape[1]), jnp.float32)
-    operands = [own, other, mask, high_t, low_t]
-    return call(kernel, [shape, shape], operands, 6 * rows * high_t.size)
+    operands = [partial, other, mask, high_t, low_t]
+    return call(kernel, [shape, shape], operands, 3 * rows * high_t.size)
 
 
 def finish(halves):
@@ -364,7 +382,8 @@
         def smooth_second():
             return smoothing(*[part(value, chunk) for value in shared["second"]])
 
-        sent = yield (lambda a, b: forward(a, b, shared["mask"], *shared["turned"])), *image
+        partial = forward_own(image[0], shared["mask"], *shared["turned"])
+        sent = yield (lambda *v: forward(*v, shared["mask"], *shared["turned"])), partial, image[1]
         return (yield from hessian(*sent, smooth_second))
 
     def between():

time: 75.4 us -> 75 us (level)
  waiting for transfers between devices: 39.6 us -> 37.9 us
  starting transfers between devices: 24.8 us -> 25.6 us
    ppermute x26, waiting for transfers between devices: 39.6 us -> 37.9 us  [swap(): lax.ppermute(value, axis, [(i, i ^ stride) for i in range(lax.axis_size(a...]
    ppermute x26, starting transfers between devices: 24.8 us -> 25.6 us  [swap(): lax.ppermute(value, axis, [(i, i ^ stride) for i in range(lax.axis_size(a...]
    pallas_call x7 -> x9, Pallas kernels: 4.59 us -> 5.01 us  [call(): pl.pallas_call(kernel, out_shape=shapes, in_specs=[VMEM] * len(operands),...]
where the time goes in v5:
time: 75 us; the launch traced here: 74.8 us
  waiting for transfers between devices  37.9 us (51%)
  starting transfers between devices  25.6 us (34%)
  Pallas kernels  9.84 us (13%)
  between operations  0.97 us (1%)
    ppermute x26, waiting for transfers between devices, swap(): lax.ppermute(value, axis, [(i, i ^ stride) for i in range(lax.axis_size(a...  37.9 us
    ppermute x26, starting transfers between devices, swap(): lax.ppermute(value, axis, [(i, i ^ stride) for i in range(lax.axis_size(a...  25.6 us
    pallas_call x9, Pallas kernels, call(): pl.pallas_call(kernel, out_shape=shapes, in_specs=[VMEM] * len(operands),...  5.01 us
    pallas_call x1, Pallas kernels, first_forward(): pl.pallas_call(kernel, in_specs=[pl.BlockSpec(memory_space=pltpu.HBM)] *...  2.95 us
    pallas_call x2, Pallas kernels, finish(): pl.pallas_call(kernel, out_shape=shape, in_specs=[VMEM] * (2 * chunks), o...  1.88 us
  transfers between devices with their start and end apart: 26, of which 18 were waited for; matrix products, arithmetic and copies ran while one was open for 1% of the time, Pallas kernels for 7%

profile of v5, /device:TPU:0, one launch (start us, length us, event | category | flops | bytes accessed | tf_op | source)
XLA Modules:
  0.0 74.8 jit_solution(13009705597785370197)
XLA Ops:
  0.6 2.9 %shard_map.68 = (bf16[1024,768]{1,0:T(8,128)(2,1)S(1)}, bf16[1024,768]{1,0:T(8,128)(2,1)S(1)}, f32[136,384]{1,0:T(8,128)S(1)}, f32[8,384]{1,0:T(8,128)S(1)}, f32...) custom-call(f32[768,128]{1,0:T(8,128)} %bitcast.8, ...), custom_call_target="tpu_custom_call" | custom-call | flops 603979776 | bytes 3145728 | tf_op jit(solution)/shard_map/pallas_call | solution.py:167
  3.6 3.1 %collective-permute-start = (f32[32,1024]{1,0:T(8,128)S(1)}, f32[32,1024]{1,0:T(8,128)S(1)}, u32[]{:S(2)}, u32[]{:S(2)}) collective-permute-start(f32[32,1024]{1,0:T(8,128)S(1)} %get-tuple-element.77), channel_id=1, source_target_pairs={{0,1},{1,0},{2,3},{3,2},{4,5},{5,4},{6,7},{7,6},{8,9},{9,8},{10,11... | collective-permute-start | bytes 393224 | tf_op jit(solution)/shard_map/ppermute | solution.py:19
  6.8 4.2 %collective-permute-done = f32[32,1024]{1,0:T(8,128)S(1)} collective-permute-done((f32[32,1024]{1,0:T(8,128)S(1)}, f32[32,1024]{1,0:T(8,128)S(1)}, u32[]{:S(2)}, u32[]{:S(2)}) %collective-permute-start) | collective-permute-done | bytes 131104 | tf_op jit(solution)/shard_map/ppermute | solution.py:19
  11.1 3.1 %collective-permute-start.1 = (f32[32,1024]{1,0:T(8,128)S(1)}, f32[32,1024]{1,0:T(8,128)S(1)}, u32[]{:S(2)}, u32[]{:S(2)}) collective-permute-start(f32[32,1024]{1,0:T(8,128)S(1)} %pad_maximum_fusion), channel_id=1, source_target_pairs={{0,2},{1,3},{2,0},{3,1},{4,6},{5,7},{6,4},{7,5},{8,10},{9,11},{10,... | collective-permute-start | bytes 393224 | tf_op jit(solution)/shard_map/ppermute | solution.py:19
  14.3 2.7 %collective-permute-start.4 = (f32[32,1024]{1,0:T(8,128)S(1)}, f32[32,1024]{1,0:T(8,128)S(1)}, u32[]{:S(2)}, u32[]{:S(2)}) collective-permute-start(f32[32,1024]{1,0:T(8,128)S(1)} %pad_maximum_fusion.1), channel_id=1, source_target_pairs={{0,2},{1,3},{2,0},{3,1},{4,6},{5,7},{6,4},{7,5},{8,10},{9,11},{10,... | collective-permute-start | bytes 393224 | tf_op jit(solution)/shard_map/ppermute | solution.py:19
  17.0 1.5 %collective-permute-start.9 = (f32[136,384]{1,0:T(8,128)S(1)}, f32[136,384]{1,0:T(8,128)S(1)}, u32[]{:S(2)}, u32[]{:S(2)}) collective-permute-start(f32[136,384]{1,0:T(8,128)S(1)} %get-tuple-element.83), channel_id=1, source_target_pairs={{0,16},{16,0},{1,17},{17,1},{2,18},{18,2},{3,19},{19,3},{4,20},{20... | collective-permute-start | bytes 626696 | tf_op jit(solution)/shard_map/ppermute | solution.py:19
  18.5 4.7 %collective-permute-done.1 = f32[32,1024]{1,0:T(8,128)S(1)} collective-permute-done((f32[32,1024]{1,0:T(8,128)S(1)}, f32[32,1024]{1,0:T(8,128)S(1)}, u32[]{:S(2)}, u32[]{:S(2)}) %collective-permute-start.1) | collective-permute-done | bytes 131104 | tf_op jit(solution)/shard_map/ppermute | solution.py:19
  25.5 3.5 %collective-permute-done.3.refs_1_ = f32[32,1024]{1,0:T(8,128)S(1)} collective-permute-done((f32[32,1024]{1,0:T(8,128)S(1)}, f32[32,1024]{1,0:T(8,128)S(1)}, u32[]{:S(2)}, u32[]{:S(2)}) %collective-permute-start.3) | collective-permute-done | bytes 131104 | tf_op jit(solution)/shard_map/ppermute | solution.py:19
  29.7 1.3 %collective-permute-done.5 = f32[64,384]{1,0:T(8,128)S(1)} collective-permute-done((f32[64,384]{1,0:T(8,128)S(1)}, f32[64,384]{1,0:T(8,128)S(1)}, u32[]{:S(2)}, u32[]{:S(2)}) %collective-permute-start.5) | collective-permute-done | bytes 98336 | tf_op jit(solution)/shard_map/ppermute | solution.py:19
  31.0 1.3 %collective-permute-start.6 = (f32[64,384]{1,0:T(8,128)S(1)}, f32[64,384]{1,0:T(8,128)S(1)}, u32[]{:S(2)}, u32[]{:S(2)}) collective-permute-start(f32[64,384]{1,0:T(8,128)S(1)} %add.76), channel_id=1, source_target_pairs={{0,8},{4,12},{8,0},{12,4},{1,9},{5,13},{9,1},{13,5},{2,10},{6,14},... | collective-permute-start | bytes 294920 | tf_op jit(solution)/shard_map/ppermute | solution.py:19
  33.0 1.3 %collective-permute-done.8 = f32[64,384]{1,0:T(8,128)S(1)} collective-permute-done((f32[64,384]{1,0:T(8,128)S(1)}, f32[64,384]{1,0:T(8,128)S(1)}, u32[]{:S(2)}, u32[]{:S(2)}) %collective-permute-start.8) | collective-permute-done | bytes 98336 | tf_op jit(solution)/shard_map/ppermute | solution.py:19
  36.6 2.6 %collective-permute-done.11 = f32[64,384]{1,0:T(8,128)S(1)} collective-permute-done((f32[64,384]{1,0:T(8,128)S(1)}, f32[64,384]{1,0:T(8,128)S(1)}, u32[]{:S(2)}, u32[]{:S(2)}) %collective-permute-start.11) | collective-permute-done | bytes 98336 | tf_op jit(solution)/shard_map/ppermute | solution.py:19
  41.9 1.7 %collective-permute-start.15 = (f32[32,1024]{1,0:T(8,128)S(1)}, f32[32,1024]{1,0:T(8,128)S(1)}, u32[]{:S(2)}, u32[]{:S(2)}) collective-permute-start(f32[32,1024]{1,0:T(8,128)S(1)} %get-tuple-element.123), channel_id=1, source_target_pairs={{0,1},{1,0},{2,3},{3,2},{4,5},{5,4},{6,7},{7,6},{8,9},{9,8},{10,11... | collective-permute-start | bytes 393224 | tf_op jit(solution)/shard_map/ppermute | solution.py:19
  44.8 2.1 %collective-permute-start.14 = (f32[32,1024]{1,0:T(8,128)S(1)}, f32[32,1024]{1,0:T(8,128)S(1)}, u32[]{:S(2)}, u32[]{:S(2)}) collective-permute-start(f32[32,1024]{1,0:T(8,128)S(1)} %pad_maximum_fusion.2), channel_id=1, source_target_pairs={{0,2},{1,3},{2,0},{3,1},{4,6},{5,7},{6,4},{7,5},{8,10},{9,11},{10,... | collective-permute-start | bytes 393224 | tf_op jit(solution)/shard_map/ppermute | solution.py:19
  49.0 2.8 %collective-permute-start.17 = (f32[32,1024]{1,0:T(8,128)S(1)}, f32[32,1024]{1,0:T(8,128)S(1)}, u32[]{:S(2)}, u32[]{:S(2)}) collective-permute-start(f32[32,1024]{1,0:T(8,128)S(1)} %pad_maximum_fusion.3), channel_id=1, source_target_pairs={{0,2},{1,3},{2,0},{3,1},{4,6},{5,7},{6,4},{7,5},{8,10},{9,11},{10,... | collective-permute-start | bytes 393224 | tf_op jit(solution)/shard_map/ppermute | solution.py:19
  51.8 4.8 %collective-permute-done.14 = f32[32,1024]{1,0:T(8,128)S(1)} collective-permute-done((f32[32,1024]{1,0:T(8,128)S(1)}, f32[32,1024]{1,0:T(8,128)S(1)}, u32[]{:S(2)}, u32[]{:S(2)}) %collective-permute-start.14) | collective-permute-done | bytes 131104 | tf_op jit(solution)/shard_map/ppermute | solution.py:19
  56.7 2.4 %collective-permute-done.17 = f32[32,1024]{1,0:T(8,128)S(1)} collective-permute-done((f32[32,1024]{1,0:T(8,128)S(1)}, f32[32,1024]{1,0:T(8,128)S(1)}, u32[]{:S(2)}, u32[]{:S(2)}) %collective-permute-start.17) | collective-permute-done | bytes 131104 | tf_op jit(solution)/shard_map/ppermute | solution.py:19
  59.2 2.4 %collective-permute-done.16.refs_1_ = f32[32,1024]{1,0:T(8,128)S(1)} collective-permute-done((f32[32,1024]{1,0:T(8,128)S(1)}, f32[32,1024]{1,0:T(8,128)S(1)}, u32[]{:S(2)}, u32[]{:S(2)}) %collective-permute-start.16) | collective-permute-done | bytes 131104 | tf_op jit(solution)/shard_map/ppermute | solution.py:19
  62.4 1.8 %collective-permute-start.22 = (f32[128,384]{1,0:T(8,128)S(1)}, f32[128,384]{1,0:T(8,128)S(1)}, u32[]{:S(2)}, u32[]{:S(2)}) collective-permute-start(f32[128,384]{1,0:T(8,128)S(1)} %maximum_multiply_fusion), channel_id=1, source_target_pairs={{0,16},{16,0},{1,17},{17,1},{2,18},{18,2},{3,19},{19,3},{4,20},{20... | collective-permute-start | bytes 589832 | tf_op jit(solution)/shard_map/ppermute | solution.py:19
  65.2 1.2 %collective-permute-start.19 = (f32[64,384]{1,0:T(8,128)S(1)}, f32[64,384]{1,0:T(8,128)S(1)}, u32[]{:S(2)}, u32[]{:S(2)}) collective-permute-start(f32[64,384]{1,0:T(8,128)S(1)} %add.88), channel_id=1, source_target_pairs={{0,8},{4,12},{8,0},{12,4},{1,9},{5,13},{9,1},{13,5},{2,10},{6,14},... | collective-permute-start | bytes 294920 | tf_op jit(solution)/shard_map/ppermute | solution.py:19
  66.5 1.2 %collective-permute-start.24 = (f32[64,384]{1,0:T(8,128)S(1)}, f32[64,384]{1,0:T(8,128)S(1)}, u32[]{:S(2)}, u32[]{:S(2)}) collective-permute-start(f32[64,384]{1,0:T(8,128)S(1)} %add.89), channel_id=1, source_target_pairs={{0,8},{4,12},{8,0},{12,4},{1,9},{5,13},{9,1},{13,5},{2,10},{6,14},... | collective-permute-start | bytes 294920 | tf_op jit(solution)/shard_map/ppermute | solution.py:19
  67.7 3.2 %collective-permute-done.19 = f32[64,384]{1,0:T(8,128)S(1)} collective-permute-done((f32[64,384]{1,0:T(8,128)S(1)}, f32[64,384]{1,0:T(8,128)S(1)}, u32[]{:S(2)}, u32[]{:S(2)}) %collective-permute-start.19) | collective-permute-done | bytes 98336 | tf_op jit(solution)/shard_map/ppermute | solution.py:19
  70.9 1.5 %collective-permute-done.24 = f32[64,384]{1,0:T(8,128)S(1)} collective-permute-done((f32[64,384]{1,0:T(8,128)S(1)}, f32[64,384]{1,0:T(8,128)S(1)}, u32[]{:S(2)}, u32[]{:S(2)}) %collective-permute-start.24) | collective-permute-done | bytes 98336 | tf_op jit(solution)/shard_map/ppermute | solution.py:19
  72.6 1.3 %collective-permute-done.25.refs_3_ = f32[64,384]{1,0:T(8,128)S(1)} collective-permute-done((f32[64,384]{1,0:T(8,128)S(1)}, f32[64,384]{1,0:T(8,128)S(1)}, u32[]{:S(2)}, u32[]{:S(2)}) %collective-permute-start.25) | collective-permute-done | bytes 98336 | tf_op jit(solution)/shard_map/ppermute | solution.py:19
  (72 shorter events, 15.2 us)
Async XLA Ops:
  3.6 7.4 %collective-permute-start = (f32[32,1024]{1,0:T(8,128)S(1)}, f32[32,1024]{1,0:T(8,128)S(1)}, u32[]{:S(2)}, u32[]{:S(2)}) collective-permute-start(f32[32,1024]{1,0:T(8,128)S(1)} %get-tuple-element.77), channel_id=1, source_target_pairs={{0,1},{1,0},{2,3},{3,2},{4,5},{5,4},{6,7},{7,6},{8,9},{9,8},{10,11... | collective-permute-start | bytes 393224 | tf_op jit(solution)/shard_map/ppermute | solution.py:19
  6.7 7.5 %collective-permute-start.2 = (f32[32,1024]{1,0:T(8,128)S(1)}, f32[32,1024]{1,0:T(8,128)S(1)}, u32[]{:S(2)}, u32[]{:S(2)}) collective-permute-start(f32[32,1024]{1,0:T(8,128)S(1)} %get-tuple-element.80), channel_id=1, source_target_pairs={{0,1},{1,0},{2,3},{3,2},{4,5},{5,4},{6,7},{7,6},{8,9},{9,8},{10,11... | collective-permute-start | bytes 393224 | tf_op jit(solution)/shard_map/ppermute | solution.py:19
  11.1 12.2 %collective-permute-start.1 = (f32[32,1024]{1,0:T(8,128)S(1)}, f32[32,1024]{1,0:T(8,128)S(1)}, u32[]{:S(2)}, u32[]{:S(2)}) collective-permute-start(f32[32,1024]{1,0:T(8,128)S(1)} %pad_maximum_fusion), channel_id=1, source_target_pairs={{0,2},{1,3},{2,0},{3,1},{4,6},{5,7},{6,4},{7,5},{8,10},{9,11},{10,... | collective-permute-start | bytes 393224 | tf_op jit(solution)/shard_map/ppermute | solution.py:19
  14.3 10.5 %collective-permute-start.4 = (f32[32,1024]{1,0:T(8,128)S(1)}, f32[32,1024]{1,0:T(8,128)S(1)}, u32[]{:S(2)}, u32[]{:S(2)}) collective-permute-start(f32[32,1024]{1,0:T(8,128)S(1)} %pad_maximum_fusion.1), channel_id=1, source_target_pairs={{0,2},{1,3},{2,0},{3,1},{4,6},{5,7},{6,4},{7,5},{8,10},{9,11},{10,... | collective-permute-start | bytes 393224 | tf_op jit(solution)/shard_map/ppermute | solution.py:19
  17.0 16.0 %collective-permute-start.9 = (f32[136,384]{1,0:T(8,128)S(1)}, f32[136,384]{1,0:T(8,128)S(1)}, u32[]{:S(2)}, u32[]{:S(2)}) collective-permute-start(f32[136,384]{1,0:T(8,128)S(1)} %get-tuple-element.83), channel_id=1, source_target_pairs={{0,16},{16,0},{1,17},{17,1},{2,18},{18,2},{3,19},{19,3},{4,20},{20... | collective-permute-start | bytes 626696 | tf_op jit(solution)/shard_map/ppermute | solution.py:19
  23.3 5.7 %collective-permute-start.3 = (f32[32,1024]{1,0:T(8,128)S(1)}, f32[32,1024]{1,0:T(8,128)S(1)}, u32[]{:S(2)}, u32[]{:S(2)}) collective-permute-start(f32[32,1024]{1,0:T(8,128)S(1)} %add_multiply_fusion.3.refs_0_), channel_id=1, source_target_pairs={{0,1},{1,0},{2,3},{3,2},{4,5},{5,4},{6,7},{7,6},{8,9},{9,8},{10,11... | collective-permute-start | bytes 393224 | tf_op jit(solution)/shard_map/ppermute | solution.py:19
  24.7 7.5 %collective-permute-start.7 = (f32[32,1024]{1,0:T(8,128)S(1)}, f32[32,1024]{1,0:T(8,128)S(1)}, u32[]{:S(2)}, u32[]{:S(2)}) collective-permute-start(f32[32,1024]{1,0:T(8,128)S(1)} %add_multiply_fusion.2.refs_0_), channel_id=1, source_target_pairs={{0,1},{1,0},{2,3},{3,2},{4,5},{5,4},{6,7},{7,6},{8,9},{9,8},{10,11... | collective-permute-start | bytes 393224 | tf_op jit(solution)/shard_map/ppermute | solution.py:19
  29.6 1.4 %collective-permute-start.5 = (f32[64,384]{1,0:T(8,128)S(1)}, f32[64,384]{1,0:T(8,128)S(1)}, u32[]{:S(2)}, u32[]{:S(2)}) collective-permute-start(f32[64,384]{1,0:T(8,128)S(1)} %get-tuple-element.93), channel_id=1, source_target_pairs={{0,4},{4,0},{8,12},{12,8},{1,5},{5,1},{9,13},{13,9},{2,6},{6,2},{1... | collective-permute-start | bytes 294920 | tf_op jit(solution)/shard_map/ppermute | solution.py:19
  31.0 5.1 %collective-permute-start.6 = (f32[64,384]{1,0:T(8,128)S(1)}, f32[64,384]{1,0:T(8,128)S(1)}, u32[]{:S(2)}, u32[]{:S(2)}) collective-permute-start(f32[64,384]{1,0:T(8,128)S(1)} %add.76), channel_id=1, source_target_pairs={{0,8},{4,12},{8,0},{12,4},{1,9},{5,13},{9,1},{13,5},{2,10},{6,14},... | collective-permute-start | bytes 294920 | tf_op jit(solution)/shard_map/ppermute | solution.py:19
  32.9 1.4 %collective-permute-start.8 = (f32[64,384]{1,0:T(8,128)S(1)}, f32[64,384]{1,0:T(8,128)S(1)}, u32[]{:S(2)}, u32[]{:S(2)}) collective-permute-start(f32[64,384]{1,0:T(8,128)S(1)} %get-tuple-element.99), channel_id=1, source_target_pairs={{0,4},{4,0},{8,12},{12,8},{1,5},{5,1},{9,13},{13,9},{2,6},{6,2},{1... | collective-permute-start | bytes 294920 | tf_op jit(solution)/shard_map/ppermute | solution.py:19
  34.3 4.9 %collective-permute-start.11 = (f32[64,384]{1,0:T(8,128)S(1)}, f32[64,384]{1,0:T(8,128)S(1)}, u32[]{:S(2)}, u32[]{:S(2)}) collective-permute-start(f32[64,384]{1,0:T(8,128)S(1)} %add.77), channel_id=1, source_target_pairs={{0,8},{4,12},{8,0},{12,4},{1,9},{5,13},{9,1},{13,5},{2,10},{6,14},... | collective-permute-start | bytes 294920 | tf_op jit(solution)/shard_map/ppermute | solution.py:19
  36.1 3.1 %collective-permute-start.10 = (f32[64,384]{1,0:T(8,128)S(1)}, f32[64,384]{1,0:T(8,128)S(1)}, u32[]{:S(2)}, u32[]{:S(2)}) collective-permute-start(f32[64,384]{1,0:T(8,128)S(1)} %fusion.11.own.refs_0_), channel_id=1, source_target_pairs={{0,4},{4,0},{8,12},{12,8},{1,5},{5,1},{9,13},{13,9},{2,6},{6,2},{1... | collective-permute-start | bytes 294920 | tf_op jit(solution)/shard_map/ppermute | solution.py:19
  39.7 5.0 %collective-permute-start.13 = (f32[32,1024]{1,0:T(8,128)S(1)}, f32[32,1024]{1,0:T(8,128)S(1)}, u32[]{:S(2)}, u32[]{:S(2)}) collective-permute-start(f32[32,1024]{1,0:T(8,128)S(1)} %get-tuple-element.113), channel_id=1, source_target_pairs={{0,1},{1,0},{2,3},{3,2},{4,5},{5,4},{6,7},{7,6},{8,9},{9,8},{10,11... | collective-permute-start | bytes 393224 | tf_op jit(solution)/shard_map/ppermute | solution.py:19
  41.9 7.1 %collective-permute-start.15 = (f32[32,1024]{1,0:T(8,128)S(1)}, f32[32,1024]{1,0:T(8,128)S(1)}, u32[]{:S(2)}, u32[]{:S(2)}) collective-permute-start(f32[32,1024]{1,0:T(8,128)S(1)} %get-tuple-element.123), channel_id=1, source_target_pairs={{0,1},{1,0},{2,3},{3,2},{4,5},{5,4},{6,7},{7,6},{8,9},{9,8},{10,11... | collective-permute-start | bytes 393224 | tf_op jit(solution)/shard_map/ppermute | solution.py:19
  44.8 11.8 %collective-permute-start.14 = (f32[32,1024]{1,0:T(8,128)S(1)}, f32[32,1024]{1,0:T(8,128)S(1)}, u32[]{:S(2)}, u32[]{:S(2)}) collective-permute-start(f32[32,1024]{1,0:T(8,128)S(1)} %pad_maximum_fusion.2), channel_id=1, source_target_pairs={{0,2},{1,3},{2,0},{3,1},{4,6},{5,7},{6,4},{7,5},{8,10},{9,11},{10,... | collective-permute-start | bytes 393224 | tf_op jit(solution)/shard_map/ppermute | solution.py:19
  49.0 10.1 %collective-permute-start.17 = (f32[32,1024]{1,0:T(8,128)S(1)}, f32[32,1024]{1,0:T(8,128)S(1)}, u32[]{:S(2)}, u32[]{:S(2)}) collective-permute-start(f32[32,1024]{1,0:T(8,128)S(1)} %pad_maximum_fusion.3), channel_id=1, source_target_pairs={{0,2},{1,3},{2,0},{3,1},{4,6},{5,7},{6,4},{7,5},{8,10},{9,11},{10,... | collective-permute-start | bytes 393224 | tf_op jit(solution)/shard_map/ppermute | solution.py:19
  56.6 5.0 %collective-permute-start.16 = (f32[32,1024]{1,0:T(8,128)S(1)}, f32[32,1024]{1,0:T(8,128)S(1)}, u32[]{:S(2)}, u32[]{:S(2)}) collective-permute-start(f32[32,1024]{1,0:T(8,128)S(1)} %add_multiply_fusion.1.refs_0_), channel_id=1, source_target_pairs={{0,1},{1,0},{2,3},{3,2},{4,5},{5,4},{6,7},{7,6},{8,9},{9,8},{10,11... | collective-permute-start | bytes 393224 | tf_op jit(solution)/shard_map/ppermute | solution.py:19
  59.2 5.3 %collective-permute-start.20 = (f32[32,1024]{1,0:T(8,128)S(1)}, f32[32,1024]{1,0:T(8,128)S(1)}, u32[]{:S(2)}, u32[]{:S(2)}) collective-permute-start(f32[32,1024]{1,0:T(8,128)S(1)} %add_multiply_fusion.refs_0_), channel_id=1, source_target_pairs={{0,1},{1,0},{2,3},{3,2},{4,5},{5,4},{6,7},{7,6},{8,9},{9,8},{10,11... | collective-permute-start | bytes 393224 | tf_op jit(solution)/shard_map/ppermute | solution.py:19
  62.3 1.9 %collective-permute-start.18 = (f32[64,384]{1,0:T(8,128)S(1)}, f32[64,384]{1,0:T(8,128)S(1)}, u32[]{:S(2)}, u32[]{:S(2)}) collective-permute-start(f32[64,384]{1,0:T(8,128)S(1)} %get-tuple-element.135), channel_id=1, source_target_pairs={{0,4},{4,0},{8,12},{12,8},{1,5},{5,1},{9,13},{13,9},{2,6},{6,2},{1... | collective-permute-start | bytes 294920 | tf_op jit(solution)/shard_map/ppermute | solution.py:19
  62.4 8.5 %collective-permute-start.22 = (f32[128,384]{1,0:T(8,128)S(1)}, f32[128,384]{1,0:T(8,128)S(1)}, u32[]{:S(2)}, u32[]{:S(2)}) collective-permute-start(f32[128,384]{1,0:T(8,128)S(1)} %maximum_multiply_fusion), channel_id=1, source_target_pairs={{0,16},{16,0},{1,17},{17,1},{2,18},{18,2},{3,19},{19,3},{4,20},{20... | collective-permute-start | bytes 589832 | tf_op jit(solution)/shard_map/ppermute | solution.py:19
  65.1 1.4 %collective-permute-start.21 = (f32[64,384]{1,0:T(8,128)S(1)}, f32[64,384]{1,0:T(8,128)S(1)}, u32[]{:S(2)}, u32[]{:S(2)}) collective-permute-start(f32[64,384]{1,0:T(8,128)S(1)} %get-tuple-element.141), channel_id=1, source_target_pairs={{0,4},{4,0},{8,12},{12,8},{1,5},{5,1},{9,13},{13,9},{2,6},{6,2},{1... | collective-permute-start | bytes 294920 | tf_op jit(solution)/shard_map/ppermute | solution.py:19
  65.2 5.7 %collective-permute-start.19 = (f32[64,384]{1,0:T(8,128)S(1)}, f32[64,384]{1,0:T(8,128)S(1)}, u32[]{:S(2)}, u32[]{:S(2)}) collective-permute-start(f32[64,384]{1,0:T(8,128)S(1)} %add.88), channel_id=1, source_target_pairs={{0,8},{4,12},{8,0},{12,4},{1,9},{5,13},{9,1},{13,5},{2,10},{6,14},... | collective-permute-start | bytes 294920 | tf_op jit(solution)/shard_map/ppermute | solution.py:19
  66.5 6.0 %collective-permute-start.24 = (f32[64,384]{1,0:T(8,128)S(1)}, f32[64,384]{1,0:T(8,128)S(1)}, u32[]{:S(2)}, u32[]{:S(2)}) collective-permute-start(f32[64,384]{1,0:T(8,128)S(1)} %add.89), channel_id=1, source_target_pairs={{0,8},{4,12},{8,0},{12,4},{1,9},{5,13},{9,1},{13,5},{2,10},{6,14},... | collective-permute-start | bytes 294920 | tf_op jit(solution)/shard_map/ppermute | solution.py:19
  70.9 1.7 %collective-permute-start.23 = (f32[64,384]{1,0:T(8,128)S(1)}, f32[64,384]{1,0:T(8,128)S(1)}, u32[]{:S(2)}, u32[]{:S(2)}) collective-permute-start(f32[64,384]{1,0:T(8,128)S(1)} %fusion.5.refs_0_), channel_id=1, source_target_pairs={{0,4},{4,0},{8,12},{12,8},{1,5},{5,1},{9,13},{13,9},{2,6},{6,2},{1... | collective-permute-start | bytes 294920 | tf_op jit(solution)/shard_map/ppermute | solution.py:19
  (4 other events, 9.5 us)
